TPU v7x, 32 devices: a whole 2x2x4 slice. The times are simulated.
32 devices in a mesh: parts: 2 (over y), dp: 4 (over z), tensor: 4 (over x, core).
Axes of the slice: x: 2, y: 2, z: 4, core: 2. Of those that a mesh axis runs over, the one named last changes fastest.
Arguments:
- tokens: bfloat16 [2048, 8192], P(('parts', 'dp'), 'tensor'), parts along dimension 0, may hold values from -6 to 6
- query_weight: bfloat16 [8192, 8192], P('dp', 'tensor'), may hold values from -0.0625 to 0.0625
- down_weights: bfloat16 [64, 16, 8192], P('parts', None, 'tensor'), parts along dimension 0, may hold values from -0.0625 to 0.0625
- up_weights: bfloat16 [64, 16, 8192], P('parts', None, 'tensor'), parts along dimension 0, may hold values from -0.0625 to 0.0625
- cotangent: bfloat16 [2048, 8192], P(('parts', 'dp'), 'tensor'), parts along dimension 0, may hold values from -1.1953125 to 1.1953125
- adapter_of_block: int32 [16], P(('parts', 'dp')), parts along dimension 0, may hold values from 0 to 31
- block_live_count: int32 [16], P(('parts', 'dp')), parts along dimension 0, may hold values from 1 to 128, 768 in all
Outputs:
- query: bfloat16 [2048, 8192], P(('parts', 'dp'), 'tensor'), parts along dimension 0
- token_gradient: bfloat16 [2048, 8192], P(('parts', 'dp'), 'tensor'), parts along dimension 0
- grad_down: float32 [64, 16, 8192], P('parts', None, 'tensor'), parts along dimension 0
- grad_up: float32 [64, 16, 8192], P('parts', None, 'tensor'), parts along dimension 0
There are 2 independent parts, one for each index of `parts`. A program takes and returns all parts, laid end to end along the dimension named above; an argument that names none is the same for every part. Nothing has to cross between parts.
Inputs may be any that keep to these rules, and one draw needn't show every extreme that they name: `block_live_count`: the counts of one part sum to three quarters of 1024, and some block is full.
All inputs are finite; a program needn't handle non-finite values.
Results may differ from a plain program's by a relative error of at most 0.012.
Values may be sent and summed in bfloat16 or wider, within the bound.
No kernel may reach another device: no remote copies, remote signals or barrier semaphores. Data moves between devices by JAX's collectives and lax.ppermute only.
A program may use at most 192 MiB of HBM per device.

v0:
```python
import jax
import jax.numpy as jnp
from jax import lax
from jax.sharding import PartitionSpec as P

ADAPTER_COUNT = 32
BLOCK = 128


def local(
    tokens, query_weight, down_weights, up_weights, cotangent, adapter_of_block, block_live_count
):
    blocks_here = adapter_of_block.shape[0]
    local_width = tokens.shape[1]
    local_columns = query_weight.shape[1]
    token_row_list = tokens.shape[0]
    input_blocks = tokens.reshape(blocks_here, BLOCK, local_width)
    positions = lax.broadcasted_iota(jnp.int32, (blocks_here, BLOCK), 1)
    live_mask = positions < block_live_count[:, None]
    grad_blocks = jnp.where(
        live_mask[:, :, None],
        cotangent.reshape(blocks_here, BLOCK, local_columns),
        jnp.zeros((), cotangent.dtype),
    )
    chosen_down = down_weights[adapter_of_block]
    chosen_up = up_weights[adapter_of_block]
    rank_forward = jnp.einsum(
        "uqv,upv->upq", input_blocks, chosen_down, preferred_element_type=jnp.float32
    )
    reduced_rank = lax.psum(rank_forward, "tensor")
    reduced_rounded = reduced_rank.astype(jnp.bfloat16)
    full_tokens = lax.all_gather(tokens, "tensor", axis=1, tiled=True)
    full_weight = lax.all_gather(query_weight, "dp", axis=0, tiled=True)
    base_output = jnp.dot(full_tokens, full_weight, preferred_element_type=jnp.float32)
    adapter_output = 2.0 * jnp.einsum(
        "psw,psd->pwd", reduced_rounded, chosen_up, preferred_element_type=jnp.float32
    )
    query = (base_output + adapter_output.reshape(token_row_list, local_columns)).astype(
        jnp.bfloat16
    )
    rank_back = 2.0 * jnp.einsum(
        "bkq,brq->brk", grad_blocks, chosen_up, preferred_element_type=jnp.float32
    )
    grad_rank = lax.psum(rank_back, "tensor")
    gradient_rounded = grad_rank.astype(jnp.bfloat16)
    grad_flat = grad_blocks.reshape(token_row_list, local_columns)
    partial_sum = lax.dot_general(
        grad_flat, full_weight, (((1,), (1,)), ((), ())), preferred_element_type=jnp.float32
    )
    summed_output = lax.psum_scatter(
        partial_sum.astype(jnp.bfloat16), "tensor", scatter_dimension=1, tiled=True
    ).astype(jnp.float32)
    adapter_backward = jnp.einsum(
        "jxq,jxo->jqo", gradient_rounded, chosen_down, preferred_element_type=jnp.float32
    )
    token_gradient = (summed_output + adapter_backward.reshape(token_row_list, local_width)).astype(
        jnp.bfloat16
    )
    down_products = jnp.einsum(
        "pgz,pzq->pgq", gradient_rounded, input_blocks, preferred_element_type=jnp.float32
    )
    up_terms = 2.0 * jnp.einsum(
        "brk,bkq->brq", reduced_rounded, grad_blocks, preferred_element_type=jnp.float32
    )
    adapter_hits = (
        adapter_of_block[:, None]
        == lax.broadcasted_iota(jnp.int32, (blocks_here, ADAPTER_COUNT), 1)
    ).astype(jnp.float32)
    down_table = jnp.einsum(
        "ba,brd->ard", adapter_hits, down_products, precision=lax.Precision.HIGHEST
    )
    up_table = jnp.einsum("ba,brq->arq", adapter_hits, up_terms, precision=lax.Precision.HIGHEST)
    grad_down, grad_up = (
        lax.psum(down_table.astype(jnp.bfloat16), "dp").astype(jnp.float32),
        lax.psum(up_table.astype(jnp.bfloat16), "dp").astype(jnp.float32),
    )
    return (query, token_gradient, grad_down, grad_up)


def solution(mesh):
    return jax.shard_map(
        local,
        mesh=mesh,
        in_specs=(
            P(("parts", "dp"), "tensor"),
            P("dp", "tensor"),
            P("parts", None, "tensor"),
            P("parts", None, "tensor"),
            P(("parts", "dp"), "tensor"),
            P(("parts", "dp")),
            P(("parts", "dp")),
        ),
        out_specs=(
            P(("parts", "dp"), "tensor"),
            P(("parts", "dp"), "tensor"),
            P("parts", None, "tensor"),
            P("parts", None, "tensor"),
        ),
        check_vma=False,
    )
```

profile of v0, /device:TPU:10, one launch (start us, length us, event | category | flops | bytes accessed | tf_op | source)
XLA Modules:
  0.0 819.7 jit_solution(604411654993243793)
XLA Ops:
  7.2 0.0 copy-start
  7.2 0.0 copy-start.4
  7.2 0.0 copy-start.6
  7.2 0.0 copy-start.2
  7.2 0.0 all-gather.5.cloned.1.call-start
  7.3 0.7 all-gather.5.cloned.1.call-update
  7.9 0.0 all-reduce.4.cloned.1.call-start
  8.0 0.0 copy-done.4
  8.0 0.8 copy-done
  8.8 0.6 gather_fusion.1
  9.3 2.1 gather_fusion
  11.5 0.0 copy-done.6
  11.5 0.1 fusion.24
  11.6 0.0 copy-done.2
  11.6 0.0 copy-start.5
  11.6 0.4 fusion.25
  12.0 1.7 convolution_multiply_fusion.1
  13.6 10.4 %all-reduce = (bf16[2,16,128]{2,1,0:T(8,128)(2,1)S(1)}, bf16[2,16,128]{2,1,0:T(8,128)(2,1)S(1)}) all-reduce(f32[2,16,128]{2,1,0:T(8,128)S(1)} %fusion.25, f32[2,16,128]{2,1,0:T(8,128)S(1)} %convolution_multiply_fusion.1), channel_id=1, replica_groups=mesh['parts'=2,'dp'=4,'tensor'=4] {'tensor'}, use_global_device_ids=true, to_apply=%region_0.1 | all-reduce | flops 8192 | bytes 49152 | tf_op jit(solution)/shard_map/psum | solution.py:30
  24.1 0.3 fusion.26
  24.3 0.0 copy-done.5
  24.3 0.3 fusion.4
  24.7 3.2 convolution_convert_fusion.2
  27.9 3.2 convolution_convert_fusion.1
  31.1 0.0 all-reduce.4.cloned.1.call-update
  31.1 0.0 all-gather.3.cloned.1.call-start
  31.2 0.7 all-gather.3.cloned.1.call-update
  31.9 0.2 reduce-scatter.2.cloned.1.call-start
  32.1 537.3 %all-gather.5.cloned.1.call-done = bf16[8192,2048]{1,0:T(8,128)(2,1)} async-done(((bf16[2048,2048]{1,0:T(8,128)(2,1)}), bf16[8192,2048]{1,0:T(8,128)(2,1)}) %all-gather.5.cloned.1.call-update) | async-done | bytes 33554448 | tf_op jit(solution)/shard_map/all_gather | solution.py:33
  569.4 17.5 %convolution_convert_fusion = bf16[256,8192]{1,0:T(8,128)(2,1)} fusion(bf16[8192,2048]{1,0:T(8,128)(2,1)} %all-gather.5.cloned.1.call-done, bf16[256,2048]{1,0:T(8,128)(2,1)S(1)} %copy-done.5, pred[256]{0:T(512)(128)(4,1)S(1)} %get-tuple-element.12), kind=kOutput, calls=%fused_computation.2 | convolution fusion | flops 8592556032 | bytes 38797568 | tf_op jit(solution)/shard_map/dot_general | solution.py:47
  587.0 0.0 reduce-scatter.2.cloned.1.call-update
  587.0 1.8 convolution_multiply_fusion
  588.8 1.9 fusion.27
  590.6 136.2 %all-reduce.4.cloned.1.call-done = (bf16[32,16,2048]{2,0,1:T(8,128)(2,1)}, bf16[32,16,2048]{2,0,1:T(8,128)(2,1)}) async-done(((bf16[32,16,2048]{2,0,1:T(8,128)(2,1)}, bf16[32,16,2048]{2,0,1:T(8,128)(2,1)}), (bf16[32,16,2048]{2,0,1:T(8,128)(2,1)}, bf16[32,16,2048]{2,0,1:T(8,128)(2,1)})) %all-reduce.4.cloned.1.call-update) | async-done | bytes 4194320 | tf_op jit(solution)/shard_map/psum | solution.py:74
  726.8 0.0 copy-start.3
  726.8 5.0 copy.11
  731.8 0.0 copy-done.3
  731.8 3.2 copy.12
  735.0 28.0 %all-gather.3.cloned.1.call-done = bf16[256,8192]{1,0:T(8,128)(2,1)} async-done(((bf16[256,2048]{1,0:T(8,128)(2,1)}), bf16[256,8192]{1,0:T(8,128)(2,1)}) %all-gather.3.cloned.1.call-update) | async-done | bytes 4194320 | tf_op jit(solution)/shard_map/all_gather | solution.py:32
  763.0 0.0 copy-start.1
  763.0 19.6 %fusion = bf16[256,2048]{1,0:T(8,128)(2,1)} fusion(f32[256,2048]{1,0:T(8,128)} %bitcast.29, bf16[256,8192]{1,0:T(8,128)(2,1)} %all-gather.3.cloned.1.call-done, bf16[8192,2048]{1,0:T(8,128)(2,1)} %all-gather.5.cloned.1.call-done), kind=kOutput, calls=%fused_computation.7 | convolution fusion | flops 8590983168 | bytes 40894464 | tf_op jit(solution)/shard_map/dot_general | solution.py:34
  782.6 27.5 %reduce-scatter.2.cloned.1.call-done = bf16[256,2048]{1,0:T(8,128)(2,1)} async-done(((bf16[256,8192]{1,0:T(8,128)(2,1)}), bf16[256,2048]{1,0:T(8,128)(2,1)}) %reduce-scatter.2.cloned.1.call-update) | async-done | bytes 1048592 | tf_op jit(solution)/shard_map/reduce_scatter | solution.py:50
  810.1 3.1 fusion.1
  813.2 0.0 copy-done.1
  (2 shorter events, 0.0 us)
Async XLA Ops:
  7.2 1.6 copy-start
  7.2 0.8 copy-start.4
  7.2 4.3 copy-start.6
  7.2 4.4 copy-start.2
  7.2 562.2 %all-gather.5.cloned.1.call-start = ((), (), s32[]{:S(2)}) async-start(), calls=%async_computation.2 | async-start | bytes 41943040 | tf_op jit(solution)/shard_map/all_gather | solution.py:33
  7.9 718.9 %all-reduce.4.cloned.1.call-start = ((), (), s32[]{:S(2)}) async-start(), calls=%async_computation.4 | async-start | bytes 8388608 | tf_op jit(solution)/shard_map/psum | solution.py:74
  11.6 12.8 %copy-start.5 = (bf16[256,2048]{1,0:T(8,128)(2,1)S(1)}, bf16[256,2048]{1,0:T(8,128)(2,1)}, u32[]{:S(2)}) copy-start(bf16[256,2048]{1,0:T(8,128)(2,1)} %param.11) | copy-start | bytes 3145732
  31.1 731.8 %all-gather.3.cloned.1.call-start = ((), (), s32[]{:S(2)}) async-start(), calls=%async_computation.1 | async-start | bytes 5242880 | tf_op jit(solution)/shard_map/all_gather | solution.py:32
  31.9 778.2 %reduce-scatter.2.cloned.1.call-start = ((), (), s32[]{:S(2)}) async-start(), calls=%async_computation.3 | async-start | bytes 5242880 | tf_op jit(solution)/shard_map/reduce_scatter | solution.py:50
  726.8 5.0 copy-start.3
  763.0 50.2 %copy-start.1 = (bf16[32,16,2048]{2,1,0:T(8,128)(2,1)S(1)}, bf16[32,16,2048]{2,1,0:T(8,128)(2,1)}, u32[]{:S(2)}) copy-start(bf16[32,16,2048]{2,1,0:T(8,128)(2,1)} %param.10) | copy-start | bytes 6291460
Sparse Core Ops, SparseCore 0:
  9.6 559.7 all-gather.4
  572.4 154.3 all-reduce.3
  728.5 34.4 all-gather.2
  765.5 44.5 reduce-scatter.1
where the time goes:
time: 822 us; the launch traced here: 820 us
  waiting for transfers between devices  730 us (89%)
  matrix products  49.9 us (6%)
  between operations  13.9 us (2%)
  local copies, waits for them, and re-layouts  11.7 us (1%)
  blocking collectives  10.4 us (1%)
    all_gather x1, waiting for transfers between devices, local(): full_weight = lax.all_gather(query_weight, 'dp', axis=0, tiled=True)  537 us
    psum x1, waiting for transfers between devices, local(): lax.psum(down_table.astype(jnp.bfloat16), 'dp').astype(jnp.float32)  136 us
    all_gather x1, waiting for transfers between devices, local(): full_tokens = lax.all_gather(tokens, 'tensor', axis=1, tiled=True)  28 us
    reduce_scatter x1, waiting for transfers between devices, local(): lax.psum_scatter(partial_sum.astype(jnp.bfloat16), 'tensor', scatter_dime...  27.5 us
    dot_general x1, matrix products, local(): jnp.dot(full_tokens, full_weight, preferred_element_type=jnp.float32)  19.6 us
    dot_general x1, matrix products, local(): lax.dot_general(grad_flat, full_weight, (((1,), (1,)), ((), ())), preferr...  17.5 us
  transfers between devices with their start and end apart: 4, of which 4 were waited for; matrix products, arithmetic and copies ran while one was open for 7% of the time, Pallas kernels for 0%

commit v1 on v0

v1 whole, which is shorter than its diff:
```python
import jax
import jax.numpy as jnp
from jax import lax
from jax.sharding import PartitionSpec as P

ADAPTER_COUNT = 32
BLOCK = 128
F32 = jnp.float32
BF16 = jnp.bfloat16


def bit_reversed(index, count):
    result = 0
    while count > 1:
        result = result * 2 + index % 2
        index, count = index // 2, count // 2
    return result


def pick(stacked, index):
    return lax.dynamic_index_in_dim(stacked, index, 0, keepdims=False)


def make_local(n):
    reversed_at = [bit_reversed(q, n) for q in range(n)]
    masks = []
    while 2 ** len(masks) < n:
        masks.append(2 ** len(masks))

    def swap(x, mask):
        return lax.ppermute(x, "tensor", [(t, t ^ mask) for t in range(n)])

    def rotate(x, k):
        return lax.ppermute(x, "dp", [(i, (i + k) % n) for i in range(n)])

    def local(
        tokens,
        query_weight,
        down_weights,
        up_weights,
        cotangent,
        adapter_of_block,
        block_live_count,
    ):
        blocks_here = adapter_of_block.shape[0]
        rows, width = tokens.shape
        columns = query_weight.shape[1]
        group = rows // n
        t = lax.axis_index("tensor")
        i = lax.axis_index("dp")
        place = jnp.array(reversed_at, jnp.int32)

        positions = lax.broadcasted_iota(jnp.int32, (blocks_here, BLOCK), 1)
        live_mask = positions < block_live_count[:, None]
        grad_blocks = jnp.where(
            live_mask[:, :, None],
            cotangent.reshape(blocks_here, BLOCK, columns),
            jnp.zeros((), cotangent.dtype),
        )
        grad_flat = grad_blocks.reshape(rows, columns)

        with jax.named_scope("spread_tokens"):
            grouped = tokens.reshape(n, group, width)
            pieces = [pick(grouped, place[t])]
            for k in range(1, n):
                pieces.append(swap(pick(grouped, place[t ^ k]), k))
            pieces = jnp.stack(pieces)
            by_source = [None] * n
            by_source[0] = pick(pieces, i ^ t)
            for k in sorted(range(1, n), key=lambda k: -abs(2 * k - n)):
                by_source[(n - k) % n] = rotate(pick(pieces, ((i + k) % n) ^ t), k)
            full = [x[None] for x in by_source]
            full = jnp.stack(full)
            for mask in reversed(masks):
                full = jnp.concatenate([full, swap(full, mask)], axis=1)
        order = [0]
        for mask in reversed(masks):
            order = order + [k ^ mask for k in order]

        with jax.named_scope("spread_cotangent"):
            up, down = [grad_flat], [grad_flat]
            for s in range(1, n):
                up.append(lax.ppermute(up[-1], "dp", [(a, a + 1) for a in range(s - 1, n - 1)]))
                down.append(lax.ppermute(down[-1], "dp", [(a + 1, a) for a in range(n - s)]))
            grads = [grad_flat] + [
                jnp.where(i + r <= n - 1, down[r], up[n - r]) for r in range(1, n)
            ]

        with jax.named_scope("ranks"):
            token_blocks = tokens.reshape(blocks_here, BLOCK, width)
            chosen_down = down_weights[adapter_of_block]
            chosen_up = up_weights[adapter_of_block]
            ranks = jnp.stack(
                [
                    jnp.einsum(
                        "uqv,upv->upq", token_blocks, chosen_down, preferred_element_type=F32
                    ),
                    2.0
                    * jnp.einsum("bkq,brq->brk", grad_blocks, chosen_up, preferred_element_type=F32),
                ]
            )
            for mask in masks:
                ranks = ranks + swap(ranks, mask)
            ranks = ranks.astype(BF16)
            shrunk, grad_rank = ranks[0], ranks[1]

        with jax.named_scope("tables"):
            products = jnp.stack(
                [
                    jnp.einsum("pgz,pzq->pgq", grad_rank, token_blocks, preferred_element_type=F32),
                    2.0
                    * jnp.einsum("brk,bkq->brq", shrunk, grad_blocks, preferred_element_type=F32),
                ],
                axis=1,
            ).astype(BF16)
            products = lax.all_gather(products, "dp", axis=0, tiled=True)
            ids = lax.all_gather(adapter_of_block, "dp", axis=0, tiled=True)
            hits = (
                lax.broadcasted_iota(jnp.int32, (ADAPTER_COUNT, ids.shape[0]), 0) == ids[None, :]
            ).astype(BF16)
            grad_down = jnp.einsum("ab,brd->ard", hits, products[:, 0], preferred_element_type=F32)
            grad_up = jnp.einsum("ab,brd->ard", hits, products[:, 1], preferred_element_type=F32)

        with jax.named_scope("forward"):
            parts = []
            for r in range(n):
                parts.append(
                    jnp.dot(
                        full[r].reshape(rows, width), query_weight, preferred_element_type=F32
                    ).astype(BF16)
                )
            up_sum = down_sum = None
            for s in range(1, n):
                d = n - s
                send_up = parts[d] if up_sum is None else parts[d] + up_sum
                send_down = parts[n - d] if down_sum is None else parts[n - d] + down_sum
                up_sum = lax.ppermute(send_up, "dp", [(a, a + 1) for a in range(s)])
                down_sum = lax.ppermute(send_down, "dp", [(a, a - 1) for a in range(d, n)])
            base = parts[0].astype(F32) + up_sum.astype(F32) + down_sum.astype(F32)
            base = base.reshape(n, group, columns)

        position = jnp.array([order.index(k) for k in range(n)], jnp.int32)
        natural = sorted(range(n), key=lambda q: reversed_at[q])

        def in_place(groups):
            return jnp.concatenate(
                [pick(groups, position[q ^ t]) for q in natural], axis=0
            )

        adapter_output = 2.0 * jnp.einsum(
            "psw,psd->pwd", shrunk, chosen_up, preferred_element_type=F32
        )
        query = (in_place(base) + adapter_output.reshape(rows, columns)).astype(BF16)

        with jax.named_scope("backward"):
            sums = [None] * n
            for r in range(n):
                value = lax.dot_general(
                    grads[r], query_weight, (((1,), (1,)), ((), ())), preferred_element_type=F32
                ).astype(BF16)
                for mask in masks:
                    halves = value.reshape(2, value.shape[0] // 2, width)
                    bit = (t // mask) % 2
                    value = pick(halves, bit) + swap(pick(halves, 1 - bit), mask)
                sums[r] = value
            home = [sums[0]] + [rotate(sums[r], r) for r in range(1, n)]
            home = jnp.stack(home)
            back = [pick(home, (i - t) % n)]
            for k in range(1, n):
                back.append(swap(pick(home, (i - (t ^ k)) % n), k))
            back = jnp.stack([back[k] for k in order])
            adapter_backward = jnp.einsum(
                "jxq,jxo->jqo", grad_rank, chosen_down, preferred_element_type=F32
            )
            token_gradient = (
                in_place(back.astype(F32)) + adapter_backward.reshape(rows, width)
            ).astype(BF16)
        return (query, token_gradient, grad_down, grad_up)

    return local


def solution(mesh):
    assert mesh.shape["dp"] == mesh.shape["tensor"]
    return jax.shard_map(
        make_local(mesh.shape["tensor"]),
        mesh=mesh,
        in_specs=(
            P(("parts", "dp"), "tensor"),
            P("dp", "tensor"),
            P("parts", None, "tensor"),
            P("parts", None, "tensor"),
            P(("parts", "dp"), "tensor"),
            P(("parts", "dp")),
            P(("parts", "dp")),
        ),
        out_specs=(
            P(("parts", "dp"), "tensor"),
            P(("parts", "dp"), "tensor"),
            P("parts", None, "tensor"),
            P("parts", None, "tensor"),
        ),
        check_vma=False,
    )
```

time: 822 us -> 312 us (0.38)
  waiting for transfers between devices: 730 us -> 159 us
  starting transfers between devices: 0.34 us -> 44.5 us
  matrix products: 49.9 us -> 39.9 us
  between operations: 13.9 us -> 23.1 us
  other arithmetic: 3.2 us -> 12.4 us
    all_gather x2 -> x1, waiting for transfers between devices: 565 us -> 0.01 us  [local(): products = lax.all_gather(products, 'dp', axis=0, tiled=True)]
    ppermute x0 -> x36, waiting for transfers between devices: none -> 159 us  [the longest x6 78.8 us: rotate(): return lax.ppermute(x, 'dp', [(i, (i + k) % n) for i in range(n)])]
    psum x1 -> x0, waiting for transfers between devices: 136 us -> none  [local(): lax.psum(down_table.astype(jnp.bfloat16), 'dp').astype(jnp.float32)]
    ppermute x0 -> x36, starting transfers between devices: none -> 44.5 us  [the longest x18 11.4 us: swap(): return lax.ppermute(x, 'tensor', [(t, t ^ mask) for t in range(n)])]
    reduce_scatter x1 -> x0, waiting for transfers between devices: 27.5 us -> none  [local(): lax.psum_scatter(partial_sum.astype(jnp.bfloat16), 'tensor', scatter_dime...]
    psum x1 -> x0, blocking collectives: 10.4 us -> none  [local(): reduced_rank = lax.psum(rank_forward, 'tensor')]
    dot_general x9 -> x15, matrix products: 48.2 us -> 38.2 us  [the longest x4 22.1 us: local(): lax.dot_general(grads[r], query_weight, (((1,), (1,)), ((), ())), preferr...]
    unnamed x0 -> x1, blocking collectives: none -> 8.48 us
  transfers between devices with their start and end apart: 4 -> 37, of which waited for: 4 -> 12; matrix products, arithmetic and copies ran while one was open for 7% -> 20% of each run, Pallas kernels for 0% -> 0%
where the time goes in v1:
time: 312 us; the launch traced here: 308 us
  waiting for transfers between devices  159 us (51%)
  starting transfers between devices  44.5 us (14%)
  matrix products  39.9 us (13%)
  between operations  23.1 us (7%)
  local copies, waits for them, and re-layouts  19.9 us (6%)
  other arithmetic  12.4 us (4%)
  blocking collectives  8.48 us (3%)
    ppermute x6, waiting for transfers between devices, rotate(): return lax.ppermute(x, 'dp', [(i, (i + k) % n) for i in range(n)])  78.8 us
    ppermute x3, waiting for transfers between devices, local(): up_sum = lax.ppermute(send_up, 'dp', [(a, a + 1) for a in range(s)])  31.4 us
    ppermute x18, waiting for transfers between devices, swap(): return lax.ppermute(x, 'tensor', [(t, t ^ mask) for t in range(n)])  26.9 us
    dot_general x4, matrix products, local(): lax.dot_general(grads[r], query_weight, (((1,), (1,)), ((), ())), preferr...  22.1 us
    ppermute x3, waiting for transfers between devices, local(): lax.ppermute(down[-1], 'dp', [(a + 1, a) for a in range(n - s)])  20 us
    unnamed x37, local copies, waits for them, and re-layouts  12.1 us
    ppermute x18, starting transfers between devices, swap(): return lax.ppermute(x, 'tensor', [(t, t ^ mask) for t in range(n)])  11.4 us
    dot_general x4, matrix products, local(): jnp.dot(full[r].reshape(rows, width), query_weight, preferred_element_typ...  9.87 us
  transfers between devices with their start and end apart: 37, of which 12 were waited for; matrix products, arithmetic and copies ran while one was open for 20% of the time, Pallas kernels for 0%

profile of v1, /device:TPU:10, one launch (start us, length us, event | category | flops | bytes accessed | tf_op | source)
XLA Modules:
  0.0 307.7 jit_solution(12079813797259986700)
XLA Ops:
  8.1 2.4 broadcast_select_fusion
  10.5 3.5 %collective-permute-start.19 = (bf16[256,2048]{1,0:T(8,128)(2,1)}, bf16[256,2048]{1,0:T(8,128)(2,1)}, u32[]{:S(2)}, u32[]{:S(2)}) collective-permute-start(bf16[256,2048]{1,0:T(8,128)(2,1)} %broadcast_select_fusion), channel_id=1, source_target_pairs={{0,4},{4,8},{8,12},{1,5},{5,9},{9,13},{2,6},{6,10},{10,14},{3,7},{... | collective-permute-start | bytes 3145736 | tf_op jit(solution)/shard_map/spread_cotangent/ppermute | solution.py:83
  14.0 3.3 %collective-permute-start.18 = (bf16[256,2048]{1,0:T(8,128)(2,1)}, bf16[256,2048]{1,0:T(8,128)(2,1)}, u32[]{:S(2)}, u32[]{:S(2)}) collective-permute-start(bf16[256,2048]{1,0:T(8,128)(2,1)} %broadcast_select_fusion), channel_id=1, source_target_pairs={{4,0},{8,4},{12,8},{5,1},{9,5},{13,9},{6,2},{10,6},{14,10},{7,3},{... | collective-permute-start | bytes 3145736 | tf_op jit(solution)/shard_map/spread_cotangent/ppermute | solution.py:84
  27.9 2.1 gather_fusion
  30.4 1.7 fusion.8
  32.2 6.1 %convolution_convert_fusion.3 = bf16[256,2048]{1,0:T(8,128)(2,1)S(1)} fusion(bf16[256,2048]{1,0:T(8,128)(2,1)} %broadcast_select_fusion, bf16[2048,2048]{1,0:T(8,128)(2,1)} %param.10), kind=kOutput, calls=%fused_computation.7 | convolution fusion | flops 2148007936 | bytes 10485760 | tf_op jit(solution)/shard_map/backward/dot_general | solution.py:158
  40.0 1.6 collective-permute-start.15
  42.4 8.5 %all-reduce = s32[8]{0:T(128)S(1)} all-reduce(s32[8]{0:T(128)S(1)} %dynamic-update-slice), channel_id=1, replica_groups=mesh['parts'=2,'dp'=4,'tensor'=4] {'dp'}, use_global_device_ids=true, to_apply=%add | all-reduce | flops 8 | bytes 64
  51.5 1.8 convolution_multiply_fusion
  53.3 1.8 fusion.22
  58.6 2.3 collective-permute-start.20
  60.8 1.9 collective-permute-start.25
  62.9 3.5 %collective-permute-start.4 = (bf16[64,2048]{1,0:T(8,128)(2,1)S(1)}, bf16[64,2048]{1,0:T(8,128)(2,1)S(1)}, u32[]{:S(2)}, u32[]{:S(2)}) collective-permute-start(bf16[64,2048]{1,0:T(8,128)(2,1)S(1)} %get-tuple-element.30), channel_id=1, source_target_pairs={{0,8},{4,12},{8,0},{12,4},{1,9},{5,13},{9,1},{13,5},{2,10},{6,14},... | collective-permute-start | bytes 786440 | tf_op jit(solution)/shard_map/spread_tokens/ppermute | solution.py:34
  66.5 55.9 %collective-permute-done.3 = bf16[64,2048]{1,0:T(8,128)(2,1)S(1)} collective-permute-done((bf16[64,2048]{1,0:T(8,128)(2,1)S(1)}, bf16[64,2048]{1,0:T(8,128)(2,1)S(1)}, u32[]{:S(2)}, u32[]{:S(2)}) %collective-permute-start.3) | collective-permute-done | bytes 262176 | tf_op jit(solution)/shard_map/spread_tokens/ppermute | solution.py:34
  123.2 1.5 collective-permute-start.6
  124.7 6.1 %convolution_convert_fusion.1 = bf16[256,2048]{1,0:T(8,128)(2,1)S(1)} fusion(bf16[2048,2048]{1,0:T(8,128)(2,1)} %param.10, bf16[256,2048]{1,0:T(8,128)(2,1)S(1)} %collective-permute-done.25, bf16[256,2048]{1,0:T(8,128)(2,1)} %collective-permute-done.20, pred[]{:T(512)S(6)} %le.10), kind=kOutput, calls=%fused_computation.5 | convolution fusion | flops 2148532224 | bytes 11534337 | tf_op jit(solution)/shard_map/backward/dot_general | solution.py:158
  131.8 20.1 %collective-permute-done.6 = bf16[4,1,64,2048]{3,2,1,0:T(8,128)(2,1)S(1)} collective-permute-done((bf16[4,1,64,2048]{3,2,1,0:T(8,128)(2,1)S(1)}, bf16[4,1,64,2048]{3,2,1,0:T(8,128)(2,1)S(1)}, u32[]{:S(2)}, u32[]{:S(2)}) %collective-permute-start.6) | collective-permute-done | bytes 1048608 | tf_op jit(solution)/shard_map/spread_tokens/ppermute | solution.py:31
  151.9 1.6 pad_maximum_fusion.1
  153.5 1.6 collective-permute-start.21
  155.2 1.8 collective-permute-start.27
  157.0 1.4 slice_bitcast_fusion
  158.6 3.8 %collective-permute-start.29 = (bf16[256,2048]{1,0:T(8,128)(2,1)S(1)}, bf16[256,2048]{1,0:T(8,128)(2,1)S(1)}, u32[]{:S(2)}, u32[]{:S(2)}) collective-permute-start(bf16[256,2048]{1,0:T(8,128)(2,1)S(1)} %copy-done.11), channel_id=1, source_target_pairs={{4,0},{5,1},{6,2},{7,3},{20,16},{21,17},{22,18},{23,19}} | collective-permute-start | bytes 3145736 | tf_op jit(solution)/shard_map/spread_cotangent/ppermute | solution.py:84
  162.4 1.6 collective-permute-done.27
  164.1 6.2 %convolution_convert_fusion.2 = bf16[256,2048]{1,0:T(8,128)(2,1)S(1)} fusion(bf16[2048,2048]{1,0:T(8,128)(2,1)} %param.10, bf16[256,2048]{1,0:T(8,128)(2,1)} %collective-permute-done.18, bf16[256,2048]{1,0:T(8,128)(2,1)} %collective-permute-done.21, pred[]{:T(512)S(6)} %le.9), kind=kOutput, calls=%fused_computation.6 | convolution fusion | flops 2148532224 | bytes 11534337 | tf_op jit(solution)/shard_map/backward/dot_general | solution.py:158
  170.5 20.0 %collective-permute-done.29 = bf16[256,2048]{1,0:T(8,128)(2,1)S(1)} collective-permute-done((bf16[256,2048]{1,0:T(8,128)(2,1)S(1)}, bf16[256,2048]{1,0:T(8,128)(2,1)S(1)}, u32[]{:S(2)}, u32[]{:S(2)}) %collective-permute-start.29) | collective-permute-done | bytes 1048608 | tf_op jit(solution)/shard_map/spread_cotangent/ppermute | solution.py:84
  190.6 3.6 %convolution_convert_fusion = bf16[256,2048]{1,0:T(8,128)(2,1)S(1)} fusion(bf16[2048,2048]{1,0:T(8,128)(2,1)S(1)} %bitcast.197, bf16[256,2048]{1,0:T(8,128)(2,1)S(1)} %collective-permute-done.29, bf16[256,2048]{1,0:T(8,128)(2,1)} %collective-permute-done.19, pred[]{:T(512)S(6)} %le.11), kind=kOutput, calls=%fused_computation.4 | convolution fusion | flops 2148532224 | bytes 11534337 | tf_op jit(solution)/shard_map/backward/dot_general | solution.py:158
  194.8 1.8 pad_maximum_fusion
  197.2 2.4 convolution_convert_fusion.6
  200.3 2.4 convolution_convert_fusion.4
  202.7 1.3 collective-permute-start.8
  204.2 1.8 collective-permute-start.31
  206.0 24.6 %collective-permute-done.8 = bf16[256,2048]{1,0:T(8,128)(2,1)S(1)} collective-permute-done((bf16[256,2048]{1,0:T(8,128)(2,1)S(1)}, bf16[256,2048]{1,0:T(8,128)(2,1)S(1)}, u32[]{:S(2)}, u32[]{:S(2)}) %collective-permute-start.8) | collective-permute-done | bytes 1048608 | tf_op jit(solution)/shard_map/forward/ppermute | solution.py:137
  230.6 2.5 fusion.33
  233.1 1.9 collective-permute-start.9
  235.1 1.3 collective-permute-start.12
  236.4 1.8 collective-permute-start.32
  239.0 4.4 %copy.15 = f32[32,16,2048]{2,1,0:T(8,128)} copy(f32[32,16,2048]{2,0,1:T(8,128)S(1)} %fusion.17) | data formatting | bytes 8388608
  243.5 22.8 %collective-permute-done.32 = bf16[64,2048]{1,0:T(8,128)(2,1)S(1)} collective-permute-done((bf16[64,2048]{1,0:T(8,128)(2,1)S(1)}, bf16[64,2048]{1,0:T(8,128)(2,1)S(1)}, u32[]{:S(2)}, u32[]{:S(2)}) %collective-permute-start.32) | collective-permute-done | bytes 262176 | tf_op jit(solution)/shard_map/backward/ppermute | solution.py:34
  266.8 1.9 collective-permute-start.10
  269.2 4.0 %collective-permute-start.13 = (bf16[256,2048]{1,0:T(8,128)(2,1)S(1)}, bf16[256,2048]{1,0:T(8,128)(2,1)S(1)}, u32[]{:S(2)}, u32[]{:S(2)}) collective-permute-start(bf16[256,2048]{1,0:T(8,128)(2,1)S(1)} %add.230), channel_id=1, source_target_pairs={{4,0},{8,4},{12,8},{5,1},{9,5},{13,9},{6,2},{10,6},{14,10},{7,3},{... | collective-permute-start | bytes 3145736 | tf_op jit(solution)/shard_map/forward/ppermute | solution.py:138
  273.3 1.8 collective-permute-start.33
  276.3 4.4 %copy.16 = f32[32,16,2048]{2,1,0:T(8,128)} copy(f32[32,16,2048]{2,0,1:T(8,128)S(1)} %fusion.15) | data formatting | bytes 8388608
  281.6 2.8 collective-permute-done.35
  284.7 6.8 %collective-permute-done.10 = bf16[256,2048]{1,0:T(8,128)(2,1)S(1)} collective-permute-done((bf16[256,2048]{1,0:T(8,128)(2,1)S(1)}, bf16[256,2048]{1,0:T(8,128)(2,1)S(1)}, u32[]{:S(2)}, u32[]{:S(2)}) %collective-permute-start.10) | collective-permute-done | bytes 1048608 | tf_op jit(solution)/shard_map/forward/ppermute | solution.py:137
  291.5 2.3 collective-permute-done.13
  293.8 2.6 fusion.2
  296.6 1.4 copy-done.3
  298.6 2.2 fusion.6
  (125 shorter events, 19.4 us)
Async XLA Ops:
  7.2 20.1 %copy-start = (bf16[32,16,2048]{2,1,0:T(8,128)(2,1)S(1)}, bf16[32,16,2048]{2,1,0:T(8,128)(2,1)}, u32[]{:S(2)}) copy-start(bf16[32,16,2048]{2,1,0:T(8,128)(2,1)} %param.12) | copy-start | bytes 6291460
  7.2 10.2 %copy-start.9 = (s32[4]{0:T(128)S(1)}, s32[4]{0:T(128)}, u32[]{:S(2)}) copy-start(s32[4]{0:T(128)} %constant.197.clone) | copy-start | bytes 52
  7.2 18.5 %copy-start.2 = (bf16[256,2048]{1,0:T(8,128)(2,1)S(1)}, bf16[256,2048]{1,0:T(8,128)(2,1)}, u32[]{:S(2)}) copy-start(bf16[256,2048]{1,0:T(8,128)(2,1)} %param.9) | copy-start | bytes 3145732
  7.2 149.8 %all-gather.2.cloned.1.call-start = ((), (), s32[]{:S(2)}) async-start(), calls=%async_computation | async-start | bytes 1310720 | tf_op jit(solution)/shard_map/tables/all_gather | solution.py:116
  8.1 19.2 %copy-start.12 = (s32[2]{0:T(128)S(1)}, s32[2]{0:T(128)}, u32[]{:S(2)}) copy-start(s32[2]{0:T(128)} %param.14) | copy-start | bytes 28
  10.5 48.0 %collective-permute-start.19 = (bf16[256,2048]{1,0:T(8,128)(2,1)}, bf16[256,2048]{1,0:T(8,128)(2,1)}, u32[]{:S(2)}, u32[]{:S(2)}) collective-permute-start(bf16[256,2048]{1,0:T(8,128)(2,1)} %broadcast_select_fusion), channel_id=1, source_target_pairs={{0,4},{4,8},{8,12},{1,5},{5,9},{9,13},{2,6},{6,10},{10,14},{3,7},{... | collective-permute-start | bytes 3145736 | tf_op jit(solution)/shard_map/spread_cotangent/ppermute | solution.py:83
  14.0 46.8 %collective-permute-start.18 = (bf16[256,2048]{1,0:T(8,128)(2,1)}, bf16[256,2048]{1,0:T(8,128)(2,1)}, u32[]{:S(2)}, u32[]{:S(2)}) collective-permute-start(bf16[256,2048]{1,0:T(8,128)(2,1)} %broadcast_select_fusion), channel_id=1, source_target_pairs={{4,0},{8,4},{12,8},{5,1},{9,5},{13,9},{6,2},{10,6},{14,10},{7,3},{... | collective-permute-start | bytes 3145736 | tf_op jit(solution)/shard_map/spread_cotangent/ppermute | solution.py:84
  26.6 29.1 %collective-permute-start.2 = (bf16[64,2048]{1,0:T(8,128)(2,1)}, bf16[64,2048]{1,0:T(8,128)(2,1)}, u32[]{:S(2)}, u32[]{:S(2)}) collective-permute-start(bf16[64,2048]{1,0:T(8,128)(2,1)} %get-tuple-element.33), channel_id=1, source_target_pairs={{0,3},{1,2},{2,1},{3,0},{4,7},{5,6},{6,5},{7,4},{8,11},{9,10},{10,... | collective-permute-start | bytes 786440 | tf_op jit(solution)/shard_map/spread_tokens/ppermute | solution.py:31
  26.6 29.9 %collective-permute-start = (bf16[64,2048]{1,0:T(8,128)(2,1)}, bf16[64,2048]{1,0:T(8,128)(2,1)}, u32[]{:S(2)}, u32[]{:S(2)}) collective-permute-start(bf16[64,2048]{1,0:T(8,128)(2,1)} %get-tuple-element.35), channel_id=1, source_target_pairs={{0,1},{1,0},{2,3},{3,2},{4,5},{5,4},{6,7},{7,6},{8,9},{9,8},{10,11... | collective-permute-start | bytes 786440 | tf_op jit(solution)/shard_map/spread_tokens/ppermute | solution.py:31
  32.1 6.3 %copy-start.13 = (u32[32]{0:T(128)S(1)}, u32[32]{0:T(128)}, u32[]{:S(2)}) copy-start(u32[32]{0:T(128)} %constant.202) | copy-start | bytes 388
  32.1 18.7 %copy-start.8 = (bf16[64,2048]{1,0:T(8,128)(2,1)S(1)}, bf16[64,2048]{1,0:T(8,128)(2,1)}, u32[]{:S(2)}) copy-start(bf16[64,2048]{1,0:T(8,128)(2,1)} %get-tuple-element.34) | copy-start | bytes 786436
  32.1 7.8 %collective-permute-start.14 = (f32[2,2,16,128]{3,2,1,0:T(8,128)S(1)}, f32[2,2,16,128]{3,2,1,0:T(8,128)S(1)}, u32[]{:S(2)}, u32[]{:S(2)}) collective-permute-start(f32[2,2,16,128]{3,2,1,0:T(8,128)S(1)} %pad_maximum_fusion.6), channel_id=1, source_target_pairs={{0,1},{1,0},{2,3},{3,2},{4,5},{5,4},{6,7},{7,6},{8,9},{9,8},{10,11... | collective-permute-start | bytes 98312 | tf_op jit(solution)/shard_map/ranks/ppermute | solution.py:31
  38.3 13.1 %copy-start.6 = (bf16[256,2048]{1,0:T(8,128)(2,1)}, bf16[256,2048]{1,0:T(8,128)(2,1)S(1)}, u32[]{:S(2)}) copy-start(bf16[256,2048]{1,0:T(8,128)(2,1)S(1)} %convolution_convert_fusion.3) | copy-start | bytes 3145732
  40.0 10.9 %collective-permute-start.15 = (f32[2,2,16,128]{3,2,1,0:T(8,128)S(1)}, f32[2,2,16,128]{3,2,1,0:T(8,128)S(1)}, u32[]{:S(2)}, u32[]{:S(2)}) collective-permute-start(f32[2,2,16,128]{3,2,1,0:T(8,128)S(1)} %fusion.31), channel_id=1, source_target_pairs={{0,2},{1,3},{2,0},{3,1},{4,6},{5,7},{6,4},{7,5},{8,10},{9,11},{10,... | collective-permute-start | bytes 98312 | tf_op jit(solution)/shard_map/ranks/ppermute | solution.py:31
  50.8 6.4 %collective-permute-start.1 = (bf16[64,2048]{1,0:T(8,128)(2,1)S(1)}, bf16[64,2048]{1,0:T(8,128)(2,1)S(1)}, u32[]{:S(2)}, u32[]{:S(2)}) collective-permute-start(bf16[64,2048]{1,0:T(8,128)(2,1)S(1)} %copy-done.8), channel_id=1, source_target_pairs={{0,2},{1,3},{2,0},{3,1},{4,6},{5,7},{6,4},{7,5},{8,10},{9,11},{10,... | collective-permute-start | bytes 786440 | tf_op jit(solution)/shard_map/spread_tokens/ppermute | solution.py:31
  55.7 10.7 %collective-permute-start.16 = (bf16[128,2048]{1,0:T(8,128)(2,1)}, bf16[128,2048]{1,0:T(8,128)(2,1)S(1)}, u32[]{:S(2)}, u32[]{:S(2)}) collective-permute-start(bf16[128,2048]{1,0:T(8,128)(2,1)} %dynamic-slice_bitcast_fusion.7), channel_id=1, source_target_pairs={{0,1},{1,0},{2,3},{3,2},{4,5},{5,4},{6,7},{7,6},{8,9},{9,8},{10,11... | collective-permute-start | bytes 1572872 | tf_op jit(solution)/shard_map/backward/ppermute | solution.py:31
  57.3 9.2 %copy-start.7 = (bf16[256,2048]{1,0:T(8,128)(2,1)S(1)}, bf16[256,2048]{1,0:T(8,128)(2,1)}, u32[]{:S(2)}) copy-start(bf16[256,2048]{1,0:T(8,128)(2,1)} %copy-done.6) | copy-start | bytes 3145732
  58.6 66.2 %collective-permute-start.20 = (bf16[256,2048]{1,0:T(8,128)(2,1)}, bf16[256,2048]{1,0:T(8,128)(2,1)}, u32[]{:S(2)}, u32[]{:S(2)}) collective-permute-start(bf16[256,2048]{1,0:T(8,128)(2,1)} %collective-permute-done.19), channel_id=1, source_target_pairs={{4,8},{8,12},{5,9},{9,13},{6,10},{10,14},{7,11},{11,15},{20,24},{2... | collective-permute-start | bytes 3145736 | tf_op jit(solution)/shard_map/spread_cotangent/ppermute | solution.py:83
  60.8 63.9 %collective-permute-start.25 = (bf16[256,2048]{1,0:T(8,128)(2,1)}, bf16[256,2048]{1,0:T(8,128)(2,1)S(1)}, u32[]{:S(2)}, u32[]{:S(2)}) collective-permute-start(bf16[256,2048]{1,0:T(8,128)(2,1)} %collective-permute-done.18), channel_id=1, source_target_pairs={{4,0},{8,4},{5,1},{9,5},{6,2},{10,6},{7,3},{11,7},{20,16},{24,20},... | collective-permute-start | bytes 3145736 | tf_op jit(solution)/shard_map/spread_cotangent/ppermute | solution.py:84
  62.8 59.7 %collective-permute-start.3 = (bf16[64,2048]{1,0:T(8,128)(2,1)S(1)}, bf16[64,2048]{1,0:T(8,128)(2,1)S(1)}, u32[]{:S(2)}, u32[]{:S(2)}) collective-permute-start(bf16[64,2048]{1,0:T(8,128)(2,1)S(1)} %get-tuple-element.31), channel_id=1, source_target_pairs={{0,12},{4,0},{8,4},{12,8},{1,13},{5,1},{9,5},{13,9},{2,14},{6,2},{... | collective-permute-start | bytes 786440 | tf_op jit(solution)/shard_map/spread_tokens/ppermute | solution.py:34
  62.9 60.1 %collective-permute-start.4 = (bf16[64,2048]{1,0:T(8,128)(2,1)S(1)}, bf16[64,2048]{1,0:T(8,128)(2,1)S(1)}, u32[]{:S(2)}, u32[]{:S(2)}) collective-permute-start(bf16[64,2048]{1,0:T(8,128)(2,1)S(1)} %get-tuple-element.30), channel_id=1, source_target_pairs={{0,8},{4,12},{8,0},{12,4},{1,9},{5,13},{9,1},{13,5},{2,10},{6,14},... | collective-permute-start | bytes 786440 | tf_op jit(solution)/shard_map/spread_tokens/ppermute | solution.py:34
  66.4 56.6 %collective-permute-start.5 = (bf16[64,2048]{1,0:T(8,128)(2,1)S(1)}, bf16[64,2048]{1,0:T(8,128)(2,1)S(1)}, u32[]{:S(2)}, u32[]{:S(2)}) collective-permute-start(bf16[64,2048]{1,0:T(8,128)(2,1)S(1)} %get-tuple-element.29), channel_id=1, source_target_pairs={{0,4},{4,8},{8,12},{12,0},{1,5},{5,9},{9,13},{13,1},{2,6},{6,10},{... | collective-permute-start | bytes 786440 | tf_op jit(solution)/shard_map/spread_tokens/ppermute | solution.py:34
  122.5 9.2 %collective-permute-start.17 = (bf16[64,2048]{1,0:T(8,128)(2,1)S(1)}, bf16[64,2048]{1,0:T(8,128)(2,1)S(1)}, u32[]{:S(2)}, u32[]{:S(2)}) collective-permute-start(bf16[64,2048]{1,0:T(8,128)(2,1)S(1)} %dynamic-slice_bitcast_fusion.18), channel_id=1, source_target_pairs={{0,2},{1,3},{2,0},{3,1},{4,6},{5,7},{6,4},{7,5},{8,10},{9,11},{10,... | collective-permute-start | bytes 786440 | tf_op jit(solution)/shard_map/backward/ppermute | solution.py:31
  123.2 28.7 %collective-permute-start.6 = (bf16[4,1,64,2048]{3,2,1,0:T(8,128)(2,1)S(1)}, bf16[4,1,64,2048]{3,2,1,0:T(8,128)(2,1)S(1)}, u32[]{:S(2)}, u32[]{:S(2)}) collective-permute-start(bf16[4,1,64,2048]{3,2,1,0:T(8,128)(2,1)S(1)} %pad_maximum_fusion.3), channel_id=1, source_target_pairs={{0,2},{1,3},{2,0},{3,1},{4,6},{5,7},{6,4},{7,5},{8,10},{9,11},{10,... | collective-permute-start | bytes 3145736 | tf_op jit(solution)/shard_map/spread_tokens/ppermute | solution.py:31
  124.7 6.1 %copy-start.10 = (bf16[256,2048]{1,0:T(8,128)(2,1)}, bf16[256,2048]{1,0:T(8,128)(2,1)S(1)}, u32[]{:S(2)}) copy-start(bf16[256,2048]{1,0:T(8,128)(2,1)S(1)} %collective-permute-done.25) | copy-start | bytes 3145732
  131.0 24.2 %collective-permute-start.26 = (bf16[128,2048]{1,0:T(8,128)(2,1)S(1)}, bf16[128,2048]{1,0:T(8,128)(2,1)S(1)}, u32[]{:S(2)}, u32[]{:S(2)}) collective-permute-start(bf16[128,2048]{1,0:T(8,128)(2,1)S(1)} %dynamic-slice_bitcast_fusion.5), channel_id=1, source_target_pairs={{0,1},{1,0},{2,3},{3,2},{4,5},{5,4},{6,7},{7,6},{8,9},{9,8},{10,11... | collective-permute-start | bytes 1572872 | tf_op jit(solution)/shard_map/backward/ppermute | solution.py:31
  153.5 41.3 %collective-permute-start.7 = (bf16[4,2,64,2048]{3,2,1,0:T(8,128)(2,1)}, bf16[4,2,64,2048]{3,2,1,0:T(8,128)(2,1)}, u32[]{:S(2)}, u32[]{:S(2)}) collective-permute-start(bf16[4,2,64,2048]{3,2,1,0:T(8,128)(2,1)} %pad_maximum_fusion.1), channel_id=1, source_target_pairs={{0,1},{1,0},{2,3},{3,2},{4,5},{5,4},{6,7},{7,6},{8,9},{9,8},{10,11... | collective-permute-start | bytes 6291464 | tf_op jit(solution)/shard_map/spread_tokens/ppermute | solution.py:31
  153.5 10.7 %collective-permute-start.21 = (bf16[256,2048]{1,0:T(8,128)(2,1)}, bf16[256,2048]{1,0:T(8,128)(2,1)}, u32[]{:S(2)}, u32[]{:S(2)}) collective-permute-start(bf16[256,2048]{1,0:T(8,128)(2,1)} %collective-permute-done.20), channel_id=1, source_target_pairs={{8,12},{9,13},{10,14},{11,15},{24,28},{25,29},{26,30},{27,31}} | collective-permute-start | bytes 3145736 | tf_op jit(solution)/shard_map/spread_cotangent/ppermute | solution.py:83
  155.2 8.8 %collective-permute-start.27 = (bf16[64,2048]{1,0:T(8,128)(2,1)S(1)}, bf16[64,2048]{1,0:T(8,128)(2,1)S(1)}, u32[]{:S(2)}, u32[]{:S(2)}) collective-permute-start(bf16[64,2048]{1,0:T(8,128)(2,1)S(1)} %dynamic-slice_bitcast_fusion.16), channel_id=1, source_target_pairs={{0,2},{1,3},{2,0},{3,1},{4,6},{5,7},{6,4},{7,5},{8,10},{9,11},{10,... | collective-permute-start | bytes 786440 | tf_op jit(solution)/shard_map/backward/ppermute | solution.py:31
  158.6 32.0 %collective-permute-start.29 = (bf16[256,2048]{1,0:T(8,128)(2,1)S(1)}, bf16[256,2048]{1,0:T(8,128)(2,1)S(1)}, u32[]{:S(2)}, u32[]{:S(2)}) collective-permute-start(bf16[256,2048]{1,0:T(8,128)(2,1)S(1)} %copy-done.11), channel_id=1, source_target_pairs={{4,0},{5,1},{6,2},{7,3},{20,16},{21,17},{22,18},{23,19}} | collective-permute-start | bytes 3145736 | tf_op jit(solution)/shard_map/spread_cotangent/ppermute | solution.py:84
  164.0 26.5 %slice-start = ((s8[8388608]{0:T(1024)(128)(4,1)}), s8[4194304]{0:T(1024)(128)(4,1)S(1)}, s32[]{:S(2)}) async-start(s8[8388608]{0:T(1024)(128)(4,1)} %bitcast.196), calls=%async_computation.1 | async-start | bytes 8388608
  164.0 26.5 %slice-start.1 = ((s8[8388608]{0:T(1024)(128)(4,1)}), s8[4194304]{0:T(1024)(128)(4,1)S(1)}, s32[]{:S(2)}) async-start(s8[8388608]{0:T(1024)(128)(4,1)} %bitcast.196), calls=%async_computation.2 | async-start | bytes 8388608
  164.1 79.4 %collective-permute-start.28 = (bf16[64,2048]{1,0:T(8,128)(2,1)S(1)}, bf16[64,2048]{1,0:T(8,128)(2,1)S(1)}, u32[]{:S(2)}, u32[]{:S(2)}) collective-permute-start(bf16[64,2048]{1,0:T(8,128)(2,1)S(1)} %bitcast_add_fusion.5), channel_id=1, source_target_pairs={{0,8},{4,12},{8,0},{12,4},{1,9},{5,13},{9,1},{13,5},{2,10},{6,14},... | collective-permute-start | bytes 786440 | tf_op jit(solution)/shard_map/backward/ppermute | solution.py:34
  170.4 23.9 %collective-permute-start.22 = (bf16[128,2048]{1,0:T(8,128)(2,1)S(1)}, bf16[128,2048]{1,0:T(8,128)(2,1)S(1)}, u32[]{:S(2)}, u32[]{:S(2)}) collective-permute-start(bf16[128,2048]{1,0:T(8,128)(2,1)S(1)} %dynamic-slice_bitcast_fusion.6), channel_id=1, source_target_pairs={{0,1},{1,0},{2,3},{3,2},{4,5},{5,4},{6,7},{7,6},{8,9},{9,8},{10,11... | collective-permute-start | bytes 1572872 | tf_op jit(solution)/shard_map/backward/ppermute | solution.py:31
  194.2 9.8 %collective-permute-start.30 = (bf16[128,2048]{1,0:T(8,128)(2,1)S(1)}, bf16[128,2048]{1,0:T(8,128)(2,1)S(1)}, u32[]{:S(2)}, u32[]{:S(2)}) collective-permute-start(bf16[128,2048]{1,0:T(8,128)(2,1)S(1)} %dynamic-slice_bitcast_fusion.4), channel_id=1, source_target_pairs={{0,1},{1,0},{2,3},{3,2},{4,5},{5,4},{6,7},{7,6},{8,9},{9,8},{10,11... | collective-permute-start | bytes 1572872 | tf_op jit(solution)/shard_map/backward/ppermute | solution.py:31
  194.4 11.5 %collective-permute-start.23 = (bf16[64,2048]{1,0:T(8,128)(2,1)S(1)}, bf16[64,2048]{1,0:T(8,128)(2,1)S(1)}, u32[]{:S(2)}, u32[]{:S(2)}) collective-permute-start(bf16[64,2048]{1,0:T(8,128)(2,1)S(1)} %dynamic-slice_bitcast_fusion.17), channel_id=1, source_target_pairs={{0,2},{1,3},{2,0},{3,1},{4,6},{5,7},{6,4},{7,5},{8,10},{9,11},{10,... | collective-permute-start | bytes 786440 | tf_op jit(solution)/shard_map/backward/ppermute | solution.py:31
  199.6 6.4 %collective-permute-start.11 = (bf16[256,2048]{1,0:T(8,128)(2,1)S(1)}, bf16[256,2048]{1,0:T(8,128)(2,1)S(1)}, u32[]{:S(2)}, u32[]{:S(2)}) collective-permute-start(bf16[256,2048]{1,0:T(8,128)(2,1)S(1)} %convolution_convert_fusion.6), channel_id=1, source_target_pairs={{12,8},{13,9},{14,10},{15,11},{28,24},{29,25},{30,26},{31,27}} | collective-permute-start | bytes 3145736 | tf_op jit(solution)/shard_map/forward/ppermute | solution.py:138
  202.7 27.9 %collective-permute-start.8 = (bf16[256,2048]{1,0:T(8,128)(2,1)S(1)}, bf16[256,2048]{1,0:T(8,128)(2,1)S(1)}, u32[]{:S(2)}, u32[]{:S(2)}) collective-permute-start(bf16[256,2048]{1,0:T(8,128)(2,1)S(1)} %convolution_convert_fusion.4), channel_id=1, source_target_pairs={{0,4},{1,5},{2,6},{3,7},{16,20},{17,21},{18,22},{19,23}} | collective-permute-start | bytes 3145736 | tf_op jit(solution)/shard_map/forward/ppermute | solution.py:137
  204.2 32.2 %collective-permute-start.31 = (bf16[64,2048]{1,0:T(8,128)(2,1)S(1)}, bf16[64,2048]{1,0:T(8,128)(2,1)S(1)}, u32[]{:S(2)}, u32[]{:S(2)}) collective-permute-start(bf16[64,2048]{1,0:T(8,128)(2,1)S(1)} %dynamic-slice_bitcast_fusion.15), channel_id=1, source_target_pairs={{0,2},{1,3},{2,0},{3,1},{4,6},{5,7},{6,4},{7,5},{8,10},{9,11},{10,... | collective-permute-start | bytes 786440 | tf_op jit(solution)/shard_map/backward/ppermute | solution.py:31
  206.0 37.5 %collective-permute-start.24 = (bf16[64,2048]{1,0:T(8,128)(2,1)S(1)}, bf16[64,2048]{1,0:T(8,128)(2,1)S(1)}, u32[]{:S(2)}, u32[]{:S(2)}) collective-permute-start(bf16[64,2048]{1,0:T(8,128)(2,1)S(1)} %bitcast_add_fusion.6), channel_id=1, source_target_pairs={{0,4},{4,8},{8,12},{12,0},{1,5},{5,9},{9,13},{13,1},{2,6},{6,10},{... | collective-permute-start | bytes 786440 | tf_op jit(solution)/shard_map/backward/ppermute | solution.py:34
  233.1 33.3 %collective-permute-start.9 = (bf16[256,2048]{1,0:T(8,128)(2,1)S(1)}, bf16[256,2048]{1,0:T(8,128)(2,1)S(1)}, u32[]{:S(2)}, u32[]{:S(2)}) collective-permute-start(bf16[256,2048]{1,0:T(8,128)(2,1)S(1)} %get-tuple-element.26), channel_id=1, source_target_pairs={{0,4},{4,8},{1,5},{5,9},{2,6},{6,10},{3,7},{7,11},{16,20},{20,24},... | collective-permute-start | bytes 3145736 | tf_op jit(solution)/shard_map/forward/ppermute | solution.py:137
  235.1 33.7 %collective-permute-start.12 = (bf16[256,2048]{1,0:T(8,128)(2,1)S(1)}, bf16[256,2048]{1,0:T(8,128)(2,1)S(1)}, u32[]{:S(2)}, u32[]{:S(2)}) collective-permute-start(bf16[256,2048]{1,0:T(8,128)(2,1)S(1)} %get-tuple-element.27), channel_id=1, source_target_pairs={{8,4},{12,8},{9,5},{13,9},{10,6},{14,10},{11,7},{15,11},{24,20},{2... | collective-permute-start | bytes 3145736 | tf_op jit(solution)/shard_map/forward/ppermute | solution.py:138
  236.4 29.9 %collective-permute-start.32 = (bf16[64,2048]{1,0:T(8,128)(2,1)S(1)}, bf16[64,2048]{1,0:T(8,128)(2,1)S(1)}, u32[]{:S(2)}, u32[]{:S(2)}) collective-permute-start(bf16[64,2048]{1,0:T(8,128)(2,1)S(1)} %bitcast_add_fusion.4), channel_id=1, source_target_pairs={{0,12},{4,0},{8,4},{12,8},{1,13},{5,1},{9,5},{13,9},{2,14},{6,2},{... | collective-permute-start | bytes 786440 | tf_op jit(solution)/shard_map/backward/ppermute | solution.py:34
  266.8 24.7 %collective-permute-start.10 = (bf16[256,2048]{1,0:T(8,128)(2,1)S(1)}, bf16[256,2048]{1,0:T(8,128)(2,1)S(1)}, u32[]{:S(2)}, u32[]{:S(2)}) collective-permute-start(bf16[256,2048]{1,0:T(8,128)(2,1)S(1)} %add.227), channel_id=1, source_target_pairs={{0,4},{4,8},{8,12},{1,5},{5,9},{9,13},{2,6},{6,10},{10,14},{3,7},{... | collective-permute-start | bytes 3145736 | tf_op jit(solution)/shard_map/forward/ppermute | solution.py:137
  269.2 24.7 %collective-permute-start.13 = (bf16[256,2048]{1,0:T(8,128)(2,1)S(1)}, bf16[256,2048]{1,0:T(8,128)(2,1)S(1)}, u32[]{:S(2)}, u32[]{:S(2)}) collective-permute-start(bf16[256,2048]{1,0:T(8,128)(2,1)S(1)} %add.230), channel_id=1, source_target_pairs={{4,0},{8,4},{12,8},{5,1},{9,5},{13,9},{6,2},{10,6},{14,10},{7,3},{... | collective-permute-start | bytes 3145736 | tf_op jit(solution)/shard_map/forward/ppermute | solution.py:138
  273.3 8.3 %collective-permute-start.33 = (bf16[64,2048]{1,0:T(8,128)(2,1)S(1)}, bf16[64,2048]{1,0:T(8,128)(2,1)S(1)}, u32[]{:S(2)}, u32[]{:S(2)}) collective-permute-start(bf16[64,2048]{1,0:T(8,128)(2,1)S(1)} %get-tuple-element.25), channel_id=1, source_target_pairs={{0,2},{1,3},{2,0},{3,1},{4,6},{5,7},{6,4},{7,5},{8,10},{9,11},{10,... | collective-permute-start | bytes 786440 | tf_op jit(solution)/shard_map/backward/ppermute | solution.py:31
  275.0 6.5 %collective-permute-start.34 = (bf16[64,2048]{1,0:T(8,128)(2,1)S(1)}, bf16[64,2048]{1,0:T(8,128)(2,1)S(1)}, u32[]{:S(2)}, u32[]{:S(2)}) collective-permute-start(bf16[64,2048]{1,0:T(8,128)(2,1)S(1)} %get-tuple-element.24), channel_id=1, source_target_pairs={{0,1},{1,0},{2,3},{3,2},{4,5},{5,4},{6,7},{7,6},{8,9},{9,8},{10,11... | collective-permute-start | bytes 786440 | tf_op jit(solution)/shard_map/backward/ppermute | solution.py:31
  275.0 9.3 %collective-permute-start.35 = (bf16[64,2048]{1,0:T(8,128)(2,1)S(1)}, bf16[64,2048]{1,0:T(8,128)(2,1)S(1)}, u32[]{:S(2)}, u32[]{:S(2)}) collective-permute-start(bf16[64,2048]{1,0:T(8,128)(2,1)S(1)} %get-tuple-element.23), channel_id=1, source_target_pairs={{0,3},{1,2},{2,1},{3,0},{4,7},{5,6},{6,5},{7,4},{8,11},{9,10},{10,... | collective-permute-start | bytes 786440 | tf_op jit(solution)/shard_map/backward/ppermute | solution.py:31
  (5 other events, 11.3 us)
Sparse Core Ops, SparseCore 0:
  56.7 43.2 all-gather.1

commit v2 on v1

v2 whole, which is shorter than its diff:
```python
import jax
import jax.numpy as jnp
from jax import lax
from jax.sharding import PartitionSpec as P

ADAPTER_COUNT = 32
BLOCK = 128
F32 = jnp.float32
BF16 = jnp.bfloat16


def bit_reversed(index, count):
    result = 0
    while count > 1:
        result = result * 2 + index % 2
        index, count = index // 2, count // 2
    return result


def pick(stacked, index):
    return lax.dynamic_index_in_dim(stacked, index, 0, keepdims=False)


def make_local(n):
    reversed_at = [bit_reversed(q, n) for q in range(n)]
    masks = []
    while 2 ** len(masks) < n:
        masks.append(2 ** len(masks))

    def swap(x, mask):
        return lax.ppermute(x, "tensor", [(t, t ^ mask) for t in range(n)])

    def rotate(x, k):
        return lax.ppermute(x, "dp", [(i, (i + k) % n) for i in range(n)])

    def local(
        tokens,
        query_weight,
        down_weights,
        up_weights,
        cotangent,
        adapter_of_block,
        block_live_count,
    ):
        blocks_here = adapter_of_block.shape[0]
        rows, width = tokens.shape
        columns = query_weight.shape[1]
        group = rows // n
        t = lax.axis_index("tensor")
        i = lax.axis_index("dp")
        positions = lax.broadcasted_iota(jnp.int32, (blocks_here, BLOCK), 1)
        live_mask = positions < block_live_count[:, None]
        grad_blocks = jnp.where(
            live_mask[:, :, None],
            cotangent.reshape(blocks_here, BLOCK, columns),
            jnp.zeros((), cotangent.dtype),
        )
        grad_flat = grad_blocks.reshape(rows, columns)

        with jax.named_scope("spread_tokens"):
            pieces = lax.all_to_all(
                jnp.stack([tokens[group * p : group * (p + 1)] for p in reversed_at]),
                "tensor",
                0,
                0,
            )
            by_source = {0: pick(pieces, i)}
            distances = sorted(range(1, n), key=lambda k: -abs(2 * k - n))
            for k in distances:
                by_source[n - k] = rotate(pick(pieces, (i + k) % n), k)
            near = [n - k for k in distances if k in (1, n - 1)]
            rest = [r for r in range(n) if r not in near]
            full = {}
            for batch in (near, rest):
                held = jnp.stack([by_source[r] for r in batch])[:, None]
                for mask in reversed(masks):
                    held = jnp.concatenate([held, swap(held, mask)], axis=1)
                for at, r in enumerate(batch):
                    full[r] = held[at].reshape(rows, width)
                last_held = held
        order = [0]
        for mask in reversed(masks):
            order = order + [k ^ mask for k in order]

        with jax.named_scope("spread_cotangent"):
            up, down = [grad_flat], [grad_flat]
            for s in range(1, n):
                up.append(lax.ppermute(up[-1], "dp", [(a, a + 1) for a in range(s - 1, n - 1)]))
                down.append(lax.ppermute(down[-1], "dp", [(a + 1, a) for a in range(n - s)]))
                if s == 1:
                    up[1], down[1], _ = lax.optimization_barrier(
                        (up[1], down[1], by_source[n // 2])
                    )
            grads = [grad_flat] + [
                jnp.where(i + r <= n - 1, down[r], up[n - r]) for r in range(1, n)
            ]

        with jax.named_scope("ranks"):
            token_blocks = tokens.reshape(blocks_here, BLOCK, width)
            chosen_down = down_weights[adapter_of_block]
            chosen_up = up_weights[adapter_of_block]
            ranks = jnp.stack(
                [
                    jnp.einsum(
                        "uqv,upv->upq", token_blocks, chosen_down, preferred_element_type=F32
                    ),
                    2.0
                    * jnp.einsum("bkq,brq->brk", grad_blocks, chosen_up, preferred_element_type=F32),
                ]
            )
            for mask in masks:
                ranks = ranks + swap(ranks, mask)
            ranks = ranks.astype(BF16)
            shrunk, grad_rank = ranks[0], ranks[1]

        with jax.named_scope("tables"):
            ids = jnp.broadcast_to(
                adapter_of_block[:, None, None].astype(BF16), (blocks_here, 1, width)
            )
            products = jnp.concatenate(
                [
                    jnp.einsum(
                        "pgz,pzq->pgq", grad_rank, token_blocks, preferred_element_type=F32
                    ).astype(BF16),
                    (
                        2.0
                        * jnp.einsum(
                            "brk,bkq->brq", shrunk, grad_blocks, preferred_element_type=F32
                        )
                    ).astype(BF16),
                    ids,
                ],
                axis=1,
            )
            products = lax.all_gather(products, "dp", axis=0, tiled=True)
            rank = shrunk.shape[1]
            ids = products[:, 2 * rank, 0].astype(jnp.int32)
            hits = (
                lax.broadcasted_iota(jnp.int32, (ADAPTER_COUNT, ids.shape[0]), 0) == ids[None, :]
            ).astype(BF16)
            grad_down = jnp.einsum(
                "ab,brd->ard", hits, products[:, :rank], preferred_element_type=F32
            )
            grad_up = jnp.einsum(
                "ab,brd->ard", hits, products[:, rank : 2 * rank], preferred_element_type=F32
            )

        with jax.named_scope("forward"):
            parts = {
                r: jnp.dot(full[r], query_weight, preferred_element_type=F32).astype(BF16)
                for r in range(1, n)
            }
            up_sum = down_sum = None
            for s in range(1, n):
                d = n - s
                send_up = parts[d] if up_sum is None else parts[d] + up_sum
                send_down = parts[n - d] if down_sum is None else parts[n - d] + down_sum
                up_sum = lax.ppermute(send_up, "dp", [(a, a + 1) for a in range(s)])
                down_sum = lax.ppermute(send_down, "dp", [(a, a - 1) for a in range(d, n)])
            own = jnp.dot(full[0], query_weight, preferred_element_type=F32)
            base = own + up_sum.astype(F32) + down_sum.astype(F32)
            base = base.reshape(n, group, columns)

        position = jnp.array([order.index(k) for k in range(n)], jnp.int32)
        natural = sorted(range(n), key=lambda q: reversed_at[q])

        def in_place(groups):
            return jnp.concatenate([pick(groups, position[q ^ t]) for q in natural], axis=0)

        adapter_output = 2.0 * jnp.einsum(
            "psw,psd->pwd", shrunk, chosen_up, preferred_element_type=F32
        )
        query = (in_place(base) + adapter_output.reshape(rows, columns)).astype(BF16)

        with jax.named_scope("backward"):
            early = [r for r in range(n) if r in (0, n // 2)]
            late = [r for r in range(n) if r not in early]
            sums = {}
            for batch in (early, late):
                held = jnp.stack([grads[r] for r in batch]).reshape(-1, columns)
                if batch is early:
                    held, _ = lax.optimization_barrier((held, last_held))
                value = (
                    lax.dot_general(
                        held, query_weight, (((1,), (1,)), ((), ())), preferred_element_type=F32
                    )
                    .astype(BF16)
                    .reshape(len(batch), rows, width)
                )
                for mask in masks:
                    halves = value.reshape(len(batch), 2, value.shape[1] // 2, width)
                    bit = (t // mask) % 2
                    value = lax.dynamic_index_in_dim(halves, bit, 1, keepdims=False) + swap(
                        lax.dynamic_index_in_dim(halves, 1 - bit, 1, keepdims=False), mask
                    )
                for at, r in enumerate(batch):
                    sums[r] = value[at]
            sums = jnp.stack([sums[r] for r in range(n)])
            back = []
            for m in range(n):
                back.append(
                    lax.ppermute(
                        pick(sums, (t + m) % n),
                        ("dp", "tensor"),
                        [
                            (a * n + b, ((a + b + m) % n) * n + a)
                            for a in range(n)
                            for b in range(n)
                        ],
                    )
                )
            back = jnp.stack(back).astype(F32)
            returned = jnp.concatenate([pick(back, (i - t - q) % n) for q in natural], axis=0)
            adapter_backward = jnp.einsum(
                "jxq,jxo->jqo", grad_rank, chosen_down, preferred_element_type=F32
            )
            token_gradient = (returned + adapter_backward.reshape(rows, width)).astype(BF16)
        return (query, token_gradient, grad_down, grad_up)

    return local


def solution(mesh):
    assert mesh.shape["dp"] == mesh.shape["tensor"]
    return jax.shard_map(
        make_local(mesh.shape["tensor"]),
        mesh=mesh,
        in_specs=(
            P(("parts", "dp"), "tensor"),
            P("dp", "tensor"),
            P("parts", None, "tensor"),
            P("parts", None, "tensor"),
            P(("parts", "dp"), "tensor"),
            P(("parts", "dp")),
            P(("parts", "dp")),
        ),
        out_specs=(
            P(("parts", "dp"), "tensor"),
            P(("parts", "dp"), "tensor"),
            P("parts", None, "tensor"),
            P("parts", None, "tensor"),
        ),
        check_vma=False,
    )
```

time: 312 us -> 268 us (0.86)
  waiting for transfers between devices: 159 us -> 109 us
  starting transfers between devices: 44.5 us -> 54.7 us
  other arithmetic: 12.4 us -> 20.9 us
  blocking collectives: 8.48 us -> 0 us
    ppermute x6 -> x3, waiting for transfers between devices: 78.8 us -> 27.3 us  [rotate(): return lax.ppermute(x, 'dp', [(i, (i + k) % n) for i in range(n)])]
    ppermute x0 -> x4, waiting for transfers between devices: none -> 21.8 us  [local(): lax.ppermute(pick(sums, (t + m) % n), ('dp', 'tensor'), [(a * n + b, (a +...]
    ppermute x18 -> x10, waiting for transfers between devices: 26.9 us -> 15.2 us  [swap(): return lax.ppermute(x, 'tensor', [(t, t ^ mask) for t in range(n)])]
    ppermute x0 -> x4, starting transfers between devices: none -> 10.5 us  [local(): lax.ppermute(pick(sums, (t + m) % n), ('dp', 'tensor'), [(a * n + b, (a +...]
    ppermute x3, waiting for transfers between devices: 31.4 us -> 21 us  [local(): up_sum = lax.ppermute(send_up, 'dp', [(a, a + 1) for a in range(s)])]
    all_to_all x0 -> x1, waiting for transfers between devices: none -> 10 us  [local(): lax.all_to_all(jnp.stack([tokens[group * p:group * (p + 1)] for p in reve...]
    unnamed x1 -> x0, blocking collectives: 8.48 us -> none
    ppermute x3, waiting for transfers between devices: 20 us -> 12.6 us  [local(): lax.ppermute(down[-1], 'dp', [(a + 1, a) for a in range(n - s)])]
  transfers between devices with their start and end apart: 37 -> 31, of which waited for: 12 -> 12; matrix products, arithmetic and copies ran while one was open for 20% -> 26% of each run, Pallas kernels for 0% -> 0%
where the time goes in v2:
time: 268 us; the launch traced here: 267 us
  waiting for transfers between devices  109 us (41%)
  starting transfers between devices  54.7 us (20%)
  matrix products  41.4 us (15%)
  between operations  22.6 us (8%)
  other arithmetic  20.9 us (8%)
  local copies, waits for them, and re-layouts  17.8 us (7%)
    ppermute x3, waiting for transfers between devices, rotate(): return lax.ppermute(x, 'dp', [(i, (i + k) % n) for i in range(n)])  27.3 us
    ppermute x4, waiting for transfers between devices, local(): lax.ppermute(pick(sums, (t + m) % n), ('dp', 'tensor'), [(a * n + b, (a +...  21.8 us
    ppermute x3, waiting for transfers between devices, local(): up_sum = lax.ppermute(send_up, 'dp', [(a, a + 1) for a in range(s)])  21 us
    dot_general x2, matrix products, local(): lax.dot_general(held, query_weight, (((1,), (1,)), ((), ())), preferred_e...  16.3 us
    ppermute x10, waiting for transfers between devices, swap(): return lax.ppermute(x, 'tensor', [(t, t ^ mask) for t in range(n)])  15.2 us
    dot_general x3, matrix products, local(): jnp.dot(full[r], query_weight, preferred_element_type=F32).astype(BF16)  14 us
    ppermute x3, waiting for transfers between devices, local(): lax.ppermute(down[-1], 'dp', [(a + 1, a) for a in range(n - s)])  12.6 us
    unnamed x32, local copies, waits for them, and re-layouts  11 us
  transfers between devices with their start and end apart: 31, of which 12 were waited for; matrix products, arithmetic and copies ran while one was open for 26% of the time, Pallas kernels for 0%

profile of v2, /device:TPU:10, one launch (start us, length us, event | category | flops | bytes accessed | tf_op | source)
XLA Modules:
  0.0 266.6 jit_solution(6125121014021380979)
XLA Ops:
  8.1 2.4 broadcast_select_fusion
  10.5 3.5 %collective-permute-start.15 = (bf16[256,2048]{1,0:T(8,128)(2,1)}, bf16[256,2048]{1,0:T(8,128)(2,1)}, u32[]{:S(2)}, u32[]{:S(2)}) collective-permute-start(bf16[256,2048]{1,0:T(8,128)(2,1)} %broadcast_select_fusion), channel_id=1, source_target_pairs={{0,4},{4,8},{8,12},{1,5},{5,9},{9,13},{2,6},{6,10},{10,14},{3,7},{... | collective-permute-start | bytes 3145736 | tf_op jit(solution)/shard_map/spread_cotangent/ppermute | solution.py:88
  14.0 3.4 %collective-permute-start.16 = (bf16[256,2048]{1,0:T(8,128)(2,1)}, bf16[256,2048]{1,0:T(8,128)(2,1)}, u32[]{:S(2)}, u32[]{:S(2)}) collective-permute-start(bf16[256,2048]{1,0:T(8,128)(2,1)} %broadcast_select_fusion), channel_id=1, source_target_pairs={{4,0},{8,4},{12,8},{5,1},{9,5},{13,9},{6,2},{10,6},{14,10},{7,3},{... | collective-permute-start | bytes 3145736 | tf_op jit(solution)/shard_map/spread_cotangent/ppermute | solution.py:89
  18.5 2.1 gather_fusion
  21.0 1.7 fusion.4
  25.6 5.1 %all-to-all-start = ((bf16[4,64,2048]{2,1,0:T(8,128)(2,1)}), bf16[4,64,2048]{2,1,0:T(8,128)(2,1)S(1)}, u32[]{:S(2)}, u32[]{:S(2)}) async-start(bf16[4,64,2048]{2,1,0:T(8,128)(2,1)} %pad_maximum_fusion.4), calls=%async_computation | async-start | bytes 2097152 | tf_op jit(solution)/shard_map/spread_tokens/all_to_all | solution.py:61
  33.5 10.0 %all-to-all-done = bf16[4,64,2048]{2,1,0:T(8,128)(2,1)S(1)} async-done(((bf16[4,64,2048]{2,1,0:T(8,128)(2,1)}), bf16[4,64,2048]{2,1,0:T(8,128)(2,1)S(1)}, u32[]{:S(2)}, u32[]{:S(2)}) %all-to-all-start) | async-done | bytes 1048608 | tf_op jit(solution)/shard_map/spread_tokens/all_to_all | solution.py:61
  43.6 2.6 collective-permute-start
  55.0 2.0 collective-permute-start.3
  57.0 18.7 %collective-permute-done = bf16[64,2048]{1,0:T(8,128)(2,1)} collective-permute-done((bf16[64,2048]{1,0:T(8,128)(2,1)S(1)}, bf16[64,2048]{1,0:T(8,128)(2,1)}, u32[]{:S(2)}, u32[]{:S(2)}) %collective-permute-start) | collective-permute-done | bytes 262176 | tf_op jit(solution)/shard_map/spread_tokens/ppermute | solution.py:34
  76.7 1.4 collective-permute-start.1
  78.1 1.8 convolution_multiply_fusion
  80.0 8.6 %collective-permute-done.4 = bf16[64,2048]{1,0:T(8,128)(2,1)S(1)} collective-permute-done((bf16[64,2048]{1,0:T(8,128)(2,1)S(1)}, bf16[64,2048]{1,0:T(8,128)(2,1)S(1)}, u32[]{:S(2)}, u32[]{:S(2)}) %collective-permute-start.4) | collective-permute-done | bytes 262176 | tf_op jit(solution)/shard_map/spread_tokens/ppermute | solution.py:34
  89.5 1.8 fusion.11
  91.3 1.9 collective-permute-start.17
  93.2 5.9 %collective-permute-start.18 = (bf16[256,2048]{1,0:T(8,128)(2,1)}, bf16[256,2048]{1,0:T(8,128)(2,1)}, u32[]{:S(2)}, u32[]{:S(2)}) collective-permute-start(bf16[256,2048]{1,0:T(8,128)(2,1)} %collective-permute-done.15), channel_id=1, source_target_pairs={{4,8},{8,12},{5,9},{9,13},{6,10},{10,14},{7,11},{11,15},{20,24},{2... | collective-permute-start | bytes 3145736 | tf_op jit(solution)/shard_map/spread_cotangent/ppermute | solution.py:88
  100.3 2.1 collective-permute-done.5
  105.6 12.6 %collective-permute-done.17 = bf16[256,2048]{1,0:T(8,128)(2,1)} collective-permute-done((bf16[256,2048]{1,0:T(8,128)(2,1)}, bf16[256,2048]{1,0:T(8,128)(2,1)}, u32[]{:S(2)}, u32[]{:S(2)}) %collective-permute-start.17) | collective-permute-done | bytes 1048608 | tf_op jit(solution)/shard_map/spread_cotangent/ppermute | solution.py:89
  118.2 2.3 collective-permute-start.22
  121.2 1.3 select_bitcast_fusion.2
  122.8 1.4 pad_maximum_fusion
  124.2 8.2 %convolution_convert_fusion.1 = bf16[512,2048]{1,0:T(8,128)(2,1)S(1)} fusion(bf16[512,2048]{1,0:T(8,128)(2,1)S(1)} %bitcast.142, bf16[2048,2048]{1,0:T(8,128)(2,1)} %param.9), kind=kOutput, calls=%fused_computation.3 | convolution fusion | flops 4296015872 | bytes 12582912 | tf_op jit(solution)/shard_map/backward/dot_general | solution.py:184
  132.5 1.4 pad_maximum_fusion.1
  134.3 5.9 %convolution_convert_fusion.4 = bf16[256,2048]{1,0:T(8,128)(2,1)S(1)} fusion(bf16[256,2048]{1,0:T(8,128)(2,1)S(1)} %bitcast.148, bf16[2048,2048]{1,0:T(8,128)(2,1)} %param.9), kind=kOutput, calls=%fused_computation.9 | convolution fusion | flops 2148007936 | bytes 10485760 | tf_op jit(solution)/shard_map/forward/dot_general | solution.py:150
  141.1 2.4 convolution_convert_fusion.2
  145.1 1.4 select_bitcast_fusion
  146.4 1.3 select_bitcast_fusion.1
  148.0 8.1 %convolution_convert_fusion = bf16[512,2048]{1,0:T(8,128)(2,1)S(1)} fusion(bf16[512,2048]{1,0:T(8,128)(2,1)S(1)} %bitcast.143, bf16[2048,2048]{1,0:T(8,128)(2,1)} %param.9), kind=kOutput, calls=%fused_computation.2 | convolution fusion | flops 4296015872 | bytes 12582912 | tf_op jit(solution)/shard_map/backward/dot_general | solution.py:184
  158.2 12.8 %collective-permute-done.7 = bf16[256,2048]{1,0:T(8,128)(2,1)S(1)} collective-permute-done((bf16[256,2048]{1,0:T(8,128)(2,1)S(1)}, bf16[256,2048]{1,0:T(8,128)(2,1)S(1)}, u32[]{:S(2)}, u32[]{:S(2)}) %collective-permute-start.7) | collective-permute-done | bytes 1048608 | tf_op jit(solution)/shard_map/forward/ppermute | solution.py:158
  170.9 5.8 %fusion.25 = (bf16[256,2048]{1,0:T(8,128)(2,1)S(1)}, bf16[256,2048]{1,0:T(8,128)(2,1)S(1)}) fusion(bf16[256,2048]{1,0:T(8,128)(2,1)S(1)} %collective-permute-done.7, bf16[256,2048]{1,0:T(8,128)(2,1)S(1)} %collective-permute-done.10, bf16[256,2048]{1,0:T(8,128)(2,1)S(1)} %bitcast.146, bf16[2048,2048]{1,0:T(8,128)(2,1)} %param.9), kind=kOutput, calls=%fused_computation.92 | convolution fusion | flops 2149056512 | bytes 13631488 | tf_op jit(solution)/shard_map/forward/dot_general | solution.py:150
  176.7 2.4 collective-permute-start.8
  179.1 1.3 collective-permute-start.11
  182.0 12.0 %collective-permute-done.24 = bf16[2,64,2048]{2,1,0:T(8,128)(2,1)S(1)} collective-permute-done((bf16[2,64,2048]{2,1,0:T(8,128)(2,1)S(1)}, bf16[2,64,2048]{2,1,0:T(8,128)(2,1)S(1)}, u32[]{:S(2)}, u32[]{:S(2)}) %collective-permute-start.24) | collective-permute-done | bytes 524320 | tf_op jit(solution)/shard_map/backward/ppermute | solution.py:31
  194.3 2.1 collective-permute-start.25
  196.5 8.2 %collective-permute-done.8 = bf16[256,2048]{1,0:T(8,128)(2,1)S(1)} collective-permute-done((bf16[256,2048]{1,0:T(8,128)(2,1)S(1)}, bf16[256,2048]{1,0:T(8,128)(2,1)S(1)}, u32[]{:S(2)}, u32[]{:S(2)}) %collective-permute-start.8) | collective-permute-done | bytes 1048608 | tf_op jit(solution)/shard_map/forward/ppermute | solution.py:158
  205.1 1.9 collective-permute-start.9
  207.0 1.3 collective-permute-done.11
  208.7 2.9 %collective-permute-start.12 = (bf16[256,2048]{1,0:T(8,128)(2,1)S(1)}, bf16[256,2048]{1,0:T(8,128)(2,1)S(1)}, u32[]{:S(2)}, u32[]{:S(2)}) collective-permute-start(bf16[256,2048]{1,0:T(8,128)(2,1)S(1)} %add.210), channel_id=1, source_target_pairs={{4,0},{8,4},{12,8},{5,1},{9,5},{13,9},{6,2},{10,6},{14,10},{7,3},{... | collective-permute-start | bytes 3145736 | tf_op jit(solution)/shard_map/forward/ppermute | solution.py:159
  212.5 4.4 %copy.22 = f32[32,16,2048]{2,1,0:T(8,128)} copy(f32[32,16,2048]{2,0,1:T(8,128)S(1)} %fusion.7) | data formatting | bytes 8388608
  216.9 1.9 collective-permute-start.26
  218.8 1.9 collective-permute-start.27
  220.8 4.5 %collective-permute-start.28 = (bf16[64,2048]{1,0:T(8,128)(2,1)S(1)}, bf16[64,2048]{1,0:T(8,128)(2,1)S(1)}, u32[]{:S(2)}, u32[]{:S(2)}) collective-permute-start(bf16[64,2048]{1,0:T(8,128)(2,1)S(1)} %get-tuple-element.37), channel_id=1, source_target_pairs={{0,12},{1,0},{2,4},{3,8},{4,1},{5,5},{6,9},{7,13},{8,6},{9,10},{10... | collective-permute-start | bytes 786440 | tf_op jit(solution)/shard_map/backward/ppermute | solution.py:202
  226.2 4.4 %copy.23 = f32[32,16,2048]{2,1,0:T(8,128)} copy(f32[32,16,2048]{2,0,1:T(8,128)S(1)} %fusion.5) | data formatting | bytes 8388608
  230.6 19.9 %collective-permute-done.26 = bf16[64,2048]{1,0:T(8,128)(2,1)S(1)} collective-permute-done((bf16[64,2048]{1,0:T(8,128)(2,1)S(1)}, bf16[64,2048]{1,0:T(8,128)(2,1)S(1)}, u32[]{:S(2)}, u32[]{:S(2)}) %collective-permute-start.26) | collective-permute-done | bytes 262176 | tf_op jit(solution)/shard_map/backward/ppermute | solution.py:202
  250.5 1.9 collective-permute-done.28
  252.8 2.5 fusion
  255.4 1.4 copy-done.3
  257.5 2.2 fusion.2
  (112 shorter events, 26.6 us)
Async XLA Ops:
  7.2 10.7 %copy-start = (bf16[32,16,2048]{2,1,0:T(8,128)(2,1)S(1)}, bf16[32,16,2048]{2,1,0:T(8,128)(2,1)}, u32[]{:S(2)}) copy-start(bf16[32,16,2048]{2,1,0:T(8,128)(2,1)} %param.11) | copy-start | bytes 6291460
  7.2 10.2 %copy-start.9 = (s32[2]{0:T(128)S(1)}, s32[2]{0:T(128)}, u32[]{:S(2)}) copy-start(s32[2]{0:T(128)} %param.13) | copy-start | bytes 28
  7.2 13.4 %copy-start.2 = (bf16[256,2048]{1,0:T(8,128)(2,1)S(1)}, bf16[256,2048]{1,0:T(8,128)(2,1)}, u32[]{:S(2)}) copy-start(bf16[256,2048]{1,0:T(8,128)(2,1)} %param.8) | copy-start | bytes 3145732
  8.1 9.8 %copy-start.7 = (pred[256]{0:T(512)(128)(4,1)}, pred[256]{0:T(512)(128)(4,1)S(1)}, u32[]{:S(2)}) copy-start(pred[256]{0:T(512)(128)(4,1)S(1)} %get-tuple-element.56) | copy-start | bytes 772
  8.1 14.6 %copy-start.10 = (pred[2,128]{1,0:T(4,128)(4,1)}, pred[2,128]{1,0:T(4,128)(4,1)S(1)}, u32[]{:S(2)}) copy-start(pred[2,128]{1,0:T(4,128)(4,1)S(1)} %get-tuple-element.57) | copy-start | bytes 772
  10.5 80.8 %collective-permute-start.15 = (bf16[256,2048]{1,0:T(8,128)(2,1)}, bf16[256,2048]{1,0:T(8,128)(2,1)}, u32[]{:S(2)}, u32[]{:S(2)}) collective-permute-start(bf16[256,2048]{1,0:T(8,128)(2,1)} %broadcast_select_fusion), channel_id=1, source_target_pairs={{0,4},{4,8},{8,12},{1,5},{5,9},{9,13},{2,6},{6,10},{10,14},{3,7},{... | collective-permute-start | bytes 3145736 | tf_op jit(solution)/shard_map/spread_cotangent/ppermute | solution.py:88
  14.0 77.4 %collective-permute-start.16 = (bf16[256,2048]{1,0:T(8,128)(2,1)}, bf16[256,2048]{1,0:T(8,128)(2,1)}, u32[]{:S(2)}, u32[]{:S(2)}) collective-permute-start(bf16[256,2048]{1,0:T(8,128)(2,1)} %broadcast_select_fusion), channel_id=1, source_target_pairs={{4,0},{8,4},{12,8},{5,1},{9,5},{13,9},{6,2},{10,6},{14,10},{7,3},{... | collective-permute-start | bytes 3145736 | tf_op jit(solution)/shard_map/spread_cotangent/ppermute | solution.py:89
  22.7 1.3 collective-permute-start.13
  24.0 6.8 %collective-permute-start.14 = (f32[2,2,16,128]{3,2,1,0:T(8,128)S(1)}, f32[2,2,16,128]{3,2,1,0:T(8,128)S(1)}, u32[]{:S(2)}, u32[]{:S(2)}) collective-permute-start(f32[2,2,16,128]{3,2,1,0:T(8,128)S(1)} %fusion.21), channel_id=1, source_target_pairs={{0,2},{1,3},{2,0},{3,1},{4,6},{5,7},{6,4},{7,5},{8,10},{9,11},{10,... | collective-permute-start | bytes 98312 | tf_op jit(solution)/shard_map/ranks/ppermute | solution.py:31
  25.6 5.4 %copy-start.5 = (bf16[256,2048]{1,0:T(8,128)(2,1)S(1)}, bf16[256,2048]{1,0:T(8,128)(2,1)}, u32[]{:S(2)}) copy-start(bf16[256,2048]{1,0:T(8,128)(2,1)} %param.12) | copy-start | bytes 3145732
  25.6 17.9 %all-to-all-start = ((bf16[4,64,2048]{2,1,0:T(8,128)(2,1)}), bf16[4,64,2048]{2,1,0:T(8,128)(2,1)S(1)}, u32[]{:S(2)}, u32[]{:S(2)}) async-start(bf16[4,64,2048]{2,1,0:T(8,128)(2,1)} %pad_maximum_fusion.4), calls=%async_computation | async-start | bytes 2097152 | tf_op jit(solution)/shard_map/spread_tokens/all_to_all | solution.py:61
  30.7 72.6 %all-gather.2.cloned.1.call-start = ((), (), s32[]{:S(2)}) async-start(), calls=%async_computation.1 | async-start | bytes 1638400 | tf_op jit(solution)/shard_map/tables/all_gather | solution.py:135
  31.0 15.2 %copy-start.8 = (pred[256]{0:T(512)(128)(4,1)S(1)}, pred[256]{0:T(512)(128)(4,1)}, u32[]{:S(2)}) copy-start(pred[256]{0:T(512)(128)(4,1)} %copy-done.7) | copy-start | bytes 772
  33.5 13.1 %copy-start.6 = (s32[4]{0:T(128)S(1)}, s32[4]{0:T(128)}, u32[]{:S(2)}) copy-start(s32[4]{0:T(128)} %constant.178.clone) | copy-start | bytes 52
  43.6 32.1 %collective-permute-start = (bf16[64,2048]{1,0:T(8,128)(2,1)S(1)}, bf16[64,2048]{1,0:T(8,128)(2,1)}, u32[]{:S(2)}, u32[]{:S(2)}) collective-permute-start(bf16[64,2048]{1,0:T(8,128)(2,1)S(1)} %get-tuple-element.44), channel_id=1, source_target_pairs={{0,8},{4,12},{8,0},{12,4},{1,9},{5,13},{9,1},{13,5},{2,10},{6,14},... | collective-permute-start | bytes 786440 | tf_op jit(solution)/shard_map/spread_tokens/ppermute | solution.py:34
  55.0 33.6 %collective-permute-start.4 = (bf16[64,2048]{1,0:T(8,128)(2,1)S(1)}, bf16[64,2048]{1,0:T(8,128)(2,1)S(1)}, u32[]{:S(2)}, u32[]{:S(2)}) collective-permute-start(bf16[64,2048]{1,0:T(8,128)(2,1)S(1)} %get-tuple-element.43), channel_id=1, source_target_pairs={{0,12},{4,0},{8,4},{12,8},{1,13},{5,1},{9,5},{13,9},{2,14},{6,2},{... | collective-permute-start | bytes 786440 | tf_op jit(solution)/shard_map/spread_tokens/ppermute | solution.py:34
  55.0 33.6 %collective-permute-start.3 = (bf16[64,2048]{1,0:T(8,128)(2,1)S(1)}, bf16[64,2048]{1,0:T(8,128)(2,1)S(1)}, u32[]{:S(2)}, u32[]{:S(2)}) collective-permute-start(bf16[64,2048]{1,0:T(8,128)(2,1)S(1)} %get-tuple-element.42), channel_id=1, source_target_pairs={{0,4},{4,8},{8,12},{12,0},{1,5},{5,9},{9,13},{13,1},{2,6},{6,10},{... | collective-permute-start | bytes 786440 | tf_op jit(solution)/shard_map/spread_tokens/ppermute | solution.py:34
  76.7 22.5 %collective-permute-start.1 = (bf16[2,1,64,2048]{3,2,0,1:T(8,128)(2,1)S(1)}, bf16[2,1,64,2048]{3,2,0,1:T(8,128)(2,1)S(1)}, u32[]{:S(2)}, u32[]{:S(2)}) collective-permute-start(bf16[2,1,64,2048]{3,2,0,1:T(8,128)(2,1)S(1)} %maximum_bitcast_fusion), channel_id=1, source_target_pairs={{0,2},{1,3},{2,0},{3,1},{4,6},{5,7},{6,4},{7,5},{8,10},{9,11},{10,... | collective-permute-start | bytes 1572872 | tf_op jit(solution)/shard_map/spread_tokens/ppermute | solution.py:31
  88.6 13.7 %collective-permute-start.5 = (bf16[2,1,64,2048]{3,2,0,1:T(8,128)(2,1)S(1)}, bf16[2,1,64,2048]{3,2,0,1:T(8,128)(2,1)S(1)}, u32[]{:S(2)}, u32[]{:S(2)}) collective-permute-start(bf16[2,1,64,2048]{3,2,0,1:T(8,128)(2,1)S(1)} %maximum_bitcast_fusion.1), channel_id=1, source_target_pairs={{0,2},{1,3},{2,0},{3,1},{4,6},{5,7},{6,4},{7,5},{8,10},{9,11},{10,... | collective-permute-start | bytes 1572872 | tf_op jit(solution)/shard_map/spread_tokens/ppermute | solution.py:31
  91.3 26.9 %collective-permute-start.17 = (bf16[256,2048]{1,0:T(8,128)(2,1)}, bf16[256,2048]{1,0:T(8,128)(2,1)}, u32[]{:S(2)}, u32[]{:S(2)}) collective-permute-start(bf16[256,2048]{1,0:T(8,128)(2,1)} %collective-permute-done.16), channel_id=1, source_target_pairs={{4,0},{8,4},{5,1},{9,5},{6,2},{10,6},{7,3},{11,7},{20,16},{24,20},... | collective-permute-start | bytes 3145736 | tf_op jit(solution)/shard_map/spread_cotangent/ppermute | solution.py:89
  93.2 27.2 %collective-permute-start.18 = (bf16[256,2048]{1,0:T(8,128)(2,1)}, bf16[256,2048]{1,0:T(8,128)(2,1)}, u32[]{:S(2)}, u32[]{:S(2)}) collective-permute-start(bf16[256,2048]{1,0:T(8,128)(2,1)} %collective-permute-done.15), channel_id=1, source_target_pairs={{4,8},{8,12},{5,9},{9,13},{6,10},{10,14},{7,11},{11,15},{20,24},{2... | collective-permute-start | bytes 3145736 | tf_op jit(solution)/shard_map/spread_cotangent/ppermute | solution.py:88
  100.2 22.5 %collective-permute-start.2 = (bf16[2,2,64,2048]{3,2,0,1:T(8,128)(2,1)}, bf16[2,2,64,2048]{3,2,0,1:T(8,128)(2,1)}, u32[]{:S(2)}, u32[]{:S(2)}) collective-permute-start(bf16[2,2,64,2048]{3,2,0,1:T(8,128)(2,1)} %pad_maximum_fusion.5), channel_id=1, source_target_pairs={{0,1},{1,0},{2,3},{3,2},{4,5},{5,4},{6,7},{7,6},{8,9},{9,8},{10,11... | collective-permute-start | bytes 3145736 | tf_op jit(solution)/shard_map/spread_tokens/ppermute | solution.py:31
  103.4 29.2 %collective-permute-start.6 = (bf16[2,2,64,2048]{3,2,0,1:T(8,128)(2,1)}, bf16[2,2,64,2048]{3,2,0,1:T(8,128)(2,1)}, u32[]{:S(2)}, u32[]{:S(2)}) collective-permute-start(bf16[2,2,64,2048]{3,2,0,1:T(8,128)(2,1)} %pad_maximum_fusion.6), channel_id=1, source_target_pairs={{0,1},{1,0},{2,3},{3,2},{4,5},{5,4},{6,7},{7,6},{8,9},{9,8},{10,11... | collective-permute-start | bytes 3145736 | tf_op jit(solution)/shard_map/spread_tokens/ppermute | solution.py:31
  118.2 26.9 %collective-permute-start.22 = (bf16[256,2048]{1,0:T(8,128)(2,1)}, bf16[256,2048]{1,0:T(8,128)(2,1)S(1)}, u32[]{:S(2)}, u32[]{:S(2)}) collective-permute-start(bf16[256,2048]{1,0:T(8,128)(2,1)} %collective-permute-done.17), channel_id=1, source_target_pairs={{4,0},{5,1},{6,2},{7,3},{20,16},{21,17},{22,18},{23,19}} | collective-permute-start | bytes 3145736 | tf_op jit(solution)/shard_map/spread_cotangent/ppermute | solution.py:89
  120.5 26.0 %collective-permute-start.21 = (bf16[256,2048]{1,0:T(8,128)(2,1)}, bf16[256,2048]{1,0:T(8,128)(2,1)S(1)}, u32[]{:S(2)}, u32[]{:S(2)}) collective-permute-start(bf16[256,2048]{1,0:T(8,128)(2,1)} %collective-permute-done.18), channel_id=1, source_target_pairs={{8,12},{9,13},{10,14},{11,15},{24,28},{25,29},{26,30},{27,31}} | collective-permute-start | bytes 3145736 | tf_op jit(solution)/shard_map/spread_cotangent/ppermute | solution.py:88
  132.5 24.3 %collective-permute-start.19 = (bf16[2,128,2048]{2,1,0:T(8,128)(2,1)S(1)}, bf16[2,128,2048]{2,1,0:T(8,128)(2,1)S(1)}, u32[]{:S(2)}, u32[]{:S(2)}) collective-permute-start(bf16[2,128,2048]{2,1,0:T(8,128)(2,1)S(1)} %dynamic-slice_bitcast_fusion.1), channel_id=1, source_target_pairs={{0,1},{1,0},{2,3},{3,2},{4,5},{5,4},{6,7},{7,6},{8,9},{9,8},{10,11... | collective-permute-start | bytes 3145736 | tf_op jit(solution)/shard_map/backward/ppermute | solution.py:31
  134.0 7.1 %slice-start = ((s8[8388608]{0:T(1024)(128)(4,1)}), s8[4194304]{0:T(1024)(128)(4,1)S(1)}, s32[]{:S(2)}) async-start(s8[8388608]{0:T(1024)(128)(4,1)} %bitcast.155), calls=%async_computation.2 | async-start | bytes 8388608
  134.2 6.8 %slice-start.1 = ((s8[8388608]{0:T(1024)(128)(4,1)}), s8[4194304]{0:T(1024)(128)(4,1)S(1)}, s32[]{:S(2)}) async-start(s8[8388608]{0:T(1024)(128)(4,1)} %bitcast.155), calls=%async_computation.3 | async-start | bytes 8388608
  140.1 18.1 %collective-permute-start.10 = (bf16[256,2048]{1,0:T(8,128)(2,1)S(1)}, bf16[256,2048]{1,0:T(8,128)(2,1)S(1)}, u32[]{:S(2)}, u32[]{:S(2)}) collective-permute-start(bf16[256,2048]{1,0:T(8,128)(2,1)S(1)} %convolution_convert_fusion.4), channel_id=1, source_target_pairs={{12,8},{13,9},{14,10},{15,11},{28,24},{29,25},{30,26},{31,27}} | collective-permute-start | bytes 3145736 | tf_op jit(solution)/shard_map/forward/ppermute | solution.py:159
  143.5 27.4 %collective-permute-start.7 = (bf16[256,2048]{1,0:T(8,128)(2,1)S(1)}, bf16[256,2048]{1,0:T(8,128)(2,1)S(1)}, u32[]{:S(2)}, u32[]{:S(2)}) collective-permute-start(bf16[256,2048]{1,0:T(8,128)(2,1)S(1)} %convolution_convert_fusion.2), channel_id=1, source_target_pairs={{0,4},{1,5},{2,6},{3,7},{16,20},{17,21},{18,22},{19,23}} | collective-permute-start | bytes 3145736 | tf_op jit(solution)/shard_map/forward/ppermute | solution.py:158
  156.2 24.2 %collective-permute-start.23 = (bf16[2,128,2048]{2,1,0:T(8,128)(2,1)S(1)}, bf16[2,128,2048]{2,1,0:T(8,128)(2,1)S(1)}, u32[]{:S(2)}, u32[]{:S(2)}) collective-permute-start(bf16[2,128,2048]{2,1,0:T(8,128)(2,1)S(1)} %dynamic-slice_bitcast_fusion), channel_id=1, source_target_pairs={{0,1},{1,0},{2,3},{3,2},{4,5},{5,4},{6,7},{7,6},{8,9},{9,8},{10,11... | collective-permute-start | bytes 3145736 | tf_op jit(solution)/shard_map/backward/ppermute | solution.py:31
  157.0 24.9 %collective-permute-start.20 = (bf16[2,64,2048]{2,1,0:T(8,128)(2,1)S(1)}, bf16[2,64,2048]{2,1,0:T(8,128)(2,1)S(1)}, u32[]{:S(2)}, u32[]{:S(2)}) collective-permute-start(bf16[2,64,2048]{2,1,0:T(8,128)(2,1)S(1)} %dynamic-slice_bitcast_fusion.7), channel_id=1, source_target_pairs={{0,2},{1,3},{2,0},{3,1},{4,6},{5,7},{6,4},{7,5},{8,10},{9,11},{10,... | collective-permute-start | bytes 1572872 | tf_op jit(solution)/shard_map/backward/ppermute | solution.py:31
  176.7 28.0 %collective-permute-start.8 = (bf16[256,2048]{1,0:T(8,128)(2,1)S(1)}, bf16[256,2048]{1,0:T(8,128)(2,1)S(1)}, u32[]{:S(2)}, u32[]{:S(2)}) collective-permute-start(bf16[256,2048]{1,0:T(8,128)(2,1)S(1)} %get-tuple-element.40), channel_id=1, source_target_pairs={{0,4},{4,8},{1,5},{5,9},{2,6},{6,10},{3,7},{7,11},{16,20},{20,24},... | collective-permute-start | bytes 3145736 | tf_op jit(solution)/shard_map/forward/ppermute | solution.py:158
  179.1 29.2 %collective-permute-start.11 = (bf16[256,2048]{1,0:T(8,128)(2,1)S(1)}, bf16[256,2048]{1,0:T(8,128)(2,1)S(1)}, u32[]{:S(2)}, u32[]{:S(2)}) collective-permute-start(bf16[256,2048]{1,0:T(8,128)(2,1)S(1)} %get-tuple-element.41), channel_id=1, source_target_pairs={{8,4},{12,8},{9,5},{13,9},{10,6},{14,10},{11,7},{15,11},{24,20},{2... | collective-permute-start | bytes 3145736 | tf_op jit(solution)/shard_map/forward/ppermute | solution.py:159
  180.6 13.3 %collective-permute-start.24 = (bf16[2,64,2048]{2,1,0:T(8,128)(2,1)S(1)}, bf16[2,64,2048]{2,1,0:T(8,128)(2,1)S(1)}, u32[]{:S(2)}, u32[]{:S(2)}) collective-permute-start(bf16[2,64,2048]{2,1,0:T(8,128)(2,1)S(1)} %dynamic-slice_bitcast_fusion.6), channel_id=1, source_target_pairs={{0,2},{1,3},{2,0},{3,1},{4,6},{5,7},{6,4},{7,5},{8,10},{9,11},{10,... | collective-permute-start | bytes 1572872 | tf_op jit(solution)/shard_map/backward/ppermute | solution.py:31
  194.3 26.4 %collective-permute-start.25 = (bf16[64,2048]{1,0:T(8,128)(2,1)S(1)}, bf16[64,2048]{1,0:T(8,128)(2,1)S(1)}, u32[]{:S(2)}, u32[]{:S(2)}) collective-permute-start(bf16[64,2048]{1,0:T(8,128)(2,1)S(1)} %get-tuple-element.36), channel_id=1, source_target_pairs={{0,0},{1,4},{2,8},{3,12},{4,5},{5,9},{6,13},{7,1},{8,10},{9,14},{1... | collective-permute-start | bytes 786440 | tf_op jit(solution)/shard_map/backward/ppermute | solution.py:202
  205.1 47.6 %collective-permute-start.9 = (bf16[256,2048]{1,0:T(8,128)(2,1)S(1)}, bf16[256,2048]{1,0:T(8,128)(2,1)S(1)}, u32[]{:S(2)}, u32[]{:S(2)}) collective-permute-start(bf16[256,2048]{1,0:T(8,128)(2,1)S(1)} %add.207), channel_id=1, source_target_pairs={{0,4},{4,8},{8,12},{1,5},{5,9},{9,13},{2,6},{6,10},{10,14},{3,7},{... | collective-permute-start | bytes 3145736 | tf_op jit(solution)/shard_map/forward/ppermute | solution.py:158
  208.7 44.0 %collective-permute-start.12 = (bf16[256,2048]{1,0:T(8,128)(2,1)S(1)}, bf16[256,2048]{1,0:T(8,128)(2,1)S(1)}, u32[]{:S(2)}, u32[]{:S(2)}) collective-permute-start(bf16[256,2048]{1,0:T(8,128)(2,1)S(1)} %add.210), channel_id=1, source_target_pairs={{4,0},{8,4},{12,8},{5,1},{9,5},{13,9},{6,2},{10,6},{14,10},{7,3},{... | collective-permute-start | bytes 3145736 | tf_op jit(solution)/shard_map/forward/ppermute | solution.py:159
  216.9 33.6 %collective-permute-start.26 = (bf16[64,2048]{1,0:T(8,128)(2,1)S(1)}, bf16[64,2048]{1,0:T(8,128)(2,1)S(1)}, u32[]{:S(2)}, u32[]{:S(2)}) collective-permute-start(bf16[64,2048]{1,0:T(8,128)(2,1)S(1)} %get-tuple-element.39), channel_id=1, source_target_pairs={{0,4},{1,8},{2,12},{3,0},{4,9},{5,13},{6,1},{7,5},{8,14},{9,2},{10... | collective-permute-start | bytes 786440 | tf_op jit(solution)/shard_map/backward/ppermute | solution.py:202
  218.8 31.7 %collective-permute-start.27 = (bf16[64,2048]{1,0:T(8,128)(2,1)S(1)}, bf16[64,2048]{1,0:T(8,128)(2,1)S(1)}, u32[]{:S(2)}, u32[]{:S(2)}) collective-permute-start(bf16[64,2048]{1,0:T(8,128)(2,1)S(1)} %get-tuple-element.38), channel_id=1, source_target_pairs={{0,8},{1,12},{2,0},{3,4},{4,13},{5,1},{6,5},{7,9},{8,2},{9,6},{10,... | collective-permute-start | bytes 786440 | tf_op jit(solution)/shard_map/backward/ppermute | solution.py:202
  220.8 31.6 %collective-permute-start.28 = (bf16[64,2048]{1,0:T(8,128)(2,1)S(1)}, bf16[64,2048]{1,0:T(8,128)(2,1)S(1)}, u32[]{:S(2)}, u32[]{:S(2)}) collective-permute-start(bf16[64,2048]{1,0:T(8,128)(2,1)S(1)} %get-tuple-element.37), channel_id=1, source_target_pairs={{0,12},{1,0},{2,4},{3,8},{4,1},{5,5},{6,9},{7,13},{8,6},{9,10},{10... | collective-permute-start | bytes 786440 | tf_op jit(solution)/shard_map/backward/ppermute | solution.py:202
  225.3 27.4 %slice-start.2 = ((s8[8388608]{0:T(1024)(128)(4,1)}), s8[4194304]{0:T(1024)(128)(4,1)S(1)}, s32[]{:S(2)}) async-start(s8[8388608]{0:T(1024)(128)(4,1)} %bitcast.157), calls=%async_computation.4 | async-start | bytes 8388608
  226.1 26.6 %slice-start.3 = ((s8[8388608]{0:T(1024)(128)(4,1)}), s8[4194304]{0:T(1024)(128)(4,1)S(1)}, s32[]{:S(2)}) async-start(s8[8388608]{0:T(1024)(128)(4,1)} %bitcast.157), calls=%async_computation.5 | async-start | bytes 8388608
  255.3 1.6 copy-start.3
  255.3 2.2 copy-start.4
  257.5 2.2 copy-start.1
Sparse Core Ops, SparseCore 0:
  33.7 51.1 all-gather.1

commit v3 on v2

v3 whole, which is shorter than its diff:
```python
import jax
import jax.numpy as jnp
from jax import lax
from jax.sharding import PartitionSpec as P

ADAPTER_COUNT = 32
BLOCK = 128
F32 = jnp.float32
BF16 = jnp.bfloat16


def pick(stacked, index):
    return lax.dynamic_index_in_dim(stacked, index, 0, keepdims=False)


def after(values, *earlier):
    return lax.optimization_barrier((tuple(values), earlier))[0]


def make_local(n):
    masks = []
    while 2 ** len(masks) < n:
        masks.append(2 ** len(masks))

    def swap(x, mask):
        return lax.ppermute(x, "tensor", [(t, t ^ mask) for t in range(n)])

    def rotate(x, k):
        return lax.ppermute(x, "dp", [(i, (i + k) % n) for i in range(n)])

    def local(
        tokens,
        query_weight,
        down_weights,
        up_weights,
        cotangent,
        adapter_of_block,
        block_live_count,
    ):
        blocks_here = adapter_of_block.shape[0]
        rows, width = tokens.shape
        columns = query_weight.shape[1]
        rank = down_weights.shape[1]
        group = rows // n
        t = lax.axis_index("tensor")
        i = lax.axis_index("dp")

        positions = lax.broadcasted_iota(jnp.int32, (blocks_here, BLOCK), 1)
        live_mask = positions < block_live_count[:, None]
        grad_blocks = jnp.where(
            live_mask[:, :, None],
            cotangent.reshape(blocks_here, BLOCK, columns),
            jnp.zeros((), cotangent.dtype),
        )
        grad_flat = grad_blocks.reshape(rows, columns)

        def hop(s, rising, falling):
            with jax.named_scope("spread_cotangent"):
                return (
                    lax.ppermute(rising, "dp", [(a, a + 1) for a in range(s - 1, n - 1)]),
                    lax.ppermute(falling, "dp", [(a + 1, a) for a in range(n - s)]),
                )

        up, down = {}, {}
        up[1], down[1] = hop(1, grad_flat, grad_flat)

        with jax.named_scope("spread_tokens"):
            pieces = lax.all_to_all(
                tokens.reshape(n, group, width), "tensor", 0, 0
            )
            distances = sorted(range(1, n), key=lambda k: -abs(2 * k - n))
            by_source = {0: pick(pieces, i)}
            for k in distances:
                by_source[n - k] = rotate(pick(pieces, (i + k) % n), k)
            near = [n - k for k in distances if k in (1, n - 1)]
            rest = [r for r in range(n) if r not in near]
            full = {}
            for batch in (near, rest):
                held = jnp.stack([by_source[r] for r in batch])
                if batch is near:
                    held, up[1], down[1] = after((held, up[1], down[1]))
                for at, mask in enumerate(reversed(masks)):
                    other = swap(held, mask)
                    odd = (t // mask) % 2 == 1
                    held = jnp.stack(
                        [jnp.where(odd, other, held), jnp.where(odd, held, other)], axis=1 + at
                    )
                for at, r in enumerate(batch):
                    full[r] = held[at].reshape(rows, width)

        with jax.named_scope("ranks"):
            token_blocks = tokens.reshape(blocks_here, BLOCK, width)
            chosen_down = down_weights[adapter_of_block]
            chosen_up = up_weights[adapter_of_block]
            ranks = jnp.stack(
                [
                    jnp.einsum(
                        "uqv,upv->upq", token_blocks, chosen_down, preferred_element_type=F32
                    ),
                    2.0
                    * jnp.einsum("bkq,brq->brk", grad_blocks, chosen_up, preferred_element_type=F32),
                ]
            )
            for mask in masks:
                ranks = ranks + swap(ranks, mask)
            ranks = ranks.astype(BF16)
            shrunk, grad_rank = ranks[0], ranks[1]
            adapter_output = 2.0 * jnp.einsum(
                "psw,psd->pwd", shrunk, chosen_up, preferred_element_type=F32
            ).reshape(rows, columns)
            adapter_backward = jnp.einsum(
                "jxq,jxo->jqo", grad_rank, chosen_down, preferred_element_type=F32
            ).reshape(rows, width)
            (adapter_backward,) = after((adapter_backward,))

        with jax.named_scope("tables"):
            down_products = jnp.einsum(
                "pgz,pzq->pgq", grad_rank, token_blocks, preferred_element_type=F32
            ).astype(BF16)
            ids = jnp.broadcast_to(
                adapter_of_block[:, None, None].astype(BF16), (blocks_here, 1, width)
            )
            parcel = jnp.concatenate(
                [down_products, ids, shrunk.reshape(blocks_here, -1, width)], axis=1
            )
            (parcel,) = after((parcel,), *[by_source[r] for r in range(n)])
            parcel = lax.all_gather(parcel, "dp", axis=0, tiled=True)
            blocks = parcel.shape[0]
            ids = parcel[:, rank, 0].astype(jnp.int32)
            all_shrunk = parcel[:, rank + 1 :].reshape(n, blocks_here, rank, BLOCK)
            shape = (ADAPTER_COUNT, rank, blocks, rank)
            hits = (
                (lax.broadcasted_iota(jnp.int32, shape, 0) == ids[None, None, :, None])
                & (
                    lax.broadcasted_iota(jnp.int32, shape, 1)
                    == lax.broadcasted_iota(jnp.int32, shape, 3)
                )
            ).astype(BF16)
            hits = hits.reshape(ADAPTER_COUNT * rank, blocks * rank)

            def table(products):
                return jnp.dot(
                    hits,
                    products.reshape(blocks * rank, products.shape[-1]),
                    preferred_element_type=F32,
                ).reshape(ADAPTER_COUNT, rank, products.shape[-1])

            grad_down = table(parcel[:, :rank])

        with jax.named_scope("forward"):

            def project(r):
                return jnp.dot(full[r], query_weight, preferred_element_type=F32)

            parts = dict(zip(near, after([project(r).astype(BF16) for r in near])))
            near_parts = tuple(parts.values())
            for r in rest:
                if r != 0:
                    (parts[r],) = after((project(r).astype(BF16),), *near_parts)
            (own,) = after((project(0) + adapter_output,), *near_parts)
            up_sum = down_sum = None
            sends = {}
            for s in range(1, n):
                d = n - s
                sends[s] = (
                    (parts[d], parts[n - d])
                    if s == 1
                    else (parts[d] + up_sum, parts[n - d] + down_sum)
                )
                up_sum = lax.ppermute(sends[s][0], "dp", [(a, a + 1) for a in range(s)])
                down_sum = lax.ppermute(sends[s][1], "dp", [(a, a - 1) for a in range(d, n)])
            query = (own + up_sum.astype(F32) + down_sum.astype(F32)).astype(BF16)

        for s in range(2, n):
            up[s - 1], down[s - 1] = after((up[s - 1], down[s - 1]), *sends[s - 1])
            up[s], down[s] = hop(s, up[s - 1], down[s - 1])
        up[n - 1], down[n - 1] = after((up[n - 1], down[n - 1]), *sends[n - 1])
        grads = [grad_flat] + [jnp.where(i + r <= n - 1, down[r], up[n - r]) for r in range(1, n)]

        with jax.named_scope("backward"):
            early = [r for r in range(n) if r in (0, n // 2)]
            late = [r for r in range(n) if r not in early]
            sums = {}
            up_products = {}
            for batch in (early, late):
                held = [grads[r] for r in batch]
                if batch is early:
                    held = after(held, own, *parts.values())
                held = jnp.stack(held)
                value = (
                    lax.dot_general(
                        held.reshape(-1, columns),
                        query_weight,
                        (((1,), (1,)), ((), ())),
                        preferred_element_type=F32,
                    )
                    .astype(BF16)
                    .reshape(len(batch), n, group, width)
                )
                for mask in masks:
                    halves = value.reshape(len(batch), value.shape[1] // 2, 2, group, width)
                    bit = (t // mask) % 2
                    value = lax.dynamic_index_in_dim(halves, bit, 2, keepdims=False) + swap(
                        lax.dynamic_index_in_dim(halves, 1 - bit, 2, keepdims=False), mask
                    )
                for at, r in enumerate(batch):
                    sums[r] = value[at, 0]
                with jax.named_scope("tables"):
                    for at, r in enumerate(batch):
                        up_products[r] = (
                            2.0
                            * jnp.einsum(
                                "brk,bkq->brq",
                                pick(all_shrunk, (i + r) % n),
                                held[at].reshape(blocks_here, BLOCK, columns),
                                preferred_element_type=F32,
                            )
                        ).astype(BF16)
            sums = jnp.stack([sums[r] for r in range(n)])
            back = [
                lax.ppermute(
                    pick(sums, (t + m) % n),
                    ("dp", "tensor"),
                    [(a * n + b, ((a + b + m) % n) * n + a) for a in range(n) for b in range(n)],
                )
                for m in range(n)
            ]
            returned = jnp.concatenate(
                [lax.select_n((i - t - q) % n, *back) for q in range(n)], axis=0
            )
            token_gradient = (returned.astype(F32) + adapter_backward).astype(BF16)

        with jax.named_scope("tables"):
            up_products = jnp.stack([up_products[r] for r in range(n)])
            grad_up = table(
                jnp.concatenate([pick(up_products, (g - i) % n) for g in range(n)], axis=0)
            )
        return (query, token_gradient, grad_down, grad_up)

    return local


def solution(mesh):
    assert mesh.shape["dp"] == mesh.shape["tensor"]
    return jax.shard_map(
        make_local(mesh.shape["tensor"]),
        mesh=mesh,
        in_specs=(
            P(("parts", "dp"), "tensor"),
            P("dp", "tensor"),
            P("parts", None, "tensor"),
            P("parts", None, "tensor"),
            P(("parts", "dp"), "tensor"),
            P(("parts", "dp")),
            P(("parts", "dp")),
        ),
        out_specs=(
            P(("parts", "dp"), "tensor"),
            P(("parts", "dp"), "tensor"),
            P("parts", None, "tensor"),
            P("parts", None, "tensor"),
        ),
        check_vma=False,
    )
```

time: 268 us -> 221 us (0.82)
  waiting for transfers between devices: 109 us -> 76.3 us
  between operations: 22.6 us -> 1.33 us
  blocking collectives: 0 us -> 18.3 us
  local copies, waits for them, and re-layouts: 17.8 us -> 6.5 us
  other arithmetic: 20.9 us -> 13.3 us
  starting transfers between devices: 54.7 us -> 61.5 us
    all_gather x0 -> x1, blocking collectives: none -> 18.3 us  [local(): parcel = lax.all_gather(parcel, 'dp', axis=0, tiled=True)]
    ppermute x12, waiting for transfers between devices: 34.9 us -> 23.3 us  [the longest x3 20.7 us: local(): up_sum = lax.ppermute(sends[s][0], 'dp', [(a, a + 1) for a in range(s)])]
    ppermute x4, waiting for transfers between devices: 21.8 us -> 12.3 us  [local(): lax.ppermute(pick(sums, (t + m) % n), ('dp', 'tensor'), [(a * n + b, (a +...]
    ppermute x3, waiting for transfers between devices: 27.3 us -> 18.2 us  [rotate(): return lax.ppermute(x, 'dp', [(i, (i + k) % n) for i in range(n)])]
    unnamed x32 -> x23, local copies, waits for them, and re-layouts: 11 us -> 1.95 us
    ppermute x4, starting transfers between devices: 10.5 us -> 16.3 us  [local(): lax.ppermute(pick(sums, (t + m) % n), ('dp', 'tensor'), [(a * n + b, (a +...]
    concatenate x5 -> x2, other arithmetic: 5.74 us -> 0.11 us  [the longest x1 0.07 us: local(): jnp.concatenate([pick(up_products, (g - i) % n) for g in range(n)], axis=0)]
    dot_general x9 -> x12, matrix products: 35.4 us -> 32.6 us  [the longest x2 16.3 us: local(): lax.dot_general(held.reshape(-1, columns), query_weight, (((1,), (1,)), (...]
  transfers between devices with their start and end apart: 31 -> 30, of which waited for: 12 -> 12; matrix products, arithmetic and copies ran while one was open for 26% -> 23% of each run, Pallas kernels for 0% -> 0%
where the time goes in v3:
time: 221 us; the launch traced here: 218 us
  waiting for transfers between devices  76.3 us (35%)
  starting transfers between devices  61.5 us (28%)
  matrix products  40.9 us (19%)
  blocking collectives  18.3 us (8%)
  other arithmetic  13.3 us (6%)
  local copies, waits for them, and re-layouts  6.5 us (3%)
    ppermute x3, waiting for transfers between devices, local(): up_sum = lax.ppermute(sends[s][0], 'dp', [(a, a + 1) for a in range(s)])  20.7 us
    all_gather x1, blocking collectives, local(): parcel = lax.all_gather(parcel, 'dp', axis=0, tiled=True)  18.3 us
    ppermute x3, waiting for transfers between devices, rotate(): return lax.ppermute(x, 'dp', [(i, (i + k) % n) for i in range(n)])  18.2 us
    dot_general x2, matrix products, local(): lax.dot_general(held.reshape(-1, columns), query_weight, (((1,), (1,)), (...  16.3 us
    ppermute x4, starting transfers between devices, local(): lax.ppermute(pick(sums, (t + m) % n), ('dp', 'tensor'), [(a * n + b, (a +...  16.3 us
    ppermute x10, waiting for transfers between devices, swap(): return lax.ppermute(x, 'tensor', [(t, t ^ mask) for t in range(n)])  13.9 us
    ppermute x4, waiting for transfers between devices, local(): lax.ppermute(pick(sums, (t + m) % n), ('dp', 'tensor'), [(a * n + b, (a +...  12.3 us
    ppermute x3, starting transfers between devices, local(): up_sum = lax.ppermute(sends[s][0], 'dp', [(a, a + 1) for a in range(s)])  9.94 us
  transfers between devices with their start and end apart: 30, of which 12 were waited for; matrix products, arithmetic and copies ran while one was open for 23% of the time, Pallas kernels for 0%

profile of v3, /device:TPU:10, one launch (start us, length us, event | category | flops | bytes accessed | tf_op | source)
XLA Modules:
  0.0 218.2 jit_solution(16441317711847006414)
XLA Ops:
  0.7 1.3 fusion.44
  3.3 2.1 gather_fusion
  5.5 1.6 convolution_bitcast_fusion
  7.0 1.7 fusion.8
  10.7 1.9 collective-permute-start.8
  12.6 3.9 %collective-permute-start.7 = (bf16[256,2048]{1,0:T(8,128)(2,1)S(1)}, bf16[256,2048]{1,0:T(8,128)(2,1)}, u32[]{:S(2)}, u32[]{:S(2)}) collective-permute-start(bf16[256,2048]{1,0:T(8,128)(2,1)S(1)} %broadcast_select_fusion), channel_id=1, source_target_pairs={{0,4},{4,8},{8,12},{1,5},{5,9},{9,13},{2,6},{6,10},{10,14},{3,7},{... | collective-permute-start | bytes 3145736 | tf_op jit(solution)/shard_map/spread_cotangent/ppermute | solution.py:60
  16.5 5.0 %all-to-all-start = ((bf16[4,64,2048]{2,1,0:T(8,128)(2,1)}), bf16[4,64,2048]{2,1,0:T(8,128)(2,1)S(1)}, u32[]{:S(2)}, u32[]{:S(2)}) async-start(bf16[4,64,2048]{2,1,0:T(8,128)(2,1)} %bitcast), calls=%async_computation | async-start | bytes 2097152 | tf_op jit(solution)/shard_map/spread_tokens/all_to_all | solution.py:68
  22.1 1.8 convolution_multiply_fusion
  23.9 1.8 fusion.33
  25.7 8.6 %all-to-all-done = bf16[4,64,2048]{2,1,0:T(8,128)(2,1)S(1)} async-done(((bf16[4,64,2048]{2,1,0:T(8,128)(2,1)}), bf16[4,64,2048]{2,1,0:T(8,128)(2,1)S(1)}, u32[]{:S(2)}, u32[]{:S(2)}) %all-to-all-start) | async-done | bytes 1048608 | tf_op jit(solution)/shard_map/spread_tokens/all_to_all | solution.py:68
  34.4 1.5 collective-permute-start.6
  37.1 1.5 convolution_convert_fusion.5
  38.5 2.6 %collective-permute-start = (bf16[64,2048]{1,0:T(8,128)(2,1)S(1)}, bf16[64,2048]{1,0:T(8,128)(2,1)S(1)}, u32[]{:S(2)}, u32[]{:S(2)}) collective-permute-start(bf16[64,2048]{1,0:T(8,128)(2,1)S(1)} %get-tuple-element.59), channel_id=1, source_target_pairs={{0,8},{4,12},{8,0},{12,4},{1,9},{5,13},{9,1},{13,5},{2,10},{6,14},... | collective-permute-start | bytes 786440 | tf_op jit(solution)/shard_map/spread_tokens/ppermute | solution.py:29
  41.3 3.2 %collective-permute-done.6 = bf16[64,2048]{1,0:T(8,128)(2,1)S(1)} collective-permute-done((bf16[64,2048]{1,0:T(8,128)(2,1)S(1)}, bf16[64,2048]{1,0:T(8,128)(2,1)S(1)}, u32[]{:S(2)}, u32[]{:S(2)}) %collective-permute-start.6) | collective-permute-done | bytes 262176 | tf_op jit(solution)/shard_map/spread_tokens/ppermute | solution.py:29
  44.5 12.5 %collective-permute-done.5 = bf16[64,2048]{1,0:T(8,128)(2,1)S(1)} collective-permute-done((bf16[64,2048]{1,0:T(8,128)(2,1)S(1)}, bf16[64,2048]{1,0:T(8,128)(2,1)S(1)}, u32[]{:S(2)}, u32[]{:S(2)}) %collective-permute-start.5) | collective-permute-done | bytes 262176 | tf_op jit(solution)/shard_map/spread_tokens/ppermute | solution.py:29
  57.0 1.6 collective-permute-start.9
  58.6 2.6 %collective-permute-done = bf16[64,2048]{1,0:T(8,128)(2,1)S(1)} collective-permute-done((bf16[64,2048]{1,0:T(8,128)(2,1)S(1)}, bf16[64,2048]{1,0:T(8,128)(2,1)S(1)}, u32[]{:S(2)}, u32[]{:S(2)}) %collective-permute-start) | collective-permute-done | bytes 262176 | tf_op jit(solution)/shard_map/spread_tokens/ppermute | solution.py:29
  62.0 1.5 collective-permute-start.1
  63.5 18.3 %all_gather.3 = bf16[8,18,2048]{2,1,0:T(8,128)(2,1)S(1)} all-gather(bf16[2,18,2048]{2,1,0:T(8,128)(2,1)S(1)} %pad_maximum_fusion.11), channel_id=1, replica_groups=mesh['parts'=2,'dp'=4,'tensor'=4] {'dp'}, dimensions={0}, use_global_device_ids=true | all-gather | bytes 737280 | tf_op jit(solution)/shard_map/tables/all_gather | solution.py:127
  83.9 2.8 %fusion.18 = f32[32,16,2048]{2,1,0:T(8,128)} fusion(bf16[128,2048,1]{1,0,2:T(8,128)(2,1)S(1)} %bitcast.163, s32[128]{0:T(128)S(1)} %copy-done.7, s32[128]{0:T(128)S(1)} %eq.94), kind=kOutput, calls=%fused_computation.85 | convolution fusion | flops 268632064 | bytes 4719616 | tf_op jit(solution)/shard_map/tables/dot_general | solution.py:142
  90.2 2.4 %convolution_convert_fusion.3 = bf16[256,2048]{1,0:T(8,128)(2,1)S(1)} fusion(bf16[256,2048]{1,0:T(8,128)(2,1)S(1)} %bitcast.173, bf16[2048,2048]{1,0:T(8,128)(2,1)S(1)} %bitcast.187), kind=kOutput, calls=%fused_computation.7 | convolution fusion | flops 2148007936 | bytes 10485760 | tf_op jit(solution)/shard_map/forward/dot_general | solution.py:153
  92.6 2.4 %convolution_convert_fusion.4 = bf16[256,2048]{1,0:T(8,128)(2,1)S(1)} fusion(bf16[256,2048]{1,0:T(8,128)(2,1)S(1)} %bitcast.174, bf16[2048,2048]{1,0:T(8,128)(2,1)S(1)} %bitcast.187), kind=kOutput, calls=%fused_computation.8 | convolution fusion | flops 2148007936 | bytes 10485760 | tf_op jit(solution)/shard_map/forward/dot_general | solution.py:153
  95.1 1.3 collective-permute-start.11
  97.5 2.4 %convolution_convert_fusion.2 = bf16[256,2048]{1,0:T(8,128)(2,1)S(1)} fusion(bf16[256,2048]{1,0:T(8,128)(2,1)S(1)} %bitcast.178, bf16[2048,2048]{1,0:T(8,128)(2,1)S(1)} %bitcast.187), kind=kOutput, calls=%fused_computation.6 | convolution fusion | flops 2148007936 | bytes 10485760 | tf_op jit(solution)/shard_map/forward/dot_general | solution.py:153
  99.9 3.6 %collective-permute-start.17 = (bf16[256,2048]{1,0:T(8,128)(2,1)}, bf16[256,2048]{1,0:T(8,128)(2,1)S(1)}, u32[]{:S(2)}, u32[]{:S(2)}) collective-permute-start(bf16[256,2048]{1,0:T(8,128)(2,1)} %collective-permute-done.7), channel_id=1, source_target_pairs={{4,8},{8,12},{5,9},{9,13},{6,10},{10,14},{7,11},{11,15},{20,24},{2... | collective-permute-start | bytes 3145736 | tf_op jit(solution)/shard_map/spread_cotangent/ppermute | solution.py:60
  103.5 2.1 collective-permute-start.18
  105.6 2.5 %convolution_add_fusion = f32[256,2048]{1,0:T(8,128)S(1)} fusion(f32[256,2048]{1,0:T(8,128)S(1)} %bitcast.169, bf16[256,2048]{1,0:T(8,128)(2,1)S(1)} %bitcast.177, bf16[2048,2048]{1,0:T(8,128)(2,1)S(1)} %bitcast.187), kind=kOutput, calls=%fused_computation.5 | convolution fusion | flops 2148007936 | bytes 13631488 | tf_op jit(solution)/shard_map/forward/dot_general | solution.py:153
  108.1 14.4 %collective-permute-done.11 = bf16[256,2048]{1,0:T(8,128)(2,1)S(1)} collective-permute-done((bf16[256,2048]{1,0:T(8,128)(2,1)S(1)}, bf16[256,2048]{1,0:T(8,128)(2,1)S(1)}, u32[]{:S(2)}, u32[]{:S(2)}) %collective-permute-start.11) | collective-permute-done | bytes 1048608 | tf_op jit(solution)/shard_map/forward/ppermute | solution.py:170
  122.7 4.3 %collective-permute-start.12 = (bf16[256,2048]{1,0:T(8,128)(2,1)S(1)}, bf16[256,2048]{1,0:T(8,128)(2,1)S(1)}, u32[]{:S(2)}, u32[]{:S(2)}) collective-permute-start(bf16[256,2048]{1,0:T(8,128)(2,1)S(1)} %get-tuple-element.52), channel_id=1, source_target_pairs={{0,4},{4,8},{1,5},{5,9},{2,6},{6,10},{3,7},{7,11},{16,20},{20,24},... | collective-permute-start | bytes 3145736 | tf_op jit(solution)/shard_map/forward/ppermute | solution.py:170
  128.3 2.6 %collective-permute-done.18 = bf16[256,2048]{1,0:T(8,128)(2,1)S(1)} collective-permute-done((bf16[256,2048]{1,0:T(8,128)(2,1)}, bf16[256,2048]{1,0:T(8,128)(2,1)S(1)}, u32[]{:S(2)}, u32[]{:S(2)}) %collective-permute-start.18) | collective-permute-done | bytes 1048608 | tf_op jit(solution)/shard_map/spread_cotangent/ppermute | solution.py:61
  130.9 2.2 %collective-permute-start.22 = (bf16[256,2048]{1,0:T(8,128)(2,1)S(1)}, bf16[256,2048]{1,0:T(8,128)(2,1)S(1)}, u32[]{:S(2)}, u32[]{:S(2)}) collective-permute-start(bf16[256,2048]{1,0:T(8,128)(2,1)S(1)} %collective-permute-done.18), channel_id=1, source_target_pairs={{4,0},{5,1},{6,2},{7,3},{20,16},{21,17},{22,18},{23,19}} | collective-permute-start | bytes 3145736 | tf_op jit(solution)/shard_map/spread_cotangent/ppermute | solution.py:61
  134.2 8.2 %convolution_convert_fusion.1 = bf16[512,2048]{1,0:T(8,128)(2,1)S(1)} fusion(bf16[512,2048]{1,0:T(8,128)(2,1)S(1)} %bitcast.171, bf16[2048,2048]{1,0:T(8,128)(2,1)} %param.8), kind=kOutput, calls=%fused_computation.3 | convolution fusion | flops 4296015872 | bytes 12582912 | tf_op jit(solution)/shard_map/backward/dot_general | solution.py:191
  143.1 6.3 %collective-permute-done.12 = bf16[256,2048]{1,0:T(8,128)(2,1)S(1)} collective-permute-done((bf16[256,2048]{1,0:T(8,128)(2,1)S(1)}, bf16[256,2048]{1,0:T(8,128)(2,1)S(1)}, u32[]{:S(2)}, u32[]{:S(2)}) %collective-permute-start.12) | collective-permute-done | bytes 1048608 | tf_op jit(solution)/shard_map/forward/ppermute | solution.py:170
  149.8 4.3 %collective-permute-start.13 = (bf16[256,2048]{1,0:T(8,128)(2,1)S(1)}, bf16[256,2048]{1,0:T(8,128)(2,1)S(1)}, u32[]{:S(2)}, u32[]{:S(2)}) collective-permute-start(bf16[256,2048]{1,0:T(8,128)(2,1)S(1)} %add.221), channel_id=1, source_target_pairs={{0,4},{4,8},{8,12},{1,5},{5,9},{9,13},{2,6},{6,10},{10,14},{3,7},{... | collective-permute-start | bytes 3145736 | tf_op jit(solution)/shard_map/forward/ppermute | solution.py:170
  154.5 1.9 collective-permute-start.16
  156.5 1.9 broadcast_select_fusion.1
  159.8 8.1 %convolution_convert_fusion = bf16[512,2048]{1,0:T(8,128)(2,1)S(1)} fusion(bf16[512,2048]{1,0:T(8,128)(2,1)S(1)} %bitcast.170, bf16[2048,2048]{1,0:T(8,128)(2,1)} %param.8), kind=kOutput, calls=%fused_computation.2 | convolution fusion | flops 4296015872 | bytes 12582912 | tf_op jit(solution)/shard_map/backward/dot_general | solution.py:191
  168.4 2.7 %fusion.16 = f32[32,16,2048]{2,1,0:T(8,128)} fusion(bf16[128,2048,1]{1,0,2:T(8,128)(2,1)S(1)} %bitcast.164, s32[128]{0:T(128)S(1)} %copy-done.7, s32[128]{0:T(128)S(1)} %eq.94), kind=kOutput, calls=%fused_computation.84 | convolution fusion | flops 268632064 | bytes 4719616 | tf_op jit(solution)/shard_map/tables/dot_general | solution.py:142
  171.3 1.6 collective-permute-start.24
  173.0 12.7 %collective-permute-done.24 = bf16[2,1,64,2048]{3,2,1,0:T(8,128)(2,1)S(1)} collective-permute-done((bf16[2,1,64,2048]{3,2,1,0:T(8,128)(2,1)S(1)}, bf16[2,1,64,2048]{3,2,1,0:T(8,128)(2,1)S(1)}, u32[]{:S(2)}, u32[]{:S(2)}) %collective-permute-start.24) | collective-permute-done | bytes 524320 | tf_op jit(solution)/shard_map/backward/ppermute | solution.py:26
  186.0 3.2 %collective-permute-start.26 = (bf16[64,2048]{1,0:T(8,128)(2,1)S(1)}, bf16[64,2048]{1,0:T(8,128)(2,1)S(1)}, u32[]{:S(2)}, u32[]{:S(2)}) collective-permute-start(bf16[64,2048]{1,0:T(8,128)(2,1)S(1)} %get-tuple-element.48), channel_id=1, source_target_pairs={{0,4},{1,8},{2,12},{3,0},{4,9},{5,13},{6,1},{7,5},{8,14},{9,2},{10... | collective-permute-start | bytes 786440 | tf_op jit(solution)/shard_map/backward/ppermute | solution.py:221
  189.2 3.8 %collective-permute-start.28 = (bf16[64,2048]{1,0:T(8,128)(2,1)S(1)}, bf16[64,2048]{1,0:T(8,128)(2,1)S(1)}, u32[]{:S(2)}, u32[]{:S(2)}) collective-permute-start(bf16[64,2048]{1,0:T(8,128)(2,1)S(1)} %get-tuple-element.49), channel_id=1, source_target_pairs={{0,12},{1,0},{2,4},{3,8},{4,1},{5,5},{6,9},{7,13},{8,6},{9,10},{10... | collective-permute-start | bytes 786440 | tf_op jit(solution)/shard_map/backward/ppermute | solution.py:221
  193.0 1.9 collective-permute-start.27
  194.9 7.4 %collective-permute-start.25 = (bf16[64,2048]{1,0:T(8,128)(2,1)S(1)}, bf16[64,2048]{1,0:T(8,128)(2,1)S(1)}, u32[]{:S(2)}, u32[]{:S(2)}) collective-permute-start(bf16[64,2048]{1,0:T(8,128)(2,1)S(1)} %get-tuple-element.51), channel_id=1, source_target_pairs={{0,0},{1,4},{2,8},{3,12},{4,5},{5,9},{6,13},{7,1},{8,10},{9,14},{1... | collective-permute-start | bytes 786440 | tf_op jit(solution)/shard_map/backward/ppermute | solution.py:221
  202.4 1.4 add_convert_fusion.1
  203.8 2.8 %collective-permute-done.28 = bf16[64,2048]{1,0:T(8,128)(2,1)S(1)} collective-permute-done((bf16[64,2048]{1,0:T(8,128)(2,1)S(1)}, bf16[64,2048]{1,0:T(8,128)(2,1)S(1)}, u32[]{:S(2)}, u32[]{:S(2)}) %collective-permute-start.28) | collective-permute-done | bytes 262176 | tf_op jit(solution)/shard_map/backward/ppermute | solution.py:221
  206.6 8.0 %collective-permute-done.27 = bf16[64,2048]{1,0:T(8,128)(2,1)S(1)} collective-permute-done((bf16[64,2048]{1,0:T(8,128)(2,1)S(1)}, bf16[64,2048]{1,0:T(8,128)(2,1)S(1)}, u32[]{:S(2)}, u32[]{:S(2)}) %collective-permute-start.27) | collective-permute-done | bytes 262176 | tf_op jit(solution)/shard_map/backward/ppermute | solution.py:221
  214.6 1.5 collective-permute-done.25
  (112 shorter events, 21.1 us)
Async XLA Ops:
  0.6 2.1 copy-start
  0.6 9.9 %copy-start.4 = (bf16[256,2048]{1,0:T(8,128)(2,1)S(1)}, bf16[256,2048]{1,0:T(8,128)(2,1)}, u32[]{:S(2)}) copy-start(bf16[256,2048]{1,0:T(8,128)(2,1)} %param.11) | copy-start | bytes 3145732
  8.7 1.2 collective-permute-start.3
  10.0 12.1 %collective-permute-start.4 = (f32[2,2,16,128]{3,2,1,0:T(8,128)S(1)}, f32[2,2,16,128]{3,2,1,0:T(8,128)S(1)}, u32[]{:S(2)}, u32[]{:S(2)}) collective-permute-start(f32[2,2,16,128]{3,2,1,0:T(8,128)S(1)} %fusion.42), channel_id=1, source_target_pairs={{0,2},{1,3},{2,0},{3,1},{4,6},{5,7},{6,4},{7,5},{8,10},{9,11},{10,... | collective-permute-start | bytes 98312 | tf_op jit(solution)/shard_map/ranks/ppermute | solution.py:26
  10.7 46.3 %collective-permute-start.8 = (bf16[256,2048]{1,0:T(8,128)(2,1)S(1)}, bf16[256,2048]{1,0:T(8,128)(2,1)}, u32[]{:S(2)}, u32[]{:S(2)}) collective-permute-start(bf16[256,2048]{1,0:T(8,128)(2,1)S(1)} %broadcast_select_fusion), channel_id=1, source_target_pairs={{4,0},{8,4},{12,8},{5,1},{9,5},{13,9},{6,2},{10,6},{14,10},{7,3},{... | collective-permute-start | bytes 3145736 | tf_op jit(solution)/shard_map/spread_cotangent/ppermute | solution.py:61
  12.6 44.4 %collective-permute-start.7 = (bf16[256,2048]{1,0:T(8,128)(2,1)S(1)}, bf16[256,2048]{1,0:T(8,128)(2,1)}, u32[]{:S(2)}, u32[]{:S(2)}) collective-permute-start(bf16[256,2048]{1,0:T(8,128)(2,1)S(1)} %broadcast_select_fusion), channel_id=1, source_target_pairs={{0,4},{4,8},{8,12},{1,5},{5,9},{9,13},{2,6},{6,10},{10,14},{3,7},{... | collective-permute-start | bytes 3145736 | tf_op jit(solution)/shard_map/spread_cotangent/ppermute | solution.py:60
  16.5 17.8 %all-to-all-start = ((bf16[4,64,2048]{2,1,0:T(8,128)(2,1)}), bf16[4,64,2048]{2,1,0:T(8,128)(2,1)S(1)}, u32[]{:S(2)}, u32[]{:S(2)}) async-start(bf16[4,64,2048]{2,1,0:T(8,128)(2,1)} %bitcast), calls=%async_computation | async-start | bytes 2097152 | tf_op jit(solution)/shard_map/spread_tokens/all_to_all | solution.py:68
  25.7 15.5 %copy-start.8 = (bf16[2]{0:T(256)(128)(2,1)S(1)}, bf16[2]{0:T(256)(128)(2,1)}, u32[]{:S(2)}) copy-start(bf16[2]{0:T(256)(128)(2,1)} %get-tuple-element.70) | copy-start | bytes 16
  34.4 10.1 %collective-permute-start.6 = (bf16[64,2048]{1,0:T(8,128)(2,1)S(1)}, bf16[64,2048]{1,0:T(8,128)(2,1)S(1)}, u32[]{:S(2)}, u32[]{:S(2)}) collective-permute-start(bf16[64,2048]{1,0:T(8,128)(2,1)S(1)} %get-tuple-element.57), channel_id=1, source_target_pairs={{0,12},{4,0},{8,4},{12,8},{1,13},{5,1},{9,5},{13,9},{2,14},{6,2},{... | collective-permute-start | bytes 786440 | tf_op jit(solution)/shard_map/spread_tokens/ppermute | solution.py:29
  35.9 21.1 %collective-permute-start.5 = (bf16[64,2048]{1,0:T(8,128)(2,1)S(1)}, bf16[64,2048]{1,0:T(8,128)(2,1)S(1)}, u32[]{:S(2)}, u32[]{:S(2)}) collective-permute-start(bf16[64,2048]{1,0:T(8,128)(2,1)S(1)} %get-tuple-element.58), channel_id=1, source_target_pairs={{0,4},{4,8},{8,12},{12,0},{1,5},{5,9},{9,13},{13,1},{2,6},{6,10},{... | collective-permute-start | bytes 786440 | tf_op jit(solution)/shard_map/spread_tokens/ppermute | solution.py:29
  38.5 22.6 %collective-permute-start = (bf16[64,2048]{1,0:T(8,128)(2,1)S(1)}, bf16[64,2048]{1,0:T(8,128)(2,1)S(1)}, u32[]{:S(2)}, u32[]{:S(2)}) collective-permute-start(bf16[64,2048]{1,0:T(8,128)(2,1)S(1)} %get-tuple-element.59), channel_id=1, source_target_pairs={{0,8},{4,12},{8,0},{12,4},{1,9},{5,13},{9,1},{13,5},{2,10},{6,14},... | collective-permute-start | bytes 786440 | tf_op jit(solution)/shard_map/spread_tokens/ppermute | solution.py:29
  57.0 25.5 %collective-permute-start.9 = (bf16[2,64,2048]{2,1,0:T(8,128)(2,1)S(1)}, bf16[2,64,2048]{2,1,0:T(8,128)(2,1)}, u32[]{:S(2)}, u32[]{:S(2)}) collective-permute-start(bf16[2,64,2048]{2,1,0:T(8,128)(2,1)S(1)} %pad_maximum_fusion.8), channel_id=1, source_target_pairs={{0,2},{1,3},{2,0},{3,1},{4,6},{5,7},{6,4},{7,5},{8,10},{9,11},{10,... | collective-permute-start | bytes 1572872 | tf_op jit(solution)/shard_map/spread_tokens/ppermute | solution.py:26
  61.2 0.9 copy-start.5
  62.0 24.7 %collective-permute-start.1 = (bf16[2,64,2048]{2,1,0:T(8,128)(2,1)}, bf16[2,64,2048]{2,1,0:T(8,128)(2,1)}, u32[]{:S(2)}, u32[]{:S(2)}) collective-permute-start(bf16[2,64,2048]{2,1,0:T(8,128)(2,1)} %pad_maximum_fusion.7), channel_id=1, source_target_pairs={{0,2},{1,3},{2,0},{3,1},{4,6},{5,7},{6,4},{7,5},{8,10},{9,11},{10,... | collective-permute-start | bytes 1572872 | tf_op jit(solution)/shard_map/spread_tokens/ppermute | solution.py:26
  82.5 1.3 copy-start.7
  83.8 4.8 %collective-permute-start.10 = (bf16[2,2,64,2048]{3,2,0,1:T(8,128)(2,1)S(1)}, bf16[2,2,64,2048]{3,2,0,1:T(8,128)(2,1)S(1)}, u32[]{:S(2)}, u32[]{:S(2)}) collective-permute-start(bf16[2,2,64,2048]{3,2,0,1:T(8,128)(2,1)S(1)} %pad_maximum_fusion.5), channel_id=1, source_target_pairs={{0,1},{1,0},{2,3},{3,2},{4,5},{5,4},{6,7},{7,6},{8,9},{9,8},{10,11... | collective-permute-start | bytes 3145736 | tf_op jit(solution)/shard_map/spread_tokens/ppermute | solution.py:26
  83.9 2.9 %copy-start.6 = (bf16[64,2048]{1,0:T(8,128)(2,1)S(1)}, bf16[64,2048]{1,0:T(8,128)(2,1)}, u32[]{:S(2)}) copy-start(bf16[64,2048]{1,0:T(8,128)(2,1)} %copy-done.5) | copy-start | bytes 786436
  83.9 5.1 %slice-start = ((s8[8388608]{0:T(1024)(128)(4,1)}), s8[4194304]{0:T(1024)(128)(4,1)S(1)}, s32[]{:S(2)}) async-start(s8[8388608]{0:T(1024)(128)(4,1)} %bitcast.186), calls=%async_computation.1 | async-start | bytes 8388608
  88.0 2.2 %slice-start.1 = ((s8[8388608]{0:T(1024)(128)(4,1)}), s8[4194304]{0:T(1024)(128)(4,1)S(1)}, s32[]{:S(2)}) async-start(s8[8388608]{0:T(1024)(128)(4,1)} %bitcast.186), calls=%async_computation.2 | async-start | bytes 8388608
  88.0 9.1 %collective-permute-start.2 = (bf16[2,2,64,2048]{3,2,1,0:T(8,128)(2,1)S(1)}, bf16[2,2,64,2048]{3,2,1,0:T(8,128)(2,1)S(1)}, u32[]{:S(2)}, u32[]{:S(2)}) collective-permute-start(bf16[2,2,64,2048]{3,2,1,0:T(8,128)(2,1)S(1)} %pad_maximum_fusion.4), channel_id=1, source_target_pairs={{0,1},{1,0},{2,3},{3,2},{4,5},{5,4},{6,7},{7,6},{8,9},{9,8},{10,11... | collective-permute-start | bytes 3145736 | tf_op jit(solution)/shard_map/spread_tokens/ppermute | solution.py:26
  95.1 27.5 %collective-permute-start.11 = (bf16[256,2048]{1,0:T(8,128)(2,1)S(1)}, bf16[256,2048]{1,0:T(8,128)(2,1)S(1)}, u32[]{:S(2)}, u32[]{:S(2)}) collective-permute-start(bf16[256,2048]{1,0:T(8,128)(2,1)S(1)} %convolution_convert_fusion.4), channel_id=1, source_target_pairs={{0,4},{1,5},{2,6},{3,7},{16,20},{17,21},{18,22},{19,23}} | collective-permute-start | bytes 3145736 | tf_op jit(solution)/shard_map/forward/ppermute | solution.py:170
  96.4 26.2 %collective-permute-start.14 = (bf16[256,2048]{1,0:T(8,128)(2,1)S(1)}, bf16[256,2048]{1,0:T(8,128)(2,1)S(1)}, u32[]{:S(2)}, u32[]{:S(2)}) collective-permute-start(bf16[256,2048]{1,0:T(8,128)(2,1)S(1)} %convolution_convert_fusion.3), channel_id=1, source_target_pairs={{12,8},{13,9},{14,10},{15,11},{28,24},{29,25},{30,26},{31,27}} | collective-permute-start | bytes 3145736 | tf_op jit(solution)/shard_map/forward/ppermute | solution.py:171
  97.4 8.2 %copy-start.3 = (f32[2,128,2048]{2,1,0:T(8,128)S(1)}, f32[2,128,2048]{2,1,0:T(8,128)}, u32[]{:S(2)}) copy-start(f32[2,128,2048]{2,1,0:T(8,128)} %convolution_multiply_fusion) | copy-start | bytes 6291460
  99.9 28.5 %collective-permute-start.17 = (bf16[256,2048]{1,0:T(8,128)(2,1)}, bf16[256,2048]{1,0:T(8,128)(2,1)S(1)}, u32[]{:S(2)}, u32[]{:S(2)}) collective-permute-start(bf16[256,2048]{1,0:T(8,128)(2,1)} %collective-permute-done.7), channel_id=1, source_target_pairs={{4,8},{8,12},{5,9},{9,13},{6,10},{10,14},{7,11},{11,15},{20,24},{2... | collective-permute-start | bytes 3145736 | tf_op jit(solution)/shard_map/spread_cotangent/ppermute | solution.py:60
  103.5 27.4 %collective-permute-start.18 = (bf16[256,2048]{1,0:T(8,128)(2,1)}, bf16[256,2048]{1,0:T(8,128)(2,1)S(1)}, u32[]{:S(2)}, u32[]{:S(2)}) collective-permute-start(bf16[256,2048]{1,0:T(8,128)(2,1)} %collective-permute-done.8), channel_id=1, source_target_pairs={{4,0},{8,4},{5,1},{9,5},{6,2},{10,6},{7,3},{11,7},{20,16},{24,20},... | collective-permute-start | bytes 3145736 | tf_op jit(solution)/shard_map/spread_cotangent/ppermute | solution.py:61
  122.7 26.7 %collective-permute-start.12 = (bf16[256,2048]{1,0:T(8,128)(2,1)S(1)}, bf16[256,2048]{1,0:T(8,128)(2,1)S(1)}, u32[]{:S(2)}, u32[]{:S(2)}) collective-permute-start(bf16[256,2048]{1,0:T(8,128)(2,1)S(1)} %get-tuple-element.52), channel_id=1, source_target_pairs={{0,4},{4,8},{1,5},{5,9},{2,6},{6,10},{3,7},{7,11},{16,20},{20,24},... | collective-permute-start | bytes 3145736 | tf_op jit(solution)/shard_map/forward/ppermute | solution.py:170
  127.0 27.1 %collective-permute-start.15 = (bf16[256,2048]{1,0:T(8,128)(2,1)S(1)}, bf16[256,2048]{1,0:T(8,128)(2,1)S(1)}, u32[]{:S(2)}, u32[]{:S(2)}) collective-permute-start(bf16[256,2048]{1,0:T(8,128)(2,1)S(1)} %get-tuple-element.53), channel_id=1, source_target_pairs={{8,4},{12,8},{9,5},{13,9},{10,6},{14,10},{11,7},{15,11},{24,20},{2... | collective-permute-start | bytes 3145736 | tf_op jit(solution)/shard_map/forward/ppermute | solution.py:171
  130.9 25.5 %collective-permute-start.22 = (bf16[256,2048]{1,0:T(8,128)(2,1)S(1)}, bf16[256,2048]{1,0:T(8,128)(2,1)S(1)}, u32[]{:S(2)}, u32[]{:S(2)}) collective-permute-start(bf16[256,2048]{1,0:T(8,128)(2,1)S(1)} %collective-permute-done.18), channel_id=1, source_target_pairs={{4,0},{5,1},{6,2},{7,3},{20,16},{21,17},{22,18},{23,19}} | collective-permute-start | bytes 3145736 | tf_op jit(solution)/shard_map/spread_cotangent/ppermute | solution.py:61
  133.2 23.3 %collective-permute-start.21 = (bf16[256,2048]{1,0:T(8,128)(2,1)S(1)}, bf16[256,2048]{1,0:T(8,128)(2,1)S(1)}, u32[]{:S(2)}, u32[]{:S(2)}) collective-permute-start(bf16[256,2048]{1,0:T(8,128)(2,1)S(1)} %collective-permute-done.17), channel_id=1, source_target_pairs={{8,12},{9,13},{10,14},{11,15},{24,28},{25,29},{26,30},{27,31}} | collective-permute-start | bytes 3145736 | tf_op jit(solution)/shard_map/spread_cotangent/ppermute | solution.py:60
  142.5 16.4 %collective-permute-start.19 = (bf16[2,2,64,2048]{3,2,1,0:T(8,128)(2,1)S(1)}, bf16[2,2,64,2048]{3,2,1,0:T(8,128)(2,1)S(1)}, u32[]{:S(2)}, u32[]{:S(2)}) collective-permute-start(bf16[2,2,64,2048]{3,2,1,0:T(8,128)(2,1)S(1)} %dynamic-slice_bitcast_fusion.1), channel_id=1, source_target_pairs={{0,1},{1,0},{2,3},{3,2},{4,5},{5,4},{6,7},{7,6},{8,9},{9,8},{10,11... | collective-permute-start | bytes 3145736 | tf_op jit(solution)/shard_map/backward/ppermute | solution.py:26
  149.8 45.2 %collective-permute-start.13 = (bf16[256,2048]{1,0:T(8,128)(2,1)S(1)}, bf16[256,2048]{1,0:T(8,128)(2,1)S(1)}, u32[]{:S(2)}, u32[]{:S(2)}) collective-permute-start(bf16[256,2048]{1,0:T(8,128)(2,1)S(1)} %add.221), channel_id=1, source_target_pairs={{0,4},{4,8},{8,12},{1,5},{5,9},{9,13},{2,6},{6,10},{10,14},{3,7},{... | collective-permute-start | bytes 3145736 | tf_op jit(solution)/shard_map/forward/ppermute | solution.py:170
  154.5 47.8 %collective-permute-start.16 = (bf16[256,2048]{1,0:T(8,128)(2,1)S(1)}, bf16[256,2048]{1,0:T(8,128)(2,1)S(1)}, u32[]{:S(2)}, u32[]{:S(2)}) collective-permute-start(bf16[256,2048]{1,0:T(8,128)(2,1)S(1)} %add.224), channel_id=1, source_target_pairs={{4,0},{8,4},{12,8},{5,1},{9,5},{13,9},{6,2},{10,6},{14,10},{7,3},{... | collective-permute-start | bytes 3145736 | tf_op jit(solution)/shard_map/forward/ppermute | solution.py:171
  159.0 13.8 %collective-permute-start.20 = (bf16[2,1,64,2048]{3,2,1,0:T(8,128)(2,1)S(1)}, bf16[2,1,64,2048]{3,2,1,0:T(8,128)(2,1)S(1)}, u32[]{:S(2)}, u32[]{:S(2)}) collective-permute-start(bf16[2,1,64,2048]{3,2,1,0:T(8,128)(2,1)S(1)} %constant_dynamic-slice_fusion.1), channel_id=1, source_target_pairs={{0,2},{1,3},{2,0},{3,1},{4,6},{5,7},{6,4},{7,5},{8,10},{9,11},{10,... | collective-permute-start | bytes 1572872 | tf_op jit(solution)/shard_map/backward/ppermute | solution.py:26
  168.1 3.0 %collective-permute-start.23 = (bf16[2,2,64,2048]{3,2,1,0:T(8,128)(2,1)S(1)}, bf16[2,2,64,2048]{3,2,1,0:T(8,128)(2,1)S(1)}, u32[]{:S(2)}, u32[]{:S(2)}) collective-permute-start(bf16[2,2,64,2048]{3,2,1,0:T(8,128)(2,1)S(1)} %dynamic-slice_bitcast_fusion), channel_id=1, source_target_pairs={{0,1},{1,0},{2,3},{3,2},{4,5},{5,4},{6,7},{7,6},{8,9},{9,8},{10,11... | collective-permute-start | bytes 3145736 | tf_op jit(solution)/shard_map/backward/ppermute | solution.py:26
  171.3 14.4 %collective-permute-start.24 = (bf16[2,1,64,2048]{3,2,1,0:T(8,128)(2,1)S(1)}, bf16[2,1,64,2048]{3,2,1,0:T(8,128)(2,1)S(1)}, u32[]{:S(2)}, u32[]{:S(2)}) collective-permute-start(bf16[2,1,64,2048]{3,2,1,0:T(8,128)(2,1)S(1)} %constant_dynamic-slice_fusion), channel_id=1, source_target_pairs={{0,2},{1,3},{2,0},{3,1},{4,6},{5,7},{6,4},{7,5},{8,10},{9,11},{10,... | collective-permute-start | bytes 1572872 | tf_op jit(solution)/shard_map/backward/ppermute | solution.py:26
  186.0 17.8 %collective-permute-start.26 = (bf16[64,2048]{1,0:T(8,128)(2,1)S(1)}, bf16[64,2048]{1,0:T(8,128)(2,1)S(1)}, u32[]{:S(2)}, u32[]{:S(2)}) collective-permute-start(bf16[64,2048]{1,0:T(8,128)(2,1)S(1)} %get-tuple-element.48), channel_id=1, source_target_pairs={{0,4},{1,8},{2,12},{3,0},{4,9},{5,13},{6,1},{7,5},{8,14},{9,2},{10... | collective-permute-start | bytes 786440 | tf_op jit(solution)/shard_map/backward/ppermute | solution.py:221
  189.2 17.3 %collective-permute-start.28 = (bf16[64,2048]{1,0:T(8,128)(2,1)S(1)}, bf16[64,2048]{1,0:T(8,128)(2,1)S(1)}, u32[]{:S(2)}, u32[]{:S(2)}) collective-permute-start(bf16[64,2048]{1,0:T(8,128)(2,1)S(1)} %get-tuple-element.49), channel_id=1, source_target_pairs={{0,12},{1,0},{2,4},{3,8},{4,1},{5,5},{6,9},{7,13},{8,6},{9,10},{10... | collective-permute-start | bytes 786440 | tf_op jit(solution)/shard_map/backward/ppermute | solution.py:221
  193.0 21.6 %collective-permute-start.27 = (bf16[64,2048]{1,0:T(8,128)(2,1)S(1)}, bf16[64,2048]{1,0:T(8,128)(2,1)S(1)}, u32[]{:S(2)}, u32[]{:S(2)}) collective-permute-start(bf16[64,2048]{1,0:T(8,128)(2,1)S(1)} %get-tuple-element.50), channel_id=1, source_target_pairs={{0,8},{1,12},{2,0},{3,4},{4,13},{5,1},{6,5},{7,9},{8,2},{9,6},{10,... | collective-permute-start | bytes 786440 | tf_op jit(solution)/shard_map/backward/ppermute | solution.py:221
  194.9 21.2 %collective-permute-start.25 = (bf16[64,2048]{1,0:T(8,128)(2,1)S(1)}, bf16[64,2048]{1,0:T(8,128)(2,1)S(1)}, u32[]{:S(2)}, u32[]{:S(2)}) collective-permute-start(bf16[64,2048]{1,0:T(8,128)(2,1)S(1)} %get-tuple-element.51), channel_id=1, source_target_pairs={{0,0},{1,4},{2,8},{3,12},{4,5},{5,9},{6,13},{7,1},{8,10},{9,14},{1... | collective-permute-start | bytes 786440 | tf_op jit(solution)/shard_map/backward/ppermute | solution.py:221
  203.8 12.4 %copy-start.2 = (f32[2,128,2048]{2,1,0:T(8,128)S(1)}, f32[2,128,2048]{2,1,0:T(8,128)}, u32[]{:S(2)}) copy-start(f32[2,128,2048]{2,1,0:T(8,128)} %fusion.33) | copy-start | bytes 6291460
  216.2 2.0 copy-start.1

commit v4 on v3

v4 whole, which is shorter than its diff:
```python
import jax
import jax.numpy as jnp
from jax import lax
from jax.sharding import PartitionSpec as P

ADAPTER_COUNT = 32
BLOCK = 128
F32 = jnp.float32
BF16 = jnp.bfloat16


def pick(stacked, index):
    return lax.dynamic_index_in_dim(stacked, index, 0, keepdims=False)


def after(values, *earlier):
    return lax.optimization_barrier((tuple(values), earlier))[0]


def make_local(n):
    masks = []
    while 2 ** len(masks) < n:
        masks.append(2 ** len(masks))

    def swap(x, mask):
        return lax.ppermute(x, "tensor", [(t, t ^ mask) for t in range(n)])

    def rotate(x, k):
        return lax.ppermute(x, "dp", [(i, (i + k) % n) for i in range(n)])

    def local(
        tokens,
        query_weight,
        down_weights,
        up_weights,
        cotangent,
        adapter_of_block,
        block_live_count,
    ):
        blocks_here = adapter_of_block.shape[0]
        rows, width = tokens.shape
        columns = query_weight.shape[1]
        rank = down_weights.shape[1]
        group = rows // n
        t = lax.axis_index("tensor")
        i = lax.axis_index("dp")
        half = n // 2
        lower = i < half

        positions = lax.broadcasted_iota(jnp.int32, (blocks_here, BLOCK), 1)
        live_mask = positions < block_live_count[:, None]
        grad_blocks = jnp.where(
            live_mask[:, :, None],
            cotangent.reshape(blocks_here, BLOCK, columns),
            jnp.zeros((), cotangent.dtype),
        )
        grad_flat = grad_blocks.reshape(rows, columns)

        def hop(s, rising, falling):
            with jax.named_scope("spread_cotangent"):
                return (
                    lax.ppermute(rising, "dp", [(a, a + 1) for a in range(s - 1, n - 1)]),
                    lax.ppermute(falling, "dp", [(a + 1, a) for a in range(n - s)]),
                )

        with jax.named_scope("spread_tokens"):
            pieces = lax.all_to_all(
                tokens.reshape(n, group, width), "tensor", 0, 0
            )

        with jax.named_scope("ranks"):
            token_blocks = tokens.reshape(blocks_here, BLOCK, width)
            chosen_down = down_weights[adapter_of_block]
            chosen_up = up_weights[adapter_of_block]
            ranks = jnp.stack(
                [
                    jnp.einsum(
                        "uqv,upv->upq", token_blocks, chosen_down, preferred_element_type=F32
                    ),
                    2.0
                    * jnp.einsum("bkq,brq->brk", grad_blocks, chosen_up, preferred_element_type=F32),
                ]
            )
            for mask in masks:
                ranks = ranks + swap(ranks, mask)
            ranks = ranks.astype(BF16)
            shrunk, grad_rank = ranks[0], ranks[1]
            adapter_output = 2.0 * jnp.einsum(
                "psw,psd->pwd", shrunk, chosen_up, preferred_element_type=F32
            ).reshape(rows, columns)
            adapter_backward = jnp.einsum(
                "jxq,jxo->jqo", grad_rank, chosen_down, preferred_element_type=F32
            ).reshape(rows, width)
            (adapter_backward,) = after((adapter_backward,))

        with jax.named_scope("tables"):
            down_products = jnp.einsum(
                "pgz,pzq->pgq", grad_rank, token_blocks, preferred_element_type=F32
            ).astype(BF16)
            ids = jnp.broadcast_to(
                adapter_of_block[:, None, None].astype(BF16), (blocks_here, 1, width)
            )
            parcel = jnp.concatenate(
                [down_products, ids, shrunk.reshape(blocks_here, -1, width)], axis=1
            )

        spare = -blocks_here * parcel.shape[1] % 16
        load = jnp.concatenate(
            [
                grad_flat,
                parcel.reshape(-1, width),
                jnp.zeros((spare, width), BF16),
            ]
        )
        up, down = {}, {}
        up[1], down[1] = hop(1, load, load)

        with jax.named_scope("spread_tokens"):
            distances = sorted(range(1, n), key=lambda k: -abs(2 * k - n))
            by_source = {0: pick(pieces, i)}
            for k in distances:
                by_source[n - k] = rotate(pick(pieces, (i + k) % n), k)
            near = [n - k for k in distances if k in (1, n - 1)]
            rest = [r for r in range(n) if r not in near]
            full = {}
            for batch in (near, rest):
                held = jnp.stack([by_source[r] for r in batch])
                for at, mask in enumerate(reversed(masks)):
                    other = swap(held, mask)
                    odd = (t // mask) % 2 == 1
                    held = jnp.stack(
                        [jnp.where(odd, other, held), jnp.where(odd, held, other)], axis=1 + at
                    )
                for at, r in enumerate(batch):
                    full[r] = held[at].reshape(rows, width)

        with jax.named_scope("forward"):

            def project(r):
                return jnp.dot(full[r], query_weight, preferred_element_type=F32)

            parts = dict(zip(near, after([project(r).astype(BF16) for r in near])))
            near_parts = tuple(parts.values())
            for r in rest:
                if r != 0:
                    (parts[r],) = after((project(r).astype(BF16),), *near_parts)
            (own,) = after((project(0) + adapter_output,), *near_parts)

        def pull_back(batch):
            return lax.dot_general(
                jnp.concatenate([value[:rows] for value in batch]),
                query_weight,
                (((1,), (1,)), ((), ())),
                preferred_element_type=F32,
            ).astype(BF16)

        def halve(value, masks_here):
            for mask in masks_here:
                count = value.shape[0]
                halves = value.reshape(count, value.shape[1] // 2, 2, group, width)
                bit = (t // mask) % 2
                value = lax.dynamic_index_in_dim(halves, bit, 2, keepdims=False) + swap(
                    lax.dynamic_index_in_dim(halves, 1 - bit, 2, keepdims=False), mask
                )
            return value

        up_sum = down_sum = None
        for s in range(1, n):
            d = n - s
            with jax.named_scope("forward"):
                sends = (
                    (parts[d], parts[n - d])
                    if s == 1
                    else (parts[d] + up_sum, parts[n - d] + down_sum)
                )
                if s == 2:
                    first = after([load, jnp.where(lower, down[1], up[1])], own)
                    first_value = pull_back(first).reshape(-1, n, group, width)
                    *sends, first_value = after((*sends, first_value))
                    first_value = halve(first_value, masks)[:, 0]
                if s == n - 1:
                    middle = after(
                        [jnp.where(lower, down[r], up[r]) for r in range(2, half + 1)], own
                    )
                    middle_value = pull_back(middle).reshape(-1, n, group, width)
                    *sends, middle_value = after((*sends, middle_value))
                up_sum = lax.ppermute(sends[0], "dp", [(a, a + 1) for a in range(s)])
                down_sum = lax.ppermute(sends[1], "dp", [(a, a - 1) for a in range(d, n)])
            up[s], down[s] = after((up[s], down[s]), *(near_parts if s == 1 else sends))
            if s < n - 1:
                up[s + 1], down[s + 1] = hop(s + 1, up[s], down[s])
        with jax.named_scope("forward"):
            query = (own + up_sum.astype(F32) + down_sum.astype(F32)).astype(BF16)

        def slot(r):
            k = jnp.minimum(r, n - r)
            return jnp.where((r == 0) | (r == half), r, jnp.where((r < half) == lower, k, half + k))

        def distance(at):
            if at <= half:
                return jnp.where(lower, at, (n - at) % n)
            return jnp.where(lower, n + half - at, at - half)

        late = [
            jnp.where(
                lower,
                jnp.where(i >= r, up[r], down[n - r]),
                jnp.where(i + r <= n - 1, down[r], up[n - r]),
            )
            for r in range(1, half)
        ]
        loads = [*first, *middle, *late]

        with jax.named_scope("backward"):
            late_value = pull_back(late).reshape(-1, n, group, width)
            last_value = halve(jnp.concatenate([middle_value, late_value]), masks)[:, 0]
            sums = jnp.concatenate([first_value, last_value])
            back = [
                lax.ppermute(
                    pick(sums, slot((t + m) % n)),
                    ("dp", "tensor"),
                    [(a * n + b, ((a + b + m) % n) * n + a) for a in range(n) for b in range(n)],
                )
                for m in range(n)
            ]
            returned = jnp.concatenate(
                [lax.select_n((i - t - q) % n, *back) for q in range(n)], axis=0
            )
            token_gradient = (returned.astype(F32) + adapter_backward).astype(BF16)

        with jax.named_scope("tables"):
            *loads, sums = after((*loads, sums))
            grads = [value[:rows] for value in loads]
            parcels = [
                value[rows : value.shape[0] - spare].reshape(blocks_here, -1, width) for value in loads
            ]
            parcels = jnp.stack(parcels)
            parcel = jnp.concatenate([pick(parcels, slot((g - i) % n)) for g in range(n)], axis=0)
            blocks = parcel.shape[0]
            ids = parcel[:, rank, 0].astype(jnp.int32)
            all_shrunk = parcel[:, rank + 1 :].reshape(n, blocks_here, rank, BLOCK)
            shape = (ADAPTER_COUNT, rank, blocks, rank)
            hits = (
                (lax.broadcasted_iota(jnp.int32, shape, 0) == ids[None, None, :, None])
                & (
                    lax.broadcasted_iota(jnp.int32, shape, 1)
                    == lax.broadcasted_iota(jnp.int32, shape, 3)
                )
            ).astype(BF16)
            hits = hits.reshape(ADAPTER_COUNT * rank, blocks * rank)

            def table(products):
                return jnp.dot(
                    hits,
                    products.reshape(blocks * rank, products.shape[-1]),
                    preferred_element_type=F32,
                ).reshape(ADAPTER_COUNT, rank, products.shape[-1])

            grad_down = table(parcel[:, :rank])
            up_products = jnp.stack(
                [
                    (
                        2.0
                        * jnp.einsum(
                            "brk,bkq->brq",
                            pick(all_shrunk, (i + distance(at)) % n),
                            held.reshape(blocks_here, BLOCK, columns),
                            preferred_element_type=F32,
                        )
                    ).astype(BF16)
                    for at, held in enumerate(grads)
                ]
            )
            grad_up = table(
                jnp.concatenate([pick(up_products, slot((g - i) % n)) for g in range(n)], axis=0)
            )
        return (query, token_gradient, grad_down, grad_up)

    return local


def solution(mesh):
    assert mesh.shape["dp"] == mesh.shape["tensor"]
    return jax.shard_map(
        make_local(mesh.shape["tensor"]),
        mesh=mesh,
        in_specs=(
            P(("parts", "dp"), "tensor"),
            P("dp", "tensor"),
            P("parts", None, "tensor"),
            P("parts", None, "tensor"),
            P(("parts", "dp"), "tensor"),
            P(("parts", "dp")),
            P(("parts", "dp")),
        ),
        out_specs=(
            P(("parts", "dp"), "tensor"),
            P(("parts", "dp"), "tensor"),
            P("parts", None, "tensor"),
            P("parts", None, "tensor"),
        ),
        check_vma=False,
    )
```

time: 221 us -> 210 us (0.950)
  blocking collectives: 18.3 us -> 0 us
  matrix products: 40.9 us -> 50.2 us
  local copies, waits for them, and re-layouts: 6.5 us -> 15.2 us
  waiting for transfers between devices: 76.3 us -> 69.5 us
  starting transfers between devices: 61.5 us -> 55.2 us
    all_gather x1 -> x0, blocking collectives: 18.3 us -> none  [local(): parcel = lax.all_gather(parcel, 'dp', axis=0, tiled=True)]
    ppermute x10, waiting for transfers between devices: 13.9 us -> 30.8 us  [swap(): return lax.ppermute(x, 'tensor', [(t, t ^ mask) for t in range(n)])]
    ppermute x10, waiting for transfers between devices: 33 us -> 22.7 us  [the longest x4 13.9 us: local(): lax.ppermute(pick(sums, slot((t + m) % n)), ('dp', 'tensor'), [(a * n + b...]
    ppermute x3, waiting for transfers between devices: 18.2 us -> 9.56 us  [rotate(): return lax.ppermute(x, 'dp', [(i, (i + k) % n) for i in range(n)])]
    all_to_all x1, waiting for transfers between devices: 8.57 us -> 0.01 us  [local(): pieces = lax.all_to_all(tokens.reshape(n, group, width), 'tensor', 0, 0)]
    ppermute x10, starting transfers between devices: 30.2 us -> 23.7 us  [the longest x4 11.4 us: local(): lax.ppermute(pick(sums, slot((t + m) % n)), ('dp', 'tensor'), [(a * n + b...]
    dot_general x6 -> x7, matrix products: 17.3 us -> 23.5 us  [the longest x3 22.5 us: pull_back(): lax.dot_general(jnp.concatenate([value[:rows] for value in batch]), query...]
    dot_general x4, matrix products: 9.69 us -> 14.1 us  [project(): return jnp.dot(full[r], query_weight, preferred_element_type=F32)]
  transfers between devices with their start and end apart: 30 -> 30, of which waited for: 12 -> 14; matrix products, arithmetic and copies ran while one was open for 23% -> 32% of each run, Pallas kernels for 0% -> 0%
where the time goes in v4:
time: 210 us; the launch traced here: 207 us
  waiting for transfers between devices  69.5 us (33%)
  starting transfers between devices  55.2 us (26%)
  matrix products  50.2 us (24%)
  other arithmetic  15.4 us (7%)
  local copies, waits for them, and re-layouts  15.2 us (7%)
    ppermute x10, waiting for transfers between devices, swap(): return lax.ppermute(x, 'tensor', [(t, t ^ mask) for t in range(n)])  30.8 us
    dot_general x3, matrix products, pull_back(): lax.dot_general(jnp.concatenate([value[:rows] for value in batch]), query...  22.5 us
    dot_general x4, matrix products, project(): return jnp.dot(full[r], query_weight, preferred_element_type=F32)  14.1 us
    ppermute x4, waiting for transfers between devices, local(): lax.ppermute(pick(sums, slot((t + m) % n)), ('dp', 'tensor'), [(a * n + b...  13.9 us
    ppermute x4, starting transfers between devices, local(): lax.ppermute(pick(sums, slot((t + m) % n)), ('dp', 'tensor'), [(a * n + b...  11.4 us
    ppermute x3, waiting for transfers between devices, rotate(): return lax.ppermute(x, 'dp', [(i, (i + k) % n) for i in range(n)])  9.56 us
    ppermute x3, waiting for transfers between devices, local(): up_sum = lax.ppermute(sends[0], 'dp', [(a, a + 1) for a in range(s)])  8.72 us
    ppermute x3, starting transfers between devices, local(): up_sum = lax.ppermute(sends[0], 'dp', [(a, a + 1) for a in range(s)])  7.59 us
  transfers between devices with their start and end apart: 30, of which 14 were waited for; matrix products, arithmetic and copies ran while one was open for 32% of the time, Pallas kernels for 0%

profile of v4, /device:TPU:10, one launch (start us, length us, event | category | flops | bytes accessed | tf_op | source)
XLA Modules:
  0.0 207.5 jit_solution(15755780257077322635)
XLA Ops:
  2.8 2.2 %gather_fusion = bf16[2,16,2048]{2,1,0:T(8,128)(2,1)S(1)} fusion(bf16[32,16,2048]{2,1,0:T(8,128)(2,1)} %param.9, s32[1024]{0:T(1024)S(1)} %pad_clamp_fusion), kind=kCustom, calls=%fused_computation | custom fusion | bytes 262152 | tf_op jit(solution)/shard_map/ranks/gather | solution.py:73
  5.0 1.6 convolution_bitcast_fusion
  6.6 1.8 fusion.11
  8.5 4.0 %all-to-all-start = ((bf16[4,64,2048]{2,1,0:T(8,128)(2,1)}), bf16[4,64,2048]{2,1,0:T(8,128)(2,1)S(1)}, u32[]{:S(2)}, u32[]{:S(2)}) async-start(bf16[4,64,2048]{2,1,0:T(8,128)(2,1)} %bitcast), calls=%async_computation | async-start | bytes 2097152 | tf_op jit(solution)/shard_map/spread_tokens/all_to_all | solution.py:67
  13.5 12.5 %collective-permute-done.4 = f32[2,2,16,128]{3,2,1,0:T(8,128)S(1)} collective-permute-done((f32[2,2,16,128]{3,2,1,0:T(8,128)S(1)}, f32[2,2,16,128]{3,2,1,0:T(8,128)S(1)}, u32[]{:S(2)}, u32[]{:S(2)}) %collective-permute-start.4) | collective-permute-done | bytes 32800 | tf_op jit(solution)/shard_map/ranks/ppermute | solution.py:26
  26.2 2.0 collective-permute-start.5
  28.2 1.5 convolution_convert_fusion.6
  29.9 4.5 %collective-permute-start = (bf16[64,2048]{1,0:T(8,128)(2,1)S(1)}, bf16[64,2048]{1,0:T(8,128)(2,1)S(1)}, u32[]{:S(2)}, u32[]{:S(2)}) collective-permute-start(bf16[64,2048]{1,0:T(8,128)(2,1)S(1)} %get-tuple-element.75), channel_id=1, source_target_pairs={{0,8},{4,12},{8,0},{12,4},{1,9},{5,13},{9,1},{13,5},{2,10},{6,14},... | collective-permute-start | bytes 786440 | tf_op jit(solution)/shard_map/spread_tokens/ppermute | solution.py:29
  35.6 7.5 %collective-permute-done.5 = bf16[64,2048]{1,0:T(8,128)(2,1)S(1)} collective-permute-done((bf16[64,2048]{1,0:T(8,128)(2,1)S(1)}, bf16[64,2048]{1,0:T(8,128)(2,1)S(1)}, u32[]{:S(2)}, u32[]{:S(2)}) %collective-permute-start.5) | collective-permute-done | bytes 262176 | tf_op jit(solution)/shard_map/spread_tokens/ppermute | solution.py:29
  43.1 1.8 collective-permute-start.7
  45.1 2.5 %collective-permute-start.12 = (bf16[304,2048]{1,0:T(8,128)(2,1)S(1)}, bf16[304,2048]{1,0:T(8,128)(2,1)S(1)}, u32[]{:S(2)}, u32[]{:S(2)}) collective-permute-start(bf16[304,2048]{1,0:T(8,128)(2,1)S(1)} %maximum_maximum_fusion), channel_id=1, source_target_pairs={{4,0},{8,4},{12,8},{5,1},{9,5},{13,9},{6,2},{10,6},{14,10},{7,3},{... | collective-permute-start | bytes 3735560 | tf_op jit(solution)/shard_map/spread_cotangent/ppermute | solution.py:63
  47.6 3.4 %collective-permute-start.11 = (bf16[304,2048]{1,0:T(8,128)(2,1)S(1)}, bf16[304,2048]{1,0:T(8,128)(2,1)S(1)}, u32[]{:S(2)}, u32[]{:S(2)}) collective-permute-start(bf16[304,2048]{1,0:T(8,128)(2,1)S(1)} %maximum_maximum_fusion), channel_id=1, source_target_pairs={{0,4},{4,8},{8,12},{1,5},{5,9},{9,13},{2,6},{6,10},{10,14},{3,7},{... | collective-permute-start | bytes 3735560 | tf_op jit(solution)/shard_map/spread_cotangent/ppermute | solution.py:62
  51.9 1.8 collective-permute-start.1
  53.7 4.3 %collective-permute-done.7 = bf16[2,64,2048]{2,1,0:T(8,128)(2,1)S(1)} collective-permute-done((bf16[2,64,2048]{2,1,0:T(8,128)(2,1)S(1)}, bf16[2,64,2048]{2,1,0:T(8,128)(2,1)S(1)}, u32[]{:S(2)}, u32[]{:S(2)}) %collective-permute-start.7) | collective-permute-done | bytes 524320 | tf_op jit(solution)/shard_map/spread_tokens/ppermute | solution.py:26
  58.3 1.8 fusion.52
  60.6 5.7 %collective-permute-done.1 = bf16[2,64,2048]{2,1,0:T(8,128)(2,1)S(1)} collective-permute-done((bf16[2,64,2048]{2,1,0:T(8,128)(2,1)S(1)}, bf16[2,64,2048]{2,1,0:T(8,128)(2,1)S(1)}, u32[]{:S(2)}, u32[]{:S(2)}) %collective-permute-start.1) | collective-permute-done | bytes 524320 | tf_op jit(solution)/shard_map/spread_tokens/ppermute | solution.py:26
  67.0 1.4 slice-done.4
  68.5 1.4 slice-done.5
  69.8 2.3 %convolution_convert_fusion.4 = bf16[256,2048]{1,0:T(8,128)(2,1)S(1)} fusion(bf16[256,2048]{1,0:T(8,128)(2,1)S(1)} %bitcast.177, bf16[2048,2048]{1,0:T(8,128)(2,1)S(1)} %bitcast.192), kind=kOutput, calls=%fused_computation.8 | convolution fusion | flops 2148007936 | bytes 10485760 | tf_op jit(solution)/shard_map/forward/dot_general | solution.py:140
  72.2 2.3 %convolution_convert_fusion.5 = bf16[256,2048]{1,0:T(8,128)(2,1)S(1)} fusion(bf16[256,2048]{1,0:T(8,128)(2,1)S(1)} %bitcast.178, bf16[2048,2048]{1,0:T(8,128)(2,1)S(1)} %bitcast.192), kind=kOutput, calls=%fused_computation.9 | convolution fusion | flops 2148007936 | bytes 10485760 | tf_op jit(solution)/shard_map/forward/dot_general | solution.py:140
  77.9 3.3 %collective-permute-start.16 = (bf16[304,2048]{1,0:T(8,128)(2,1)S(1)}, bf16[304,2048]{1,0:T(8,128)(2,1)S(1)}, u32[]{:S(2)}, u32[]{:S(2)}) collective-permute-start(bf16[304,2048]{1,0:T(8,128)(2,1)S(1)} %collective-permute-done.12), channel_id=1, source_target_pairs={{4,0},{8,4},{5,1},{9,5},{6,2},{10,6},{7,3},{11,7},{20,16},{24,20},... | collective-permute-start | bytes 3735560 | tf_op jit(solution)/shard_map/spread_cotangent/ppermute | solution.py:63
  81.2 2.8 %collective-permute-start.15 = (bf16[304,2048]{1,0:T(8,128)(2,1)S(1)}, bf16[304,2048]{1,0:T(8,128)(2,1)S(1)}, u32[]{:S(2)}, u32[]{:S(2)}) collective-permute-start(bf16[304,2048]{1,0:T(8,128)(2,1)S(1)} %collective-permute-done.11), channel_id=1, source_target_pairs={{4,8},{8,12},{5,9},{9,13},{6,10},{10,14},{7,11},{11,15},{20,24},{2... | collective-permute-start | bytes 3735560 | tf_op jit(solution)/shard_map/spread_cotangent/ppermute | solution.py:62
  84.6 3.8 %convolution_add_fusion = f32[256,2048]{1,0:T(8,128)} fusion(f32[256,2048]{1,0:T(8,128)S(1)} %bitcast.174, bf16[256,2048]{1,0:T(8,128)(2,1)S(1)} %bitcast.186, bf16[2048,2048]{1,0:T(8,128)(2,1)S(1)} %bitcast.192), kind=kOutput, calls=%fused_computation.4 | convolution fusion | flops 2148007936 | bytes 13631488 | tf_op jit(solution)/shard_map/forward/dot_general | solution.py:140
  88.5 8.5 %convolution_convert_fusion = bf16[512,2048]{1,0:T(8,128)(2,1)S(1)} fusion(bf16[2048,2048]{1,0:T(8,128)(2,1)} %param.8, bf16[256,2048]{1,0:T(8,128)(2,1)S(1)} %slice.70, bf16[256,2048]{1,0:T(8,128)(2,1)S(1)} %slice.69), kind=kOutput, calls=%fused_computation.2 | convolution fusion | flops 4300210176 | bytes 12582912 | tf_op jit(solution)/shard_map/forward/dot_general | solution.py:150
  97.0 5.7 %convolution_convert_fusion.3 = bf16[256,2048]{1,0:T(8,128)(2,1)S(1)} fusion(bf16[256,2048]{1,0:T(8,128)(2,1)S(1)} %bitcast.185, bf16[2048,2048]{1,0:T(8,128)(2,1)} %param.8), kind=kOutput, calls=%fused_computation.7 | convolution fusion | flops 2148007936 | bytes 10485760 | tf_op jit(solution)/shard_map/forward/dot_general | solution.py:140
  103.2 1.9 collective-permute-start.13
  106.5 2.1 %collective-permute-done.16 = bf16[304,2048]{1,0:T(8,128)(2,1)S(1)} collective-permute-done((bf16[304,2048]{1,0:T(8,128)(2,1)S(1)}, bf16[304,2048]{1,0:T(8,128)(2,1)S(1)}, u32[]{:S(2)}, u32[]{:S(2)}) %collective-permute-start.16) | collective-permute-done | bytes 1245216 | tf_op jit(solution)/shard_map/spread_cotangent/ppermute | solution.py:63
  108.6 3.1 %collective-permute-done.15 = bf16[304,2048]{1,0:T(8,128)(2,1)S(1)} collective-permute-done((bf16[304,2048]{1,0:T(8,128)(2,1)S(1)}, bf16[304,2048]{1,0:T(8,128)(2,1)S(1)}, u32[]{:S(2)}, u32[]{:S(2)}) %collective-permute-start.15) | collective-permute-done | bytes 1245216 | tf_op jit(solution)/shard_map/spread_cotangent/ppermute | solution.py:62
  113.9 7.3 %convolution_convert_fusion.2 = bf16[256,2048]{1,0:T(8,128)(2,1)} fusion(bf16[2048,2048]{1,0:T(8,128)(2,1)} %param.8, bf16[304,2048]{1,0:T(8,128)(2,1)S(1)} %broadcast_select_fusion), kind=kOutput, calls=%fused_computation.6 | convolution fusion | flops 2148007936 | bytes 10485760 | tf_op jit(solution)/shard_map/forward/dot_general | solution.py:150
  122.2 1.4 collective-permute-start.20
  123.6 8.7 %collective-permute-done.13 = bf16[256,2048]{1,0:T(8,128)(2,1)S(1)} collective-permute-done((bf16[256,2048]{1,0:T(8,128)(2,1)S(1)}, bf16[256,2048]{1,0:T(8,128)(2,1)S(1)}, u32[]{:S(2)}, u32[]{:S(2)}) %collective-permute-start.13) | collective-permute-done | bytes 1048608 | tf_op jit(solution)/shard_map/forward/ppermute | solution.py:187
  132.3 1.4 add.270
  133.7 1.4 add.271
  135.0 4.4 %collective-permute-start.17 = (bf16[256,2048]{1,0:T(8,128)(2,1)}, bf16[256,2048]{1,0:T(8,128)(2,1)}, u32[]{:S(2)}, u32[]{:S(2)}) collective-permute-start(bf16[256,2048]{1,0:T(8,128)(2,1)} %add.270), channel_id=1, source_target_pairs={{0,4},{4,8},{8,12},{1,5},{5,9},{9,13},{2,6},{6,10},{10,14},{3,7},{... | collective-permute-start | bytes 3145736 | tf_op jit(solution)/shard_map/forward/ppermute | solution.py:187
  139.4 2.7 %collective-permute-start.18 = (bf16[256,2048]{1,0:T(8,128)(2,1)}, bf16[256,2048]{1,0:T(8,128)(2,1)}, u32[]{:S(2)}, u32[]{:S(2)}) collective-permute-start(bf16[256,2048]{1,0:T(8,128)(2,1)} %add.271), channel_id=1, source_target_pairs={{4,0},{8,4},{12,8},{5,1},{9,5},{13,9},{6,2},{10,6},{14,10},{7,3},{... | collective-permute-start | bytes 3145736 | tf_op jit(solution)/shard_map/forward/ppermute | solution.py:188
  147.0 1.5 pad_maximum_fusion.5
  148.5 6.7 %convolution_convert_fusion.1 = bf16[256,2048]{1,0:T(8,128)(2,1)} fusion(bf16[2048,2048]{1,0:T(8,128)(2,1)} %param.8, bf16[304,2048]{1,0:T(8,128)(2,1)S(1)} %select_select_fusion), kind=kOutput, calls=%fused_computation.5 | convolution fusion | flops 2148007936 | bytes 10485760 | tf_op jit(solution)/shard_map/backward/dot_general | solution.py:150
  160.1 2.7 %fusion.35 = f32[32,16,2048]{2,1,0:T(8,128)} fusion(bf16[128,2048,1]{1,0,2:T(8,128)(2,1)S(1)} %bitcast.173, s32[128]{0:T(128)S(1)} %iota.42, s32[128]{0:T(128)S(1)} %eq.206), kind=kOutput, calls=%fused_computation.106 | convolution fusion | flops 268632064 | bytes 4719616 | tf_op jit(solution)/shard_map/tables/dot_general | solution.py:253
  162.9 1.5 collective-permute-start.24
  164.4 2.7 %fusion.37 = f32[32,16,2048]{2,1,0:T(8,128)} fusion(bf16[128,2048,1]{1,0,2:T(8,128)(2,1)S(1)} %bitcast.172, s32[128]{0:T(128)S(1)} %iota.42, s32[128]{0:T(128)S(1)} %eq.206), kind=kOutput, calls=%fused_computation.107 | convolution fusion | flops 268632064 | bytes 4719616 | tf_op jit(solution)/shard_map/tables/dot_general | solution.py:253
  168.2 8.2 %collective-permute-done.24 = bf16[2,1,64,2048]{3,2,1,0:T(8,128)(2,1)S(1)} collective-permute-done((bf16[2,1,64,2048]{3,2,1,0:T(8,128)(2,1)S(1)}, bf16[2,1,64,2048]{3,2,1,0:T(8,128)(2,1)S(1)}, u32[]{:S(2)}, u32[]{:S(2)}) %collective-permute-start.24) | collective-permute-done | bytes 524320 | tf_op jit(solution)/shard_map/backward/ppermute | solution.py:26
  176.9 1.9 collective-permute-start.26
  178.9 3.8 %collective-permute-start.27 = (bf16[64,2048]{1,0:T(8,128)(2,1)S(1)}, bf16[64,2048]{1,0:T(8,128)(2,1)S(1)}, u32[]{:S(2)}, u32[]{:S(2)}) collective-permute-start(bf16[64,2048]{1,0:T(8,128)(2,1)S(1)} %get-tuple-element.65), channel_id=1, source_target_pairs={{0,8},{1,12},{2,0},{3,4},{4,13},{5,1},{6,5},{7,9},{8,2},{9,6},{10,... | collective-permute-start | bytes 786440 | tf_op jit(solution)/shard_map/backward/ppermute | solution.py:219
  182.7 2.6 %collective-permute-start.28 = (bf16[64,2048]{1,0:T(8,128)(2,1)S(1)}, bf16[64,2048]{1,0:T(8,128)(2,1)S(1)}, u32[]{:S(2)}, u32[]{:S(2)}) collective-permute-start(bf16[64,2048]{1,0:T(8,128)(2,1)S(1)} %get-tuple-element.66), channel_id=1, source_target_pairs={{0,12},{1,0},{2,4},{3,8},{4,1},{5,5},{6,9},{7,13},{8,6},{9,10},{10... | collective-permute-start | bytes 786440 | tf_op jit(solution)/shard_map/backward/ppermute | solution.py:219
  185.3 3.0 %collective-permute-start.25 = (bf16[64,2048]{1,0:T(8,128)(2,1)S(1)}, bf16[64,2048]{1,0:T(8,128)(2,1)S(1)}, u32[]{:S(2)}, u32[]{:S(2)}) collective-permute-start(bf16[64,2048]{1,0:T(8,128)(2,1)S(1)} %get-tuple-element.67), channel_id=1, source_target_pairs={{0,0},{1,4},{2,8},{3,12},{4,5},{5,9},{6,13},{7,1},{8,10},{9,14},{1... | collective-permute-start | bytes 786440 | tf_op jit(solution)/shard_map/backward/ppermute | solution.py:219
  188.4 3.1 %add_convert_fusion.1 = bf16[256,2048]{1,0:T(8,128)(2,1)} fusion(bf16[256,2048]{1,0:T(8,128)(2,1)} %collective-permute-done.18, f32[256,2048]{1,0:T(8,128)S(1)} %copy-done.9, bf16[256,2048]{1,0:T(8,128)(2,1)} %collective-permute-done.17), kind=kLoop, calls=%fused_computation.35 | loop fusion | flops 2621440 | bytes 5242880 | tf_op jit(solution)/shard_map/forward/convert_element_type | solution.py:193
  191.5 10.3 %collective-permute-done.27 = bf16[64,2048]{1,0:T(8,128)(2,1)S(1)} collective-permute-done((bf16[64,2048]{1,0:T(8,128)(2,1)S(1)}, bf16[64,2048]{1,0:T(8,128)(2,1)S(1)}, u32[]{:S(2)}, u32[]{:S(2)}) %collective-permute-start.27) | collective-permute-done | bytes 262176 | tf_op jit(solution)/shard_map/backward/ppermute | solution.py:219
  201.8 2.3 %collective-permute-done.28 = bf16[64,2048]{1,0:T(8,128)(2,1)S(1)} collective-permute-done((bf16[64,2048]{1,0:T(8,128)(2,1)S(1)}, bf16[64,2048]{1,0:T(8,128)(2,1)S(1)}, u32[]{:S(2)}, u32[]{:S(2)}) %collective-permute-start.28) | collective-permute-done | bytes 262176 | tf_op jit(solution)/shard_map/backward/ppermute | solution.py:219
  (150 shorter events, 30.6 us)
Async XLA Ops:
  0.6 1.6 copy-start
  2.8 5.6 %copy-start.12 = (bf16[2,16,2048]{2,1,0:T(8,128)(2,1)}, bf16[2,16,2048]{2,1,0:T(8,128)(2,1)S(1)}, u32[]{:S(2)}) copy-start(bf16[2,16,2048]{2,1,0:T(8,128)(2,1)S(1)} %gather_fusion.1) | copy-start | bytes 393220
  6.6 6.0 %copy-start.10 = (bf16[256,2048]{1,0:T(8,128)(2,1)S(1)}, bf16[256,2048]{1,0:T(8,128)(2,1)}, u32[]{:S(2)}) copy-start(bf16[256,2048]{1,0:T(8,128)(2,1)} %param.11) | copy-start | bytes 3145732
  8.4 4.1 %collective-permute-start.3 = (f32[2,2,16,128]{3,2,1,0:T(8,128)S(1)}, f32[2,2,16,128]{3,2,1,0:T(8,128)S(1)}, u32[]{:S(2)}, u32[]{:S(2)}) collective-permute-start(f32[2,2,16,128]{3,2,1,0:T(8,128)S(1)} %pad_maximum_fusion.11), channel_id=1, source_target_pairs={{0,1},{1,0},{2,3},{3,2},{4,5},{5,4},{6,7},{7,6},{8,9},{9,8},{10,11... | collective-permute-start | bytes 98312 | tf_op jit(solution)/shard_map/ranks/ppermute | solution.py:26
  8.5 17.6 %all-to-all-start = ((bf16[4,64,2048]{2,1,0:T(8,128)(2,1)}), bf16[4,64,2048]{2,1,0:T(8,128)(2,1)S(1)}, u32[]{:S(2)}, u32[]{:S(2)}) async-start(bf16[4,64,2048]{2,1,0:T(8,128)(2,1)} %bitcast), calls=%async_computation | async-start | bytes 2097152 | tf_op jit(solution)/shard_map/spread_tokens/all_to_all | solution.py:67
  12.5 13.5 %collective-permute-start.4 = (f32[2,2,16,128]{3,2,1,0:T(8,128)S(1)}, f32[2,2,16,128]{3,2,1,0:T(8,128)S(1)}, u32[]{:S(2)}, u32[]{:S(2)}) collective-permute-start(f32[2,2,16,128]{3,2,1,0:T(8,128)S(1)} %fusion.57), channel_id=1, source_target_pairs={{0,2},{1,3},{2,0},{3,1},{4,6},{5,7},{6,4},{7,5},{8,10},{9,11},{10,... | collective-permute-start | bytes 98312 | tf_op jit(solution)/shard_map/ranks/ppermute | solution.py:26
  26.1 9.4 %collective-permute-start.6 = (bf16[64,2048]{1,0:T(8,128)(2,1)S(1)}, bf16[64,2048]{1,0:T(8,128)(2,1)S(1)}, u32[]{:S(2)}, u32[]{:S(2)}) collective-permute-start(bf16[64,2048]{1,0:T(8,128)(2,1)S(1)} %get-tuple-element.73), channel_id=1, source_target_pairs={{0,12},{4,0},{8,4},{12,8},{1,13},{5,1},{9,5},{13,9},{2,14},{6,2},{... | collective-permute-start | bytes 786440 | tf_op jit(solution)/shard_map/spread_tokens/ppermute | solution.py:29
  26.2 16.8 %collective-permute-start.5 = (bf16[64,2048]{1,0:T(8,128)(2,1)S(1)}, bf16[64,2048]{1,0:T(8,128)(2,1)S(1)}, u32[]{:S(2)}, u32[]{:S(2)}) collective-permute-start(bf16[64,2048]{1,0:T(8,128)(2,1)S(1)} %get-tuple-element.74), channel_id=1, source_target_pairs={{0,4},{4,8},{8,12},{12,0},{1,5},{5,9},{9,13},{13,1},{2,6},{6,10},{... | collective-permute-start | bytes 786440 | tf_op jit(solution)/shard_map/spread_tokens/ppermute | solution.py:29
  29.9 22.0 %collective-permute-start = (bf16[64,2048]{1,0:T(8,128)(2,1)S(1)}, bf16[64,2048]{1,0:T(8,128)(2,1)S(1)}, u32[]{:S(2)}, u32[]{:S(2)}) collective-permute-start(bf16[64,2048]{1,0:T(8,128)(2,1)S(1)} %get-tuple-element.75), channel_id=1, source_target_pairs={{0,8},{4,12},{8,0},{12,4},{1,9},{5,13},{9,1},{13,5},{2,10},{6,14},... | collective-permute-start | bytes 786440 | tf_op jit(solution)/shard_map/spread_tokens/ppermute | solution.py:29
  43.1 14.9 %collective-permute-start.7 = (bf16[2,64,2048]{2,1,0:T(8,128)(2,1)S(1)}, bf16[2,64,2048]{2,1,0:T(8,128)(2,1)S(1)}, u32[]{:S(2)}, u32[]{:S(2)}) collective-permute-start(bf16[2,64,2048]{2,1,0:T(8,128)(2,1)S(1)} %pad_maximum_fusion.7), channel_id=1, source_target_pairs={{0,2},{1,3},{2,0},{3,1},{4,6},{5,7},{6,4},{7,5},{8,10},{9,11},{10,... | collective-permute-start | bytes 1572872 | tf_op jit(solution)/shard_map/spread_tokens/ppermute | solution.py:26
  45.1 32.8 %collective-permute-start.12 = (bf16[304,2048]{1,0:T(8,128)(2,1)S(1)}, bf16[304,2048]{1,0:T(8,128)(2,1)S(1)}, u32[]{:S(2)}, u32[]{:S(2)}) collective-permute-start(bf16[304,2048]{1,0:T(8,128)(2,1)S(1)} %maximum_maximum_fusion), channel_id=1, source_target_pairs={{4,0},{8,4},{12,8},{5,1},{9,5},{13,9},{6,2},{10,6},{14,10},{7,3},{... | collective-permute-start | bytes 3735560 | tf_op jit(solution)/shard_map/spread_cotangent/ppermute | solution.py:63
  47.6 30.3 %collective-permute-start.11 = (bf16[304,2048]{1,0:T(8,128)(2,1)S(1)}, bf16[304,2048]{1,0:T(8,128)(2,1)S(1)}, u32[]{:S(2)}, u32[]{:S(2)}) collective-permute-start(bf16[304,2048]{1,0:T(8,128)(2,1)S(1)} %maximum_maximum_fusion), channel_id=1, source_target_pairs={{0,4},{4,8},{8,12},{1,5},{5,9},{9,13},{2,6},{6,10},{10,14},{3,7},{... | collective-permute-start | bytes 3735560 | tf_op jit(solution)/shard_map/spread_cotangent/ppermute | solution.py:62
  51.9 14.4 %collective-permute-start.1 = (bf16[2,64,2048]{2,1,0:T(8,128)(2,1)S(1)}, bf16[2,64,2048]{2,1,0:T(8,128)(2,1)S(1)}, u32[]{:S(2)}, u32[]{:S(2)}) collective-permute-start(bf16[2,64,2048]{2,1,0:T(8,128)(2,1)S(1)} %pad_maximum_fusion.6), channel_id=1, source_target_pairs={{0,2},{1,3},{2,0},{3,1},{4,6},{5,7},{6,4},{7,5},{8,10},{9,11},{10,... | collective-permute-start | bytes 1572872 | tf_op jit(solution)/shard_map/spread_tokens/ppermute | solution.py:26
  58.1 2.0 copy-start.13
  58.2 8.3 %collective-permute-start.8 = (bf16[2,2,64,2048]{3,2,0,1:T(8,128)(2,1)S(1)}, bf16[2,2,64,2048]{3,2,0,1:T(8,128)(2,1)S(1)}, u32[]{:S(2)}, u32[]{:S(2)}) collective-permute-start(bf16[2,2,64,2048]{3,2,0,1:T(8,128)(2,1)S(1)} %pad_maximum_fusion.4), channel_id=1, source_target_pairs={{0,1},{1,0},{2,3},{3,2},{4,5},{5,4},{6,7},{7,6},{8,9},{9,8},{10,11... | collective-permute-start | bytes 3145736 | tf_op jit(solution)/shard_map/spread_tokens/ppermute | solution.py:26
  66.3 2.2 %slice-start.4 = ((s8[8388608]{0:T(1024)(128)(4,1)}), s8[4194304]{0:T(1024)(128)(4,1)S(1)}, s32[]{:S(2)}) async-start(s8[8388608]{0:T(1024)(128)(4,1)} %bitcast.191), calls=%async_computation.5 | async-start | bytes 8388608
  66.4 17.8 %collective-permute-start.2 = (bf16[2,2,64,2048]{3,2,1,0:T(8,128)(2,1)S(1)}, bf16[2,2,64,2048]{3,2,1,0:T(8,128)(2,1)S(1)}, u32[]{:S(2)}, u32[]{:S(2)}) collective-permute-start(bf16[2,2,64,2048]{3,2,1,0:T(8,128)(2,1)S(1)} %pad_maximum_fusion.3), channel_id=1, source_target_pairs={{0,1},{1,0},{2,3},{3,2},{4,5},{5,4},{6,7},{7,6},{8,9},{9,8},{10,11... | collective-permute-start | bytes 3145736 | tf_op jit(solution)/shard_map/spread_tokens/ppermute | solution.py:26
  66.7 3.1 %slice-start.5 = ((s8[8388608]{0:T(1024)(128)(4,1)}), s8[4194304]{0:T(1024)(128)(4,1)S(1)}, s32[]{:S(2)}) async-start(s8[8388608]{0:T(1024)(128)(4,1)} %bitcast.191), calls=%async_computation.6 | async-start | bytes 8388608
  74.5 28.2 %collective-permute-start.9 = (bf16[256,2048]{1,0:T(8,128)(2,1)S(1)}, bf16[256,2048]{1,0:T(8,128)(2,1)S(1)}, u32[]{:S(2)}, u32[]{:S(2)}) collective-permute-start(bf16[256,2048]{1,0:T(8,128)(2,1)S(1)} %convolution_convert_fusion.5), channel_id=1, source_target_pairs={{0,4},{1,5},{2,6},{3,7},{16,20},{17,21},{18,22},{19,23}} | collective-permute-start | bytes 3145736 | tf_op jit(solution)/shard_map/forward/ppermute | solution.py:187
  75.8 26.9 %collective-permute-start.10 = (bf16[256,2048]{1,0:T(8,128)(2,1)S(1)}, bf16[256,2048]{1,0:T(8,128)(2,1)S(1)}, u32[]{:S(2)}, u32[]{:S(2)}) collective-permute-start(bf16[256,2048]{1,0:T(8,128)(2,1)S(1)} %convolution_convert_fusion.4), channel_id=1, source_target_pairs={{12,8},{13,9},{14,10},{15,11},{28,24},{29,25},{30,26},{31,27}} | collective-permute-start | bytes 3145736 | tf_op jit(solution)/shard_map/forward/ppermute | solution.py:188
  77.9 30.7 %collective-permute-start.16 = (bf16[304,2048]{1,0:T(8,128)(2,1)S(1)}, bf16[304,2048]{1,0:T(8,128)(2,1)S(1)}, u32[]{:S(2)}, u32[]{:S(2)}) collective-permute-start(bf16[304,2048]{1,0:T(8,128)(2,1)S(1)} %collective-permute-done.12), channel_id=1, source_target_pairs={{4,0},{8,4},{5,1},{9,5},{6,2},{10,6},{7,3},{11,7},{20,16},{24,20},... | collective-permute-start | bytes 3735560 | tf_op jit(solution)/shard_map/spread_cotangent/ppermute | solution.py:63
  81.2 30.4 %collective-permute-start.15 = (bf16[304,2048]{1,0:T(8,128)(2,1)S(1)}, bf16[304,2048]{1,0:T(8,128)(2,1)S(1)}, u32[]{:S(2)}, u32[]{:S(2)}) collective-permute-start(bf16[304,2048]{1,0:T(8,128)(2,1)S(1)} %collective-permute-done.11), channel_id=1, source_target_pairs={{4,8},{8,12},{5,9},{9,13},{6,10},{10,14},{7,11},{11,15},{20,24},{2... | collective-permute-start | bytes 3735560 | tf_op jit(solution)/shard_map/spread_cotangent/ppermute | solution.py:62
  84.2 60.1 %copy-start.2 = (bf16[304,2048]{1,0:T(8,128)(2,1)}, bf16[304,2048]{1,0:T(8,128)(2,1)S(1)}, u32[]{:S(2)}) copy-start(bf16[304,2048]{1,0:T(8,128)(2,1)S(1)} %broadcast_select_fusion.1) | copy-start | bytes 3735556
  103.2 18.0 %collective-permute-start.19 = (bf16[2,2,64,2048]{3,2,0,1:T(8,128)(2,1)S(1)}, bf16[2,2,64,2048]{3,2,0,1:T(8,128)(2,1)S(1)}, u32[]{:S(2)}, u32[]{:S(2)}) collective-permute-start(bf16[2,2,64,2048]{3,2,0,1:T(8,128)(2,1)S(1)} %bitcast.176), channel_id=1, source_target_pairs={{0,1},{1,0},{2,3},{3,2},{4,5},{5,4},{6,7},{7,6},{8,9},{9,8},{10,11... | collective-permute-start | bytes 3145736 | tf_op jit(solution)/shard_map/forward/ppermute | solution.py:26
  103.2 29.0 %collective-permute-start.13 = (bf16[256,2048]{1,0:T(8,128)(2,1)S(1)}, bf16[256,2048]{1,0:T(8,128)(2,1)S(1)}, u32[]{:S(2)}, u32[]{:S(2)}) collective-permute-start(bf16[256,2048]{1,0:T(8,128)(2,1)S(1)} %get-tuple-element.35), channel_id=1, source_target_pairs={{0,4},{4,8},{1,5},{5,9},{2,6},{6,10},{3,7},{7,11},{16,20},{20,24},... | collective-permute-start | bytes 3145736 | tf_op jit(solution)/shard_map/forward/ppermute | solution.py:187
  105.2 28.5 %collective-permute-start.14 = (bf16[256,2048]{1,0:T(8,128)(2,1)S(1)}, bf16[256,2048]{1,0:T(8,128)(2,1)S(1)}, u32[]{:S(2)}, u32[]{:S(2)}) collective-permute-start(bf16[256,2048]{1,0:T(8,128)(2,1)S(1)} %get-tuple-element.36), channel_id=1, source_target_pairs={{8,4},{12,8},{9,5},{13,9},{10,6},{14,10},{11,7},{15,11},{24,20},{2... | collective-permute-start | bytes 3145736 | tf_op jit(solution)/shard_map/forward/ppermute | solution.py:188
  111.6 30.5 %collective-permute-start.22 = (bf16[304,2048]{1,0:T(8,128)(2,1)S(1)}, bf16[304,2048]{1,0:T(8,128)(2,1)S(1)}, u32[]{:S(2)}, u32[]{:S(2)}) collective-permute-start(bf16[304,2048]{1,0:T(8,128)(2,1)S(1)} %collective-permute-done.16), channel_id=1, source_target_pairs={{4,0},{5,1},{6,2},{7,3},{20,16},{21,17},{22,18},{23,19}} | collective-permute-start | bytes 3735560 | tf_op jit(solution)/shard_map/spread_cotangent/ppermute | solution.py:63
  113.0 29.2 %collective-permute-start.21 = (bf16[304,2048]{1,0:T(8,128)(2,1)S(1)}, bf16[304,2048]{1,0:T(8,128)(2,1)S(1)}, u32[]{:S(2)}, u32[]{:S(2)}) collective-permute-start(bf16[304,2048]{1,0:T(8,128)(2,1)S(1)} %collective-permute-done.15), channel_id=1, source_target_pairs={{8,12},{9,13},{10,14},{11,15},{24,28},{25,29},{26,30},{27,31}} | collective-permute-start | bytes 3735560 | tf_op jit(solution)/shard_map/spread_cotangent/ppermute | solution.py:62
  113.9 30.4 %copy-start.5 = (bf16[304,2048]{1,0:T(8,128)(2,1)}, bf16[304,2048]{1,0:T(8,128)(2,1)S(1)}, u32[]{:S(2)}) copy-start(bf16[304,2048]{1,0:T(8,128)(2,1)S(1)} %broadcast_select_fusion) | copy-start | bytes 3735556
  122.2 45.0 %collective-permute-start.20 = (bf16[2,1,64,2048]{3,2,0,1:T(8,128)(2,1)}, bf16[2,1,64,2048]{3,2,0,1:T(8,128)(2,1)}, u32[]{:S(2)}, u32[]{:S(2)}) collective-permute-start(bf16[2,1,64,2048]{3,2,0,1:T(8,128)(2,1)} %constant_dynamic-slice_fusion.9), channel_id=1, source_target_pairs={{0,2},{1,3},{2,0},{3,1},{4,6},{5,7},{6,4},{7,5},{8,10},{9,11},{10,... | collective-permute-start | bytes 1572872 | tf_op jit(solution)/shard_map/forward/ppermute | solution.py:26
  135.0 50.3 %collective-permute-start.17 = (bf16[256,2048]{1,0:T(8,128)(2,1)}, bf16[256,2048]{1,0:T(8,128)(2,1)}, u32[]{:S(2)}, u32[]{:S(2)}) collective-permute-start(bf16[256,2048]{1,0:T(8,128)(2,1)} %add.270), channel_id=1, source_target_pairs={{0,4},{4,8},{8,12},{1,5},{5,9},{9,13},{2,6},{6,10},{10,14},{3,7},{... | collective-permute-start | bytes 3145736 | tf_op jit(solution)/shard_map/forward/ppermute | solution.py:187
  139.4 49.0 %collective-permute-start.18 = (bf16[256,2048]{1,0:T(8,128)(2,1)}, bf16[256,2048]{1,0:T(8,128)(2,1)}, u32[]{:S(2)}, u32[]{:S(2)}) collective-permute-start(bf16[256,2048]{1,0:T(8,128)(2,1)} %add.271), channel_id=1, source_target_pairs={{4,0},{8,4},{12,8},{5,1},{9,5},{13,9},{6,2},{10,6},{14,10},{7,3},{... | collective-permute-start | bytes 3145736 | tf_op jit(solution)/shard_map/forward/ppermute | solution.py:188
  142.5 6.0 %copy-start.4 = (bf16[304,2048]{1,0:T(8,128)(2,1)}, bf16[304,2048]{1,0:T(8,128)(2,1)S(1)}, u32[]{:S(2)}) copy-start(bf16[304,2048]{1,0:T(8,128)(2,1)S(1)} %select_select_fusion) | copy-start | bytes 3735556
  155.2 2.5 %copy-start.6 = (bf16[256,2048]{1,0:T(8,128)(2,1)S(1)}, bf16[256,2048]{1,0:T(8,128)(2,1)}, u32[]{:S(2)}) copy-start(bf16[256,2048]{1,0:T(8,128)(2,1)} %convolution_convert_fusion.2) | copy-start | bytes 3145732
  155.2 2.5 %copy-start.7 = (bf16[256,2048]{1,0:T(8,128)(2,1)S(1)}, bf16[256,2048]{1,0:T(8,128)(2,1)}, u32[]{:S(2)}) copy-start(bf16[256,2048]{1,0:T(8,128)(2,1)} %convolution_convert_fusion.1) | copy-start | bytes 3145732
  156.6 1.4 slice-start.3
  157.7 1.3 slice-start.1
  157.7 1.6 copy-start.8
  157.8 1.8 slice-start.2
  157.8 4.9 %collective-permute-start.23 = (bf16[2,2,64,2048]{3,2,1,0:T(8,128)(2,1)S(1)}, bf16[2,2,64,2048]{3,2,1,0:T(8,128)(2,1)S(1)}, u32[]{:S(2)}, u32[]{:S(2)}) collective-permute-start(bf16[2,2,64,2048]{3,2,1,0:T(8,128)(2,1)S(1)} %fusion.15), channel_id=1, source_target_pairs={{0,1},{1,0},{2,3},{3,2},{4,5},{5,4},{6,7},{7,6},{8,9},{9,8},{10,11... | collective-permute-start | bytes 3145736 | tf_op jit(solution)/shard_map/backward/ppermute | solution.py:26
  162.9 13.5 %collective-permute-start.24 = (bf16[2,1,64,2048]{3,2,1,0:T(8,128)(2,1)S(1)}, bf16[2,1,64,2048]{3,2,1,0:T(8,128)(2,1)S(1)}, u32[]{:S(2)}, u32[]{:S(2)}) collective-permute-start(bf16[2,1,64,2048]{3,2,1,0:T(8,128)(2,1)S(1)} %constant_dynamic-slice_fusion.8), channel_id=1, source_target_pairs={{0,2},{1,3},{2,0},{3,1},{4,6},{5,7},{6,4},{7,5},{8,10},{9,11},{10,... | collective-permute-start | bytes 1572872 | tf_op jit(solution)/shard_map/backward/ppermute | solution.py:26
  168.2 20.2 %copy-start.9 = (f32[256,2048]{1,0:T(8,128)S(1)}, f32[256,2048]{1,0:T(8,128)}, u32[]{:S(2)}) copy-start(f32[256,2048]{1,0:T(8,128)} %convolution_add_fusion) | copy-start | bytes 6291460
  176.9 14.5 %collective-permute-start.26 = (bf16[64,2048]{1,0:T(8,128)(2,1)S(1)}, bf16[64,2048]{1,0:T(8,128)(2,1)S(1)}, u32[]{:S(2)}, u32[]{:S(2)}) collective-permute-start(bf16[64,2048]{1,0:T(8,128)(2,1)S(1)} %get-tuple-element.64), channel_id=1, source_target_pairs={{0,4},{1,8},{2,12},{3,0},{4,9},{5,13},{6,1},{7,5},{8,14},{9,2},{10... | collective-permute-start | bytes 786440 | tf_op jit(solution)/shard_map/backward/ppermute | solution.py:219
  178.9 22.9 %collective-permute-start.27 = (bf16[64,2048]{1,0:T(8,128)(2,1)S(1)}, bf16[64,2048]{1,0:T(8,128)(2,1)S(1)}, u32[]{:S(2)}, u32[]{:S(2)}) collective-permute-start(bf16[64,2048]{1,0:T(8,128)(2,1)S(1)} %get-tuple-element.65), channel_id=1, source_target_pairs={{0,8},{1,12},{2,0},{3,4},{4,13},{5,1},{6,5},{7,9},{8,2},{9,6},{10,... | collective-permute-start | bytes 786440 | tf_op jit(solution)/shard_map/backward/ppermute | solution.py:219
  182.7 21.4 %collective-permute-start.28 = (bf16[64,2048]{1,0:T(8,128)(2,1)S(1)}, bf16[64,2048]{1,0:T(8,128)(2,1)S(1)}, u32[]{:S(2)}, u32[]{:S(2)}) collective-permute-start(bf16[64,2048]{1,0:T(8,128)(2,1)S(1)} %get-tuple-element.66), channel_id=1, source_target_pairs={{0,12},{1,0},{2,4},{3,8},{4,1},{5,5},{6,9},{7,13},{8,6},{9,10},{10... | collective-permute-start | bytes 786440 | tf_op jit(solution)/shard_map/backward/ppermute | solution.py:219
  185.3 20.0 %collective-permute-start.25 = (bf16[64,2048]{1,0:T(8,128)(2,1)S(1)}, bf16[64,2048]{1,0:T(8,128)(2,1)S(1)}, u32[]{:S(2)}, u32[]{:S(2)}) collective-permute-start(bf16[64,2048]{1,0:T(8,128)(2,1)S(1)} %get-tuple-element.67), channel_id=1, source_target_pairs={{0,0},{1,4},{2,8},{3,12},{4,5},{5,9},{6,13},{7,1},{8,10},{9,14},{1... | collective-permute-start | bytes 786440 | tf_op jit(solution)/shard_map/backward/ppermute | solution.py:219
  191.4 14.1 %copy-start.3 = (f32[2,128,2048]{2,1,0:T(8,128)S(1)}, f32[2,128,2048]{2,1,0:T(8,128)}, u32[]{:S(2)}) copy-start(f32[2,128,2048]{2,1,0:T(8,128)} %fusion.52) | copy-start | bytes 6291460
  205.5 2.0 copy-start.1
  (2 other events, 1.9 us)

commit v5 on v4

--- a/solution.py
+++ b/solution.py
@@ -213,8 +213,8 @@
 
         with jax.named_scope("backward"):
             late_value = pull_back(late).reshape(-1, n, group, width)
-            last_value = halve(jnp.concatenate([middle_value, late_value]), masks)[:, 0]
-            sums = jnp.concatenate([first_value, last_value])
+            middle_sums, late_sums = halve(middle_value, masks)[:, 0], halve(late_value, masks)[:, 0]
+            sums = jnp.concatenate([first_value, middle_sums, late_sums])
             back = [
                 lax.ppermute(
                     pick(sums, slot((t + m) % n)),

time: 210 us -> 206 us (0.981)
  other arithmetic: 15.4 us -> 8.92 us
  waiting for transfers between devices: 69.5 us -> 75.3 us
    ppermute x3, waiting for transfers between devices: 0.01 us -> 11.1 us  [local(): down_sum = lax.ppermute(sends[1], 'dp', [(a, a - 1) for a in range(d, n)])]
    ppermute x3, waiting for transfers between devices: 8.72 us -> 5.1 us  [local(): up_sum = lax.ppermute(sends[0], 'dp', [(a, a + 1) for a in range(s)])]
    ppermute x3, waiting for transfers between devices: 9.56 us -> 13.2 us  [rotate(): return lax.ppermute(x, 'dp', [(i, (i + k) % n) for i in range(n)])]
    ppermute x4, waiting for transfers between devices: 13.9 us -> 10.8 us  [local(): lax.ppermute(pick(sums, slot((t + m) % n)), ('dp', 'tensor'), [(a * n + b...]
    ppermute x3, waiting for transfers between devices: 3.07 us -> 0.1 us  [hop(): lax.ppermute(rising, 'dp', [(a, a + 1) for a in range(s - 1, n - 1)])]
    ppermute x3, waiting for transfers between devices: 3.39 us -> 6.09 us  [hop(): lax.ppermute(falling, 'dp', [(a + 1, a) for a in range(n - s)])]
    ppermute x10 -> x12, waiting for transfers between devices: 30.8 us -> 28.9 us  [swap(): return lax.ppermute(x, 'tensor', [(t, t ^ mask) for t in range(n)])]
    ppermute x10 -> x12, starting transfers between devices: 6.81 us -> 7.59 us  [swap(): return lax.ppermute(x, 'tensor', [(t, t ^ mask) for t in range(n)])]
  transfers between devices with their start and end apart: 30 -> 32, of which waited for: 14 -> 16; matrix products, arithmetic and copies ran while one was open for 32% -> 25% of each run, Pallas kernels for 0% -> 0%
where the time goes in v5:
time: 206 us; the launch traced here: 205 us
  waiting for transfers between devices  75.3 us (37%)
  starting transfers between devices  56.7 us (28%)
  matrix products  48.2 us (23%)
  local copies, waits for them, and re-layouts  14 us (7%)
  other arithmetic  8.92 us (4%)
  between operations  2.08 us (1%)
    ppermute x12, waiting for transfers between devices, swap(): return lax.ppermute(x, 'tensor', [(t, t ^ mask) for t in range(n)])  28.9 us
    dot_general x3, matrix products, pull_back(): lax.dot_general(jnp.concatenate([value[:rows] for value in batch]), query...  21.9 us
    ppermute x4, starting transfers between devices, local(): lax.ppermute(pick(sums, slot((t + m) % n)), ('dp', 'tensor'), [(a * n + b...  13.2 us
    ppermute x3, waiting for transfers between devices, rotate(): return lax.ppermute(x, 'dp', [(i, (i + k) % n) for i in range(n)])  13.2 us
    dot_general x4, matrix products, project(): return jnp.dot(full[r], query_weight, preferred_element_type=F32)  12.8 us
    ppermute x3, waiting for transfers between devices, local(): down_sum = lax.ppermute(sends[1], 'dp', [(a, a - 1) for a in range(d, n)])  11.1 us
    ppermute x4, waiting for transfers between devices, local(): lax.ppermute(pick(sums, slot((t + m) % n)), ('dp', 'tensor'), [(a * n + b...  10.8 us
    ppermute x3, starting transfers between devices, hop(): lax.ppermute(rising, 'dp', [(a, a + 1) for a in range(s - 1, n - 1)])  7.82 us
  transfers between devices with their start and end apart: 32, of which 16 were waited for; matrix products, arithmetic and copies ran while one was open for 25% of the time, Pallas kernels for 0%

profile of v5, /device:TPU:10, one launch (start us, length us, event | category | flops | bytes accessed | tf_op | source)
XLA Modules:
  0.0 205.1 jit_solution(15953654587649028524)
XLA Ops:
  2.8 2.2 %gather_fusion = bf16[2,16,2048]{2,1,0:T(8,128)(2,1)S(1)} fusion(bf16[32,16,2048]{2,1,0:T(8,128)(2,1)} %param.9, s32[1024]{0:T(1024)S(1)} %pad_clamp_fusion), kind=kCustom, calls=%fused_computation | custom fusion | bytes 262152 | tf_op jit(solution)/shard_map/ranks/gather | solution.py:73
  5.0 1.6 convolution_bitcast_fusion
  6.6 1.8 fusion.11
  8.5 4.0 %all-to-all-start = ((bf16[4,64,2048]{2,1,0:T(8,128)(2,1)}), bf16[4,64,2048]{2,1,0:T(8,128)(2,1)S(1)}, u32[]{:S(2)}, u32[]{:S(2)}) async-start(bf16[4,64,2048]{2,1,0:T(8,128)(2,1)} %bitcast), calls=%async_computation | async-start | bytes 2097152 | tf_op jit(solution)/shard_map/spread_tokens/all_to_all | solution.py:67
  13.5 12.5 %collective-permute-done.4 = f32[2,2,16,128]{3,2,1,0:T(8,128)S(1)} collective-permute-done((f32[2,2,16,128]{3,2,1,0:T(8,128)S(1)}, f32[2,2,16,128]{3,2,1,0:T(8,128)S(1)}, u32[]{:S(2)}, u32[]{:S(2)}) %collective-permute-start.4) | collective-permute-done | bytes 32800 | tf_op jit(solution)/shard_map/ranks/ppermute | solution.py:26
  26.1 1.6 collective-permute-start.5
  28.2 1.5 convolution_convert_fusion.6
  29.9 2.7 %collective-permute-start = (bf16[64,2048]{1,0:T(8,128)(2,1)S(1)}, bf16[64,2048]{1,0:T(8,128)(2,1)S(1)}, u32[]{:S(2)}, u32[]{:S(2)}) collective-permute-start(bf16[64,2048]{1,0:T(8,128)(2,1)S(1)} %get-tuple-element.75), channel_id=1, source_target_pairs={{0,8},{4,12},{8,0},{12,4},{1,9},{5,13},{9,1},{13,5},{2,10},{6,14},... | collective-permute-start | bytes 786440 | tf_op jit(solution)/shard_map/spread_tokens/ppermute | solution.py:29
  32.5 13.2 %collective-permute-done.5 = bf16[64,2048]{1,0:T(8,128)(2,1)S(1)} collective-permute-done((bf16[64,2048]{1,0:T(8,128)(2,1)S(1)}, bf16[64,2048]{1,0:T(8,128)(2,1)S(1)}, u32[]{:S(2)}, u32[]{:S(2)}) %collective-permute-start.5) | collective-permute-done | bytes 262176 | tf_op jit(solution)/shard_map/spread_tokens/ppermute | solution.py:29
  45.8 1.8 collective-permute-start.7
  47.8 4.4 %collective-permute-start.11 = (bf16[304,2048]{1,0:T(8,128)(2,1)S(1)}, bf16[304,2048]{1,0:T(8,128)(2,1)S(1)}, u32[]{:S(2)}, u32[]{:S(2)}) collective-permute-start(bf16[304,2048]{1,0:T(8,128)(2,1)S(1)} %maximum_maximum_fusion), channel_id=1, source_target_pairs={{0,4},{4,8},{8,12},{1,5},{5,9},{9,13},{2,6},{6,10},{10,14},{3,7},{... | collective-permute-start | bytes 3735560 | tf_op jit(solution)/shard_map/spread_cotangent/ppermute | solution.py:62
  52.2 1.9 collective-permute-start.12
  54.6 4.0 %collective-permute-done.7 = bf16[2,64,2048]{2,1,0:T(8,128)(2,1)S(1)} collective-permute-done((bf16[2,64,2048]{2,1,0:T(8,128)(2,1)S(1)}, bf16[2,64,2048]{2,1,0:T(8,128)(2,1)S(1)}, u32[]{:S(2)}, u32[]{:S(2)}) %collective-permute-start.7) | collective-permute-done | bytes 524320 | tf_op jit(solution)/shard_map/spread_tokens/ppermute | solution.py:26
  58.8 1.8 fusion.42
  61.1 5.5 %collective-permute-done.1 = bf16[2,64,2048]{2,1,0:T(8,128)(2,1)S(1)} collective-permute-done((bf16[2,64,2048]{2,1,0:T(8,128)(2,1)S(1)}, bf16[2,64,2048]{2,1,0:T(8,128)(2,1)S(1)}, u32[]{:S(2)}, u32[]{:S(2)}) %collective-permute-start.1) | collective-permute-done | bytes 524320 | tf_op jit(solution)/shard_map/spread_tokens/ppermute | solution.py:26
  67.4 1.4 slice-done.5
  68.8 1.4 slice-done.6
  70.1 2.3 %convolution_convert_fusion.4 = bf16[256,2048]{1,0:T(8,128)(2,1)S(1)} fusion(bf16[256,2048]{1,0:T(8,128)(2,1)S(1)} %bitcast.174, bf16[2048,2048]{1,0:T(8,128)(2,1)S(1)} %bitcast.193), kind=kOutput, calls=%fused_computation.8 | convolution fusion | flops 2148007936 | bytes 10485760 | tf_op jit(solution)/shard_map/forward/dot_general | solution.py:140
  72.5 2.3 %convolution_convert_fusion.5 = bf16[256,2048]{1,0:T(8,128)(2,1)S(1)} fusion(bf16[256,2048]{1,0:T(8,128)(2,1)S(1)} %bitcast.175, bf16[2048,2048]{1,0:T(8,128)(2,1)S(1)} %bitcast.193), kind=kOutput, calls=%fused_computation.9 | convolution fusion | flops 2148007936 | bytes 10485760 | tf_op jit(solution)/shard_map/forward/dot_general | solution.py:140
  77.0 1.8 collective-permute-done.12
  78.7 2.7 %collective-permute-start.15 = (bf16[304,2048]{1,0:T(8,128)(2,1)S(1)}, bf16[304,2048]{1,0:T(8,128)(2,1)S(1)}, u32[]{:S(2)}, u32[]{:S(2)}) collective-permute-start(bf16[304,2048]{1,0:T(8,128)(2,1)S(1)} %collective-permute-done.11), channel_id=1, source_target_pairs={{4,8},{8,12},{5,9},{9,13},{6,10},{10,14},{7,11},{11,15},{20,24},{2... | collective-permute-start | bytes 3735560 | tf_op jit(solution)/shard_map/spread_cotangent/ppermute | solution.py:62
  81.4 2.1 %collective-permute-start.16 = (bf16[304,2048]{1,0:T(8,128)(2,1)S(1)}, bf16[304,2048]{1,0:T(8,128)(2,1)S(1)}, u32[]{:S(2)}, u32[]{:S(2)}) collective-permute-start(bf16[304,2048]{1,0:T(8,128)(2,1)S(1)} %collective-permute-done.12), channel_id=1, source_target_pairs={{4,0},{8,4},{5,1},{9,5},{6,2},{10,6},{7,3},{11,7},{20,16},{24,20},... | collective-permute-start | bytes 3735560 | tf_op jit(solution)/shard_map/spread_cotangent/ppermute | solution.py:63
  84.1 2.4 %convolution_add_fusion = f32[256,2048]{1,0:T(8,128)S(1)} fusion(f32[256,2048]{1,0:T(8,128)S(1)} %bitcast.172, bf16[256,2048]{1,0:T(8,128)(2,1)S(1)} %bitcast.187, bf16[2048,2048]{1,0:T(8,128)(2,1)S(1)} %bitcast.193), kind=kOutput, calls=%fused_computation.4 | convolution fusion | flops 2148007936 | bytes 13631488 | tf_op jit(solution)/shard_map/forward/dot_general | solution.py:140
  86.6 8.5 %convolution_convert_fusion = bf16[512,2048]{1,0:T(8,128)(2,1)S(1)} fusion(bf16[2048,2048]{1,0:T(8,128)(2,1)} %param.8, bf16[256,2048]{1,0:T(8,128)(2,1)S(1)} %slice.70, bf16[256,2048]{1,0:T(8,128)(2,1)S(1)} %slice.69), kind=kOutput, calls=%fused_computation.2 | convolution fusion | flops 4300210176 | bytes 12582912 | tf_op jit(solution)/shard_map/forward/dot_general | solution.py:150
  95.2 5.7 %convolution_convert_fusion.3 = bf16[256,2048]{1,0:T(8,128)(2,1)S(1)} fusion(bf16[256,2048]{1,0:T(8,128)(2,1)S(1)} %bitcast.186, bf16[2048,2048]{1,0:T(8,128)(2,1)} %param.8), kind=kOutput, calls=%fused_computation.7 | convolution fusion | flops 2148007936 | bytes 10485760 | tf_op jit(solution)/shard_map/forward/dot_general | solution.py:140
  104.7 4.6 %collective-permute-start.13 = (bf16[256,2048]{1,0:T(8,128)(2,1)S(1)}, bf16[256,2048]{1,0:T(8,128)(2,1)S(1)}, u32[]{:S(2)}, u32[]{:S(2)}) collective-permute-start(bf16[256,2048]{1,0:T(8,128)(2,1)S(1)} %get-tuple-element.35), channel_id=1, source_target_pairs={{0,4},{4,8},{1,5},{5,9},{2,6},{6,10},{3,7},{7,11},{16,20},{20,24},... | collective-permute-start | bytes 3145736 | tf_op jit(solution)/shard_map/forward/ppermute | solution.py:187
  109.3 4.3 %collective-permute-done.16 = bf16[304,2048]{1,0:T(8,128)(2,1)S(1)} collective-permute-done((bf16[304,2048]{1,0:T(8,128)(2,1)S(1)}, bf16[304,2048]{1,0:T(8,128)(2,1)S(1)}, u32[]{:S(2)}, u32[]{:S(2)}) %collective-permute-start.16) | collective-permute-done | bytes 1245216 | tf_op jit(solution)/shard_map/spread_cotangent/ppermute | solution.py:63
  115.9 7.2 %convolution_convert_fusion.2 = bf16[256,2048]{1,0:T(8,128)(2,1)} fusion(bf16[2048,2048]{1,0:T(8,128)(2,1)} %param.8, bf16[304,2048]{1,0:T(8,128)(2,1)S(1)} %broadcast_select_fusion), kind=kOutput, calls=%fused_computation.6 | convolution fusion | flops 2148007936 | bytes 10485760 | tf_op jit(solution)/shard_map/forward/dot_general | solution.py:150
  123.3 1.5 collective-permute-start.20
  124.7 9.2 %collective-permute-done.14 = bf16[256,2048]{1,0:T(8,128)(2,1)S(1)} collective-permute-done((bf16[256,2048]{1,0:T(8,128)(2,1)S(1)}, bf16[256,2048]{1,0:T(8,128)(2,1)S(1)}, u32[]{:S(2)}, u32[]{:S(2)}) %collective-permute-start.14) | collective-permute-done | bytes 1048608 | tf_op jit(solution)/shard_map/forward/ppermute | solution.py:188
  135.7 1.9 collective-permute-start.17
  137.6 4.2 %collective-permute-start.18 = (bf16[256,2048]{1,0:T(8,128)(2,1)S(1)}, bf16[256,2048]{1,0:T(8,128)(2,1)S(1)}, u32[]{:S(2)}, u32[]{:S(2)}) collective-permute-start(bf16[256,2048]{1,0:T(8,128)(2,1)S(1)} %add.285), channel_id=1, source_target_pairs={{4,0},{8,4},{12,8},{5,1},{9,5},{13,9},{6,2},{10,6},{14,10},{7,3},{... | collective-permute-start | bytes 3145736 | tf_op jit(solution)/shard_map/forward/ppermute | solution.py:188
  142.1 6.2 %convolution_convert_fusion.1 = bf16[256,2048]{1,0:T(8,128)(2,1)S(1)} fusion(bf16[2048,2048]{1,0:T(8,128)(2,1)} %param.8, bf16[304,2048]{1,0:T(8,128)(2,1)S(1)} %select_select_fusion), kind=kOutput, calls=%fused_computation.5 | convolution fusion | flops 2148007936 | bytes 10485760 | tf_op jit(solution)/shard_map/backward/dot_general | solution.py:150
  148.5 1.8 collective-permute-start.22
  150.4 6.9 %collective-permute-done.22 = bf16[1,1,64,2048]{3,2,1,0:T(8,128)(2,1)S(1)} collective-permute-done((bf16[1,1,64,2048]{3,2,1,0:T(8,128)(2,1)S(1)}, bf16[1,1,64,2048]{3,2,1,0:T(8,128)(2,1)S(1)}, u32[]{:S(2)}, u32[]{:S(2)}) %collective-permute-start.22) | collective-permute-done | bytes 262176 | tf_op jit(solution)/shard_map/backward/ppermute | solution.py:26
  157.4 1.8 collective-permute-start.26
  159.2 3.9 %collective-permute-done.17 = bf16[256,2048]{1,0:T(8,128)(2,1)S(1)} collective-permute-done((bf16[256,2048]{1,0:T(8,128)(2,1)S(1)}, bf16[256,2048]{1,0:T(8,128)(2,1)S(1)}, u32[]{:S(2)}, u32[]{:S(2)}) %collective-permute-start.17) | collective-permute-done | bytes 1048608 | tf_op jit(solution)/shard_map/forward/ppermute | solution.py:187
  163.1 1.9 collective-permute-done.18
  165.1 1.4 add_convert_fusion.1
  173.6 2.4 %collective-permute-start.27 = (bf16[64,2048]{1,0:T(8,128)(2,1)S(1)}, bf16[64,2048]{1,0:T(8,128)(2,1)S(1)}, u32[]{:S(2)}, u32[]{:S(2)}) collective-permute-start(bf16[64,2048]{1,0:T(8,128)(2,1)S(1)} %get-tuple-element.67), channel_id=1, source_target_pairs={{0,0},{1,4},{2,8},{3,12},{4,5},{5,9},{6,13},{7,1},{8,10},{9,14},{1... | collective-permute-start | bytes 786440 | tf_op jit(solution)/shard_map/backward/ppermute | solution.py:219
  176.0 4.3 %collective-permute-start.28 = (bf16[64,2048]{1,0:T(8,128)(2,1)S(1)}, bf16[64,2048]{1,0:T(8,128)(2,1)S(1)}, u32[]{:S(2)}, u32[]{:S(2)}) collective-permute-start(bf16[64,2048]{1,0:T(8,128)(2,1)S(1)} %get-tuple-element.64), channel_id=1, source_target_pairs={{0,4},{1,8},{2,12},{3,0},{4,9},{5,13},{6,1},{7,5},{8,14},{9,2},{10... | collective-permute-start | bytes 786440 | tf_op jit(solution)/shard_map/backward/ppermute | solution.py:219
  180.3 3.1 %collective-permute-start.29 = (bf16[64,2048]{1,0:T(8,128)(2,1)S(1)}, bf16[64,2048]{1,0:T(8,128)(2,1)S(1)}, u32[]{:S(2)}, u32[]{:S(2)}) collective-permute-start(bf16[64,2048]{1,0:T(8,128)(2,1)S(1)} %get-tuple-element.66), channel_id=1, source_target_pairs={{0,8},{1,12},{2,0},{3,4},{4,13},{5,1},{6,5},{7,9},{8,2},{9,6},{10,... | collective-permute-start | bytes 786440 | tf_op jit(solution)/shard_map/backward/ppermute | solution.py:219
  183.4 3.4 %collective-permute-start.30 = (bf16[64,2048]{1,0:T(8,128)(2,1)S(1)}, bf16[64,2048]{1,0:T(8,128)(2,1)S(1)}, u32[]{:S(2)}, u32[]{:S(2)}) collective-permute-start(bf16[64,2048]{1,0:T(8,128)(2,1)S(1)} %get-tuple-element.65), channel_id=1, source_target_pairs={{0,12},{1,0},{2,4},{3,8},{4,1},{5,5},{6,9},{7,13},{8,6},{9,10},{10... | collective-permute-start | bytes 786440 | tf_op jit(solution)/shard_map/backward/ppermute | solution.py:219
  186.8 2.7 %fusion.21 = f32[32,16,2048]{2,1,0:T(8,128)} fusion(bf16[128,2048,1]{1,0,2:T(8,128)(2,1)S(1)} %bitcast.171, s32[128]{0:T(128)S(1)} %iota.42, s32[128]{0:T(128)S(1)} %eq.208), kind=kOutput, calls=%fused_computation.89 | convolution fusion | flops 268632064 | bytes 4719616 | tf_op jit(solution)/shard_map/tables/dot_general | solution.py:253
  189.6 2.7 %fusion.23 = f32[32,16,2048]{2,1,0:T(8,128)} fusion(bf16[128,2048,1]{1,0,2:T(8,128)(2,1)S(1)} %bitcast.170, s32[128]{0:T(128)S(1)} %iota.42, s32[128]{0:T(128)S(1)} %eq.208), kind=kOutput, calls=%fused_computation.90 | convolution fusion | flops 268632064 | bytes 4719616 | tf_op jit(solution)/shard_map/tables/dot_general | solution.py:253
  192.3 2.4 %collective-permute-done.27 = bf16[64,2048]{1,0:T(8,128)(2,1)S(1)} collective-permute-done((bf16[64,2048]{1,0:T(8,128)(2,1)S(1)}, bf16[64,2048]{1,0:T(8,128)(2,1)S(1)}, u32[]{:S(2)}, u32[]{:S(2)}) %collective-permute-start.27) | collective-permute-done | bytes 262176 | tf_op jit(solution)/shard_map/backward/ppermute | solution.py:219
  194.7 6.2 %collective-permute-done.28 = bf16[64,2048]{1,0:T(8,128)(2,1)S(1)} collective-permute-done((bf16[64,2048]{1,0:T(8,128)(2,1)S(1)}, bf16[64,2048]{1,0:T(8,128)(2,1)S(1)}, u32[]{:S(2)}, u32[]{:S(2)}) %collective-permute-start.28) | collective-permute-done | bytes 262176 | tf_op jit(solution)/shard_map/backward/ppermute | solution.py:219
  200.9 1.4 collective-permute-done.29
  (156 shorter events, 26.6 us)
Async XLA Ops:
  0.6 1.6 copy-start
  2.8 5.6 %copy-start.10 = (bf16[2,16,2048]{2,1,0:T(8,128)(2,1)}, bf16[2,16,2048]{2,1,0:T(8,128)(2,1)S(1)}, u32[]{:S(2)}) copy-start(bf16[2,16,2048]{2,1,0:T(8,128)(2,1)S(1)} %gather_fusion.1) | copy-start | bytes 393220
  6.6 6.0 %copy-start.7 = (bf16[256,2048]{1,0:T(8,128)(2,1)S(1)}, bf16[256,2048]{1,0:T(8,128)(2,1)}, u32[]{:S(2)}) copy-start(bf16[256,2048]{1,0:T(8,128)(2,1)} %param.11) | copy-start | bytes 3145732
  8.4 4.1 %collective-permute-start.3 = (f32[2,2,16,128]{3,2,1,0:T(8,128)S(1)}, f32[2,2,16,128]{3,2,1,0:T(8,128)S(1)}, u32[]{:S(2)}, u32[]{:S(2)}) collective-permute-start(f32[2,2,16,128]{3,2,1,0:T(8,128)S(1)} %pad_maximum_fusion.11), channel_id=1, source_target_pairs={{0,1},{1,0},{2,3},{3,2},{4,5},{5,4},{6,7},{7,6},{8,9},{9,8},{10,11... | collective-permute-start | bytes 98312 | tf_op jit(solution)/shard_map/ranks/ppermute | solution.py:26
  8.5 17.6 %all-to-all-start = ((bf16[4,64,2048]{2,1,0:T(8,128)(2,1)}), bf16[4,64,2048]{2,1,0:T(8,128)(2,1)S(1)}, u32[]{:S(2)}, u32[]{:S(2)}) async-start(bf16[4,64,2048]{2,1,0:T(8,128)(2,1)} %bitcast), calls=%async_computation | async-start | bytes 2097152 | tf_op jit(solution)/shard_map/spread_tokens/all_to_all | solution.py:67
  12.5 13.5 %collective-permute-start.4 = (f32[2,2,16,128]{3,2,1,0:T(8,128)S(1)}, f32[2,2,16,128]{3,2,1,0:T(8,128)S(1)}, u32[]{:S(2)}, u32[]{:S(2)}) collective-permute-start(f32[2,2,16,128]{3,2,1,0:T(8,128)S(1)} %fusion.47), channel_id=1, source_target_pairs={{0,2},{1,3},{2,0},{3,1},{4,6},{5,7},{6,4},{7,5},{8,10},{9,11},{10,... | collective-permute-start | bytes 98312 | tf_op jit(solution)/shard_map/ranks/ppermute | solution.py:26
  26.1 19.6 %collective-permute-start.5 = (bf16[64,2048]{1,0:T(8,128)(2,1)S(1)}, bf16[64,2048]{1,0:T(8,128)(2,1)S(1)}, u32[]{:S(2)}, u32[]{:S(2)}) collective-permute-start(bf16[64,2048]{1,0:T(8,128)(2,1)S(1)} %get-tuple-element.74), channel_id=1, source_target_pairs={{0,4},{4,8},{8,12},{12,0},{1,5},{5,9},{9,13},{13,1},{2,6},{6,10},{... | collective-permute-start | bytes 786440 | tf_op jit(solution)/shard_map/spread_tokens/ppermute | solution.py:29
  27.8 17.9 %collective-permute-start.6 = (bf16[64,2048]{1,0:T(8,128)(2,1)S(1)}, bf16[64,2048]{1,0:T(8,128)(2,1)S(1)}, u32[]{:S(2)}, u32[]{:S(2)}) collective-permute-start(bf16[64,2048]{1,0:T(8,128)(2,1)S(1)} %get-tuple-element.73), channel_id=1, source_target_pairs={{0,12},{4,0},{8,4},{12,8},{1,13},{5,1},{9,5},{13,9},{2,14},{6,2},{... | collective-permute-start | bytes 786440 | tf_op jit(solution)/shard_map/spread_tokens/ppermute | solution.py:29
  29.9 24.2 %collective-permute-start = (bf16[64,2048]{1,0:T(8,128)(2,1)S(1)}, bf16[64,2048]{1,0:T(8,128)(2,1)S(1)}, u32[]{:S(2)}, u32[]{:S(2)}) collective-permute-start(bf16[64,2048]{1,0:T(8,128)(2,1)S(1)} %get-tuple-element.75), channel_id=1, source_target_pairs={{0,8},{4,12},{8,0},{12,4},{1,9},{5,13},{9,1},{13,5},{2,10},{6,14},... | collective-permute-start | bytes 786440 | tf_op jit(solution)/shard_map/spread_tokens/ppermute | solution.py:29
  45.8 12.8 %collective-permute-start.7 = (bf16[2,64,2048]{2,1,0:T(8,128)(2,1)S(1)}, bf16[2,64,2048]{2,1,0:T(8,128)(2,1)S(1)}, u32[]{:S(2)}, u32[]{:S(2)}) collective-permute-start(bf16[2,64,2048]{2,1,0:T(8,128)(2,1)S(1)} %pad_maximum_fusion.7), channel_id=1, source_target_pairs={{0,2},{1,3},{2,0},{3,1},{4,6},{5,7},{6,4},{7,5},{8,10},{9,11},{10,... | collective-permute-start | bytes 1572872 | tf_op jit(solution)/shard_map/spread_tokens/ppermute | solution.py:26
  47.8 29.2 %collective-permute-start.11 = (bf16[304,2048]{1,0:T(8,128)(2,1)S(1)}, bf16[304,2048]{1,0:T(8,128)(2,1)S(1)}, u32[]{:S(2)}, u32[]{:S(2)}) collective-permute-start(bf16[304,2048]{1,0:T(8,128)(2,1)S(1)} %maximum_maximum_fusion), channel_id=1, source_target_pairs={{0,4},{4,8},{8,12},{1,5},{5,9},{9,13},{2,6},{6,10},{10,14},{3,7},{... | collective-permute-start | bytes 3735560 | tf_op jit(solution)/shard_map/spread_cotangent/ppermute | solution.py:62
  52.2 26.5 %collective-permute-start.12 = (bf16[304,2048]{1,0:T(8,128)(2,1)S(1)}, bf16[304,2048]{1,0:T(8,128)(2,1)S(1)}, u32[]{:S(2)}, u32[]{:S(2)}) collective-permute-start(bf16[304,2048]{1,0:T(8,128)(2,1)S(1)} %maximum_maximum_fusion), channel_id=1, source_target_pairs={{4,0},{8,4},{12,8},{5,1},{9,5},{13,9},{6,2},{10,6},{14,10},{7,3},{... | collective-permute-start | bytes 3735560 | tf_op jit(solution)/shard_map/spread_cotangent/ppermute | solution.py:63
  54.2 12.4 %collective-permute-start.1 = (bf16[2,64,2048]{2,1,0:T(8,128)(2,1)S(1)}, bf16[2,64,2048]{2,1,0:T(8,128)(2,1)S(1)}, u32[]{:S(2)}, u32[]{:S(2)}) collective-permute-start(bf16[2,64,2048]{2,1,0:T(8,128)(2,1)S(1)} %pad_maximum_fusion.6), channel_id=1, source_target_pairs={{0,2},{1,3},{2,0},{3,1},{4,6},{5,7},{6,4},{7,5},{8,10},{9,11},{10,... | collective-permute-start | bytes 1572872 | tf_op jit(solution)/shard_map/spread_tokens/ppermute | solution.py:26
  58.6 2.0 copy-start.11
  58.7 8.1 %collective-permute-start.8 = (bf16[2,2,64,2048]{3,2,0,1:T(8,128)(2,1)S(1)}, bf16[2,2,64,2048]{3,2,0,1:T(8,128)(2,1)S(1)}, u32[]{:S(2)}, u32[]{:S(2)}) collective-permute-start(bf16[2,2,64,2048]{3,2,0,1:T(8,128)(2,1)S(1)} %pad_maximum_fusion.3), channel_id=1, source_target_pairs={{0,1},{1,0},{2,3},{3,2},{4,5},{5,4},{6,7},{7,6},{8,9},{9,8},{10,11... | collective-permute-start | bytes 3145736 | tf_op jit(solution)/shard_map/spread_tokens/ppermute | solution.py:26
  66.6 2.2 %slice-start.5 = ((s8[8388608]{0:T(1024)(128)(4,1)}), s8[4194304]{0:T(1024)(128)(4,1)S(1)}, s32[]{:S(2)}) async-start(s8[8388608]{0:T(1024)(128)(4,1)} %bitcast.192), calls=%async_computation.6 | async-start | bytes 8388608
  66.8 16.9 %collective-permute-start.2 = (bf16[2,2,64,2048]{3,2,1,0:T(8,128)(2,1)S(1)}, bf16[2,2,64,2048]{3,2,1,0:T(8,128)(2,1)S(1)}, u32[]{:S(2)}, u32[]{:S(2)}) collective-permute-start(bf16[2,2,64,2048]{3,2,1,0:T(8,128)(2,1)S(1)} %pad_maximum_fusion.2), channel_id=1, source_target_pairs={{0,1},{1,0},{2,3},{3,2},{4,5},{5,4},{6,7},{7,6},{8,9},{9,8},{10,11... | collective-permute-start | bytes 3145736 | tf_op jit(solution)/shard_map/spread_tokens/ppermute | solution.py:26
  67.0 3.1 %slice-start.6 = ((s8[8388608]{0:T(1024)(128)(4,1)}), s8[4194304]{0:T(1024)(128)(4,1)S(1)}, s32[]{:S(2)}) async-start(s8[8388608]{0:T(1024)(128)(4,1)} %bitcast.192), calls=%async_computation.7 | async-start | bytes 8388608
  74.8 26.0 %collective-permute-start.10 = (bf16[256,2048]{1,0:T(8,128)(2,1)S(1)}, bf16[256,2048]{1,0:T(8,128)(2,1)S(1)}, u32[]{:S(2)}, u32[]{:S(2)}) collective-permute-start(bf16[256,2048]{1,0:T(8,128)(2,1)S(1)} %convolution_convert_fusion.4), channel_id=1, source_target_pairs={{12,8},{13,9},{14,10},{15,11},{28,24},{29,25},{30,26},{31,27}} | collective-permute-start | bytes 3145736 | tf_op jit(solution)/shard_map/forward/ppermute | solution.py:188
  75.6 26.5 %collective-permute-start.9 = (bf16[256,2048]{1,0:T(8,128)(2,1)S(1)}, bf16[256,2048]{1,0:T(8,128)(2,1)S(1)}, u32[]{:S(2)}, u32[]{:S(2)}) collective-permute-start(bf16[256,2048]{1,0:T(8,128)(2,1)S(1)} %convolution_convert_fusion.5), channel_id=1, source_target_pairs={{0,4},{1,5},{2,6},{3,7},{16,20},{17,21},{18,22},{19,23}} | collective-permute-start | bytes 3145736 | tf_op jit(solution)/shard_map/forward/ppermute | solution.py:187
  78.7 30.6 %collective-permute-start.15 = (bf16[304,2048]{1,0:T(8,128)(2,1)S(1)}, bf16[304,2048]{1,0:T(8,128)(2,1)S(1)}, u32[]{:S(2)}, u32[]{:S(2)}) collective-permute-start(bf16[304,2048]{1,0:T(8,128)(2,1)S(1)} %collective-permute-done.11), channel_id=1, source_target_pairs={{4,8},{8,12},{5,9},{9,13},{6,10},{10,14},{7,11},{11,15},{20,24},{2... | collective-permute-start | bytes 3735560 | tf_op jit(solution)/shard_map/spread_cotangent/ppermute | solution.py:62
  81.4 32.2 %collective-permute-start.16 = (bf16[304,2048]{1,0:T(8,128)(2,1)S(1)}, bf16[304,2048]{1,0:T(8,128)(2,1)S(1)}, u32[]{:S(2)}, u32[]{:S(2)}) collective-permute-start(bf16[304,2048]{1,0:T(8,128)(2,1)S(1)} %collective-permute-done.12), channel_id=1, source_target_pairs={{4,0},{8,4},{5,1},{9,5},{6,2},{10,6},{7,3},{11,7},{20,16},{24,20},... | collective-permute-start | bytes 3735560 | tf_op jit(solution)/shard_map/spread_cotangent/ppermute | solution.py:63
  83.7 84.7 %copy-start.2 = (bf16[304,2048]{1,0:T(8,128)(2,1)}, bf16[304,2048]{1,0:T(8,128)(2,1)S(1)}, u32[]{:S(2)}) copy-start(bf16[304,2048]{1,0:T(8,128)(2,1)S(1)} %broadcast_select_fusion.1) | copy-start | bytes 3735556
  103.5 19.6 %collective-permute-start.19 = (bf16[2,2,64,2048]{3,2,0,1:T(8,128)(2,1)}, bf16[2,2,64,2048]{3,2,0,1:T(8,128)(2,1)S(1)}, u32[]{:S(2)}, u32[]{:S(2)}) collective-permute-start(bf16[2,2,64,2048]{3,2,0,1:T(8,128)(2,1)} %bitcast.163), channel_id=1, source_target_pairs={{0,1},{1,0},{2,3},{3,2},{4,5},{5,4},{6,7},{7,6},{8,9},{9,8},{10,11... | collective-permute-start | bytes 3145736 | tf_op jit(solution)/shard_map/forward/ppermute | solution.py:26
  103.5 30.5 %collective-permute-start.14 = (bf16[256,2048]{1,0:T(8,128)(2,1)S(1)}, bf16[256,2048]{1,0:T(8,128)(2,1)S(1)}, u32[]{:S(2)}, u32[]{:S(2)}) collective-permute-start(bf16[256,2048]{1,0:T(8,128)(2,1)S(1)} %get-tuple-element.36), channel_id=1, source_target_pairs={{8,4},{12,8},{9,5},{13,9},{10,6},{14,10},{11,7},{15,11},{24,20},{2... | collective-permute-start | bytes 3145736 | tf_op jit(solution)/shard_map/forward/ppermute | solution.py:188
  104.7 29.6 %collective-permute-start.13 = (bf16[256,2048]{1,0:T(8,128)(2,1)S(1)}, bf16[256,2048]{1,0:T(8,128)(2,1)S(1)}, u32[]{:S(2)}, u32[]{:S(2)}) collective-permute-start(bf16[256,2048]{1,0:T(8,128)(2,1)S(1)} %get-tuple-element.35), channel_id=1, source_target_pairs={{0,4},{4,8},{1,5},{5,9},{2,6},{6,10},{3,7},{7,11},{16,20},{20,24},... | collective-permute-start | bytes 3145736 | tf_op jit(solution)/shard_map/forward/ppermute | solution.py:187
  113.7 24.0 %collective-permute-start.23 = (bf16[304,2048]{1,0:T(8,128)(2,1)S(1)}, bf16[304,2048]{1,0:T(8,128)(2,1)S(1)}, u32[]{:S(2)}, u32[]{:S(2)}) collective-permute-start(bf16[304,2048]{1,0:T(8,128)(2,1)S(1)} %collective-permute-done.15), channel_id=1, source_target_pairs={{8,12},{9,13},{10,14},{11,15},{24,28},{25,29},{26,30},{27,31}} | collective-permute-start | bytes 3735560 | tf_op jit(solution)/shard_map/spread_cotangent/ppermute | solution.py:62
  114.4 27.4 %collective-permute-start.24 = (bf16[304,2048]{1,0:T(8,128)(2,1)S(1)}, bf16[304,2048]{1,0:T(8,128)(2,1)S(1)}, u32[]{:S(2)}, u32[]{:S(2)}) collective-permute-start(bf16[304,2048]{1,0:T(8,128)(2,1)S(1)} %collective-permute-done.16), channel_id=1, source_target_pairs={{4,0},{5,1},{6,2},{7,3},{20,16},{21,17},{22,18},{23,19}} | collective-permute-start | bytes 3735560 | tf_op jit(solution)/shard_map/spread_cotangent/ppermute | solution.py:63
  115.9 52.5 %copy-start.4 = (bf16[304,2048]{1,0:T(8,128)(2,1)}, bf16[304,2048]{1,0:T(8,128)(2,1)S(1)}, u32[]{:S(2)}) copy-start(bf16[304,2048]{1,0:T(8,128)(2,1)S(1)} %broadcast_select_fusion) | copy-start | bytes 3735556
  123.3 27.0 %collective-permute-start.20 = (bf16[2,1,64,2048]{3,2,0,1:T(8,128)(2,1)S(1)}, bf16[2,1,64,2048]{3,2,0,1:T(8,128)(2,1)S(1)}, u32[]{:S(2)}, u32[]{:S(2)}) collective-permute-start(bf16[2,1,64,2048]{3,2,0,1:T(8,128)(2,1)S(1)} %constant_dynamic-slice_fusion.6), channel_id=1, source_target_pairs={{0,2},{1,3},{2,0},{3,1},{4,6},{5,7},{6,4},{7,5},{8,10},{9,11},{10,... | collective-permute-start | bytes 1572872 | tf_op jit(solution)/shard_map/forward/ppermute | solution.py:26
  134.3 1.2 copy-start.8
  135.6 12.8 %collective-permute-start.21 = (bf16[1,2,64,2048]{3,2,1,0:T(8,128)(2,1)S(1)}, bf16[1,2,64,2048]{3,2,1,0:T(8,128)(2,1)S(1)}, u32[]{:S(2)}, u32[]{:S(2)}) collective-permute-start(bf16[1,2,64,2048]{3,2,1,0:T(8,128)(2,1)S(1)} %dynamic-slice_bitcast_fusion.1), channel_id=1, source_target_pairs={{0,1},{1,0},{2,3},{3,2},{4,5},{5,4},{6,7},{7,6},{8,9},{9,8},{10,11... | collective-permute-start | bytes 1572872 | tf_op jit(solution)/shard_map/backward/ppermute | solution.py:26
  135.7 27.4 %collective-permute-start.17 = (bf16[256,2048]{1,0:T(8,128)(2,1)S(1)}, bf16[256,2048]{1,0:T(8,128)(2,1)S(1)}, u32[]{:S(2)}, u32[]{:S(2)}) collective-permute-start(bf16[256,2048]{1,0:T(8,128)(2,1)S(1)} %add.284), channel_id=1, source_target_pairs={{0,4},{4,8},{8,12},{1,5},{5,9},{9,13},{2,6},{6,10},{10,14},{3,7},{... | collective-permute-start | bytes 3145736 | tf_op jit(solution)/shard_map/forward/ppermute | solution.py:187
  137.6 27.4 %collective-permute-start.18 = (bf16[256,2048]{1,0:T(8,128)(2,1)S(1)}, bf16[256,2048]{1,0:T(8,128)(2,1)S(1)}, u32[]{:S(2)}, u32[]{:S(2)}) collective-permute-start(bf16[256,2048]{1,0:T(8,128)(2,1)S(1)} %add.285), channel_id=1, source_target_pairs={{4,0},{8,4},{12,8},{5,1},{9,5},{13,9},{6,2},{10,6},{14,10},{7,3},{... | collective-permute-start | bytes 3145736 | tf_op jit(solution)/shard_map/forward/ppermute | solution.py:188
  142.1 26.4 %copy-start.5 = (bf16[304,2048]{1,0:T(8,128)(2,1)}, bf16[304,2048]{1,0:T(8,128)(2,1)S(1)}, u32[]{:S(2)}) copy-start(bf16[304,2048]{1,0:T(8,128)(2,1)S(1)} %select_select_fusion) | copy-start | bytes 3735556
  148.3 9.0 %collective-permute-start.25 = (bf16[1,2,64,2048]{3,2,1,0:T(8,128)(2,1)S(1)}, bf16[1,2,64,2048]{3,2,1,0:T(8,128)(2,1)S(1)}, u32[]{:S(2)}, u32[]{:S(2)}) collective-permute-start(bf16[1,2,64,2048]{3,2,1,0:T(8,128)(2,1)S(1)} %dynamic-slice_bitcast_fusion), channel_id=1, source_target_pairs={{0,1},{1,0},{2,3},{3,2},{4,5},{5,4},{6,7},{7,6},{8,9},{9,8},{10,11... | collective-permute-start | bytes 1572872 | tf_op jit(solution)/shard_map/backward/ppermute | solution.py:26
  148.5 8.8 %collective-permute-start.22 = (bf16[1,1,64,2048]{3,2,1,0:T(8,128)(2,1)S(1)}, bf16[1,1,64,2048]{3,2,1,0:T(8,128)(2,1)S(1)}, u32[]{:S(2)}, u32[]{:S(2)}) collective-permute-start(bf16[1,1,64,2048]{3,2,1,0:T(8,128)(2,1)S(1)} %constant_dynamic-slice_fusion.5), channel_id=1, source_target_pairs={{0,2},{1,3},{2,0},{3,1},{4,6},{5,7},{6,4},{7,5},{8,10},{9,11},{10,... | collective-permute-start | bytes 786440 | tf_op jit(solution)/shard_map/backward/ppermute | solution.py:26
  157.4 9.1 %collective-permute-start.26 = (bf16[1,1,64,2048]{3,2,1,0:T(8,128)(2,1)S(1)}, bf16[1,1,64,2048]{3,2,1,0:T(8,128)(2,1)S(1)}, u32[]{:S(2)}, u32[]{:S(2)}) collective-permute-start(bf16[1,1,64,2048]{3,2,1,0:T(8,128)(2,1)S(1)} %constant_dynamic-slice_fusion.4), channel_id=1, source_target_pairs={{0,2},{1,3},{2,0},{3,1},{4,6},{5,7},{6,4},{7,5},{8,10},{9,11},{10,... | collective-permute-start | bytes 786440 | tf_op jit(solution)/shard_map/backward/ppermute | solution.py:26
  169.7 1.5 slice-start.3
  170.0 1.5 copy-start.6
  170.4 1.4 slice-start.1
  171.2 1.3 slice-start.4
  173.6 21.1 %collective-permute-start.27 = (bf16[64,2048]{1,0:T(8,128)(2,1)S(1)}, bf16[64,2048]{1,0:T(8,128)(2,1)S(1)}, u32[]{:S(2)}, u32[]{:S(2)}) collective-permute-start(bf16[64,2048]{1,0:T(8,128)(2,1)S(1)} %get-tuple-element.67), channel_id=1, source_target_pairs={{0,0},{1,4},{2,8},{3,12},{4,5},{5,9},{6,13},{7,1},{8,10},{9,14},{1... | collective-permute-start | bytes 786440 | tf_op jit(solution)/shard_map/backward/ppermute | solution.py:219
  176.0 24.9 %collective-permute-start.28 = (bf16[64,2048]{1,0:T(8,128)(2,1)S(1)}, bf16[64,2048]{1,0:T(8,128)(2,1)S(1)}, u32[]{:S(2)}, u32[]{:S(2)}) collective-permute-start(bf16[64,2048]{1,0:T(8,128)(2,1)S(1)} %get-tuple-element.64), channel_id=1, source_target_pairs={{0,4},{1,8},{2,12},{3,0},{4,9},{5,13},{6,1},{7,5},{8,14},{9,2},{10... | collective-permute-start | bytes 786440 | tf_op jit(solution)/shard_map/backward/ppermute | solution.py:219
  180.3 22.0 %collective-permute-start.29 = (bf16[64,2048]{1,0:T(8,128)(2,1)S(1)}, bf16[64,2048]{1,0:T(8,128)(2,1)S(1)}, u32[]{:S(2)}, u32[]{:S(2)}) collective-permute-start(bf16[64,2048]{1,0:T(8,128)(2,1)S(1)} %get-tuple-element.66), channel_id=1, source_target_pairs={{0,8},{1,12},{2,0},{3,4},{4,13},{5,1},{6,5},{7,9},{8,2},{9,6},{10,... | collective-permute-start | bytes 786440 | tf_op jit(solution)/shard_map/backward/ppermute | solution.py:219
  183.4 19.7 %collective-permute-start.30 = (bf16[64,2048]{1,0:T(8,128)(2,1)S(1)}, bf16[64,2048]{1,0:T(8,128)(2,1)S(1)}, u32[]{:S(2)}, u32[]{:S(2)}) collective-permute-start(bf16[64,2048]{1,0:T(8,128)(2,1)S(1)} %get-tuple-element.65), channel_id=1, source_target_pairs={{0,12},{1,0},{2,4},{3,8},{4,1},{5,5},{6,9},{7,13},{8,6},{9,10},{10... | collective-permute-start | bytes 786440 | tf_op jit(solution)/shard_map/backward/ppermute | solution.py:219
  192.3 10.9 %copy-start.3 = (f32[2,128,2048]{2,1,0:T(8,128)S(1)}, f32[2,128,2048]{2,1,0:T(8,128)}, u32[]{:S(2)}) copy-start(f32[2,128,2048]{2,1,0:T(8,128)} %fusion.42) | copy-start | bytes 6291460
  203.2 2.0 copy-start.1
  (3 other events, 3.0 us)

commit v6 on v5

--- a/solution.py
+++ b/solution.py
@@ -144,7 +144,7 @@
             for r in rest:
                 if r != 0:
                     (parts[r],) = after((project(r).astype(BF16),), *near_parts)
-            (own,) = after((project(0) + adapter_output,), *near_parts)
+            (own,) = after((project(0) + adapter_output,), *near_parts, *parts.values())
 
         def pull_back(batch):
             return lax.dot_general(

time: 206 us -> 206 us (level)
  matrix products: 48.2 us -> 44.8 us
  waiting for transfers between devices: 75.3 us -> 78.6 us
    ppermute x3, waiting for transfers between devices: 5.1 us -> 8.47 us  [local(): up_sum = lax.ppermute(sends[0], 'dp', [(a, a + 1) for a in range(s)])]
    dot_general x4, matrix products: 12.8 us -> 9.42 us  [project(): return jnp.dot(full[r], query_weight, preferred_element_type=F32)]
  transfers between devices with their start and end apart: 32 -> 32, of which waited for: 16 -> 16; matrix products, arithmetic and copies ran while one was open for 25% -> 23% of each run, Pallas kernels for 0% -> 0%
where the time goes in v6:
time: 206 us; the launch traced here: 205 us
  waiting for transfers between devices  78.6 us (38%)
  starting transfers between devices  56.7 us (28%)
  matrix products  44.8 us (22%)
  local copies, waits for them, and re-layouts  14 us (7%)
  other arithmetic  8.92 us (4%)
  between operations  2.08 us (1%)
    ppermute x12, waiting for transfers between devices, swap(): return lax.ppermute(x, 'tensor', [(t, t ^ mask) for t in range(n)])  28.9 us
    dot_general x3, matrix products, pull_back(): lax.dot_general(jnp.concatenate([value[:rows] for value in batch]), query...  21.9 us
    ppermute x4, starting transfers between devices, local(): lax.ppermute(pick(sums, slot((t + m) % n)), ('dp', 'tensor'), [(a * n + b...  13.2 us
    ppermute x3, waiting for transfers between devices, rotate(): return lax.ppermute(x, 'dp', [(i, (i + k) % n) for i in range(n)])  13.2 us
    ppermute x3, waiting for transfers between devices, local(): down_sum = lax.ppermute(sends[1], 'dp', [(a, a - 1) for a in range(d, n)])  11.1 us
    ppermute x4, waiting for transfers between devices, local(): lax.ppermute(pick(sums, slot((t + m) % n)), ('dp', 'tensor'), [(a * n + b...  10.8 us
    dot_general x4, matrix products, project(): return jnp.dot(full[r], query_weight, preferred_element_type=F32)  9.42 us
    ppermute x3, waiting for transfers between devices, local(): up_sum = lax.ppermute(sends[0], 'dp', [(a, a + 1) for a in range(s)])  8.47 us
  transfers between devices with their start and end apart: 32, of which 16 were waited for; matrix products, arithmetic and copies ran while one was open for 23% of the time, Pallas kernels for 0%

profile of v6, /device:TPU:10, one launch (start us, length us, event | category | flops | bytes accessed | tf_op | source)
XLA Modules:
  0.0 205.1 jit_solution(14183152779681808698)
XLA Ops:
  2.8 2.2 %gather_fusion = bf16[2,16,2048]{2,1,0:T(8,128)(2,1)S(1)} fusion(bf16[32,16,2048]{2,1,0:T(8,128)(2,1)} %param.9, s32[1024]{0:T(1024)S(1)} %pad_clamp_fusion), kind=kCustom, calls=%fused_computation | custom fusion | bytes 262152 | tf_op jit(solution)/shard_map/ranks/gather | solution.py:73
  5.0 1.6 convolution_bitcast_fusion
  6.6 1.8 fusion.11
  8.5 4.0 %all-to-all-start = ((bf16[4,64,2048]{2,1,0:T(8,128)(2,1)}), bf16[4,64,2048]{2,1,0:T(8,128)(2,1)S(1)}, u32[]{:S(2)}, u32[]{:S(2)}) async-start(bf16[4,64,2048]{2,1,0:T(8,128)(2,1)} %bitcast), calls=%async_computation | async-start | bytes 2097152 | tf_op jit(solution)/shard_map/spread_tokens/all_to_all | solution.py:67
  13.5 12.5 %collective-permute-done.4 = f32[2,2,16,128]{3,2,1,0:T(8,128)S(1)} collective-permute-done((f32[2,2,16,128]{3,2,1,0:T(8,128)S(1)}, f32[2,2,16,128]{3,2,1,0:T(8,128)S(1)}, u32[]{:S(2)}, u32[]{:S(2)}) %collective-permute-start.4) | collective-permute-done | bytes 32800 | tf_op jit(solution)/shard_map/ranks/ppermute | solution.py:26
  26.1 1.6 collective-permute-start.5
  28.2 1.5 convolution_convert_fusion.6
  29.9 2.7 %collective-permute-start = (bf16[64,2048]{1,0:T(8,128)(2,1)S(1)}, bf16[64,2048]{1,0:T(8,128)(2,1)S(1)}, u32[]{:S(2)}, u32[]{:S(2)}) collective-permute-start(bf16[64,2048]{1,0:T(8,128)(2,1)S(1)} %get-tuple-element.75), channel_id=1, source_target_pairs={{0,8},{4,12},{8,0},{12,4},{1,9},{5,13},{9,1},{13,5},{2,10},{6,14},... | collective-permute-start | bytes 786440 | tf_op jit(solution)/shard_map/spread_tokens/ppermute | solution.py:29
  32.5 13.2 %collective-permute-done.5 = bf16[64,2048]{1,0:T(8,128)(2,1)S(1)} collective-permute-done((bf16[64,2048]{1,0:T(8,128)(2,1)S(1)}, bf16[64,2048]{1,0:T(8,128)(2,1)S(1)}, u32[]{:S(2)}, u32[]{:S(2)}) %collective-permute-start.5) | collective-permute-done | bytes 262176 | tf_op jit(solution)/shard_map/spread_tokens/ppermute | solution.py:29
  45.8 1.8 collective-permute-start.7
  47.8 4.4 %collective-permute-start.11 = (bf16[304,2048]{1,0:T(8,128)(2,1)S(1)}, bf16[304,2048]{1,0:T(8,128)(2,1)S(1)}, u32[]{:S(2)}, u32[]{:S(2)}) collective-permute-start(bf16[304,2048]{1,0:T(8,128)(2,1)S(1)} %maximum_maximum_fusion), channel_id=1, source_target_pairs={{0,4},{4,8},{8,12},{1,5},{5,9},{9,13},{2,6},{6,10},{10,14},{3,7},{... | collective-permute-start | bytes 3735560 | tf_op jit(solution)/shard_map/spread_cotangent/ppermute | solution.py:62
  52.2 1.9 collective-permute-start.12
  54.6 4.0 %collective-permute-done.7 = bf16[2,64,2048]{2,1,0:T(8,128)(2,1)S(1)} collective-permute-done((bf16[2,64,2048]{2,1,0:T(8,128)(2,1)S(1)}, bf16[2,64,2048]{2,1,0:T(8,128)(2,1)S(1)}, u32[]{:S(2)}, u32[]{:S(2)}) %collective-permute-start.7) | collective-permute-done | bytes 524320 | tf_op jit(solution)/shard_map/spread_tokens/ppermute | solution.py:26
  58.8 1.8 fusion.42
  61.1 5.5 %collective-permute-done.1 = bf16[2,64,2048]{2,1,0:T(8,128)(2,1)S(1)} collective-permute-done((bf16[2,64,2048]{2,1,0:T(8,128)(2,1)S(1)}, bf16[2,64,2048]{2,1,0:T(8,128)(2,1)S(1)}, u32[]{:S(2)}, u32[]{:S(2)}) %collective-permute-start.1) | collective-permute-done | bytes 524320 | tf_op jit(solution)/shard_map/spread_tokens/ppermute | solution.py:26
  67.4 1.4 slice-done.5
  70.1 2.3 %convolution_convert_fusion.4 = bf16[256,2048]{1,0:T(8,128)(2,1)S(1)} fusion(bf16[256,2048]{1,0:T(8,128)(2,1)S(1)} %bitcast.174, bf16[2048,2048]{1,0:T(8,128)(2,1)S(1)} %bitcast.193), kind=kOutput, calls=%fused_computation.8 | convolution fusion | flops 2148007936 | bytes 10485760 | tf_op jit(solution)/shard_map/forward/dot_general | solution.py:140
  72.5 2.3 %convolution_convert_fusion.5 = bf16[256,2048]{1,0:T(8,128)(2,1)S(1)} fusion(bf16[256,2048]{1,0:T(8,128)(2,1)S(1)} %bitcast.175, bf16[2048,2048]{1,0:T(8,128)(2,1)S(1)} %bitcast.193), kind=kOutput, calls=%fused_computation.9 | convolution fusion | flops 2148007936 | bytes 10485760 | tf_op jit(solution)/shard_map/forward/dot_general | solution.py:140
  77.0 1.8 collective-permute-done.12
  78.7 2.7 %collective-permute-start.15 = (bf16[304,2048]{1,0:T(8,128)(2,1)S(1)}, bf16[304,2048]{1,0:T(8,128)(2,1)S(1)}, u32[]{:S(2)}, u32[]{:S(2)}) collective-permute-start(bf16[304,2048]{1,0:T(8,128)(2,1)S(1)} %collective-permute-done.11), channel_id=1, source_target_pairs={{4,8},{8,12},{5,9},{9,13},{6,10},{10,14},{7,11},{11,15},{20,24},{2... | collective-permute-start | bytes 3735560 | tf_op jit(solution)/shard_map/spread_cotangent/ppermute | solution.py:62
  81.4 2.1 %collective-permute-start.16 = (bf16[304,2048]{1,0:T(8,128)(2,1)S(1)}, bf16[304,2048]{1,0:T(8,128)(2,1)S(1)}, u32[]{:S(2)}, u32[]{:S(2)}) collective-permute-start(bf16[304,2048]{1,0:T(8,128)(2,1)S(1)} %collective-permute-done.12), channel_id=1, source_target_pairs={{4,0},{8,4},{5,1},{9,5},{6,2},{10,6},{7,3},{11,7},{20,16},{24,20},... | collective-permute-start | bytes 3735560 | tf_op jit(solution)/shard_map/spread_cotangent/ppermute | solution.py:63
  84.1 2.3 %convolution_convert_fusion.3 = bf16[256,2048]{1,0:T(8,128)(2,1)S(1)} fusion(bf16[256,2048]{1,0:T(8,128)(2,1)S(1)} %bitcast.187, bf16[2048,2048]{1,0:T(8,128)(2,1)S(1)} %bitcast.193), kind=kOutput, calls=%fused_computation.7 | convolution fusion | flops 2148007936 | bytes 10485760 | tf_op jit(solution)/shard_map/forward/dot_general | solution.py:140
  86.4 2.4 %convolution_add_fusion = f32[256,2048]{1,0:T(8,128)S(1)} fusion(f32[256,2048]{1,0:T(8,128)S(1)} %bitcast.172, bf16[256,2048]{1,0:T(8,128)(2,1)S(1)} %bitcast.186, bf16[2048,2048]{1,0:T(8,128)(2,1)S(1)} %bitcast.193), kind=kOutput, calls=%fused_computation.4 | convolution fusion | flops 2148007936 | bytes 13631488 | tf_op jit(solution)/shard_map/forward/dot_general | solution.py:140
  89.0 8.5 %convolution_convert_fusion = bf16[512,2048]{1,0:T(8,128)(2,1)S(1)} fusion(bf16[2048,2048]{1,0:T(8,128)(2,1)} %param.8, bf16[256,2048]{1,0:T(8,128)(2,1)S(1)} %slice.70, bf16[256,2048]{1,0:T(8,128)(2,1)S(1)} %slice.69), kind=kOutput, calls=%fused_computation.2 | convolution fusion | flops 4300210176 | bytes 12582912 | tf_op jit(solution)/shard_map/forward/dot_general | solution.py:150
  97.5 4.6 %collective-permute-done.9 = bf16[256,2048]{1,0:T(8,128)(2,1)S(1)} collective-permute-done((bf16[256,2048]{1,0:T(8,128)(2,1)S(1)}, bf16[256,2048]{1,0:T(8,128)(2,1)S(1)}, u32[]{:S(2)}, u32[]{:S(2)}) %collective-permute-start.9) | collective-permute-done | bytes 1048608 | tf_op jit(solution)/shard_map/forward/ppermute | solution.py:187
  104.7 4.6 %collective-permute-start.13 = (bf16[256,2048]{1,0:T(8,128)(2,1)S(1)}, bf16[256,2048]{1,0:T(8,128)(2,1)S(1)}, u32[]{:S(2)}, u32[]{:S(2)}) collective-permute-start(bf16[256,2048]{1,0:T(8,128)(2,1)S(1)} %get-tuple-element.35), channel_id=1, source_target_pairs={{0,4},{4,8},{1,5},{5,9},{2,6},{6,10},{3,7},{7,11},{16,20},{20,24},... | collective-permute-start | bytes 3145736 | tf_op jit(solution)/shard_map/forward/ppermute | solution.py:187
  109.3 4.3 %collective-permute-done.16 = bf16[304,2048]{1,0:T(8,128)(2,1)S(1)} collective-permute-done((bf16[304,2048]{1,0:T(8,128)(2,1)S(1)}, bf16[304,2048]{1,0:T(8,128)(2,1)S(1)}, u32[]{:S(2)}, u32[]{:S(2)}) %collective-permute-start.16) | collective-permute-done | bytes 1245216 | tf_op jit(solution)/shard_map/spread_cotangent/ppermute | solution.py:63
  115.9 7.2 %convolution_convert_fusion.2 = bf16[256,2048]{1,0:T(8,128)(2,1)} fusion(bf16[2048,2048]{1,0:T(8,128)(2,1)} %param.8, bf16[304,2048]{1,0:T(8,128)(2,1)S(1)} %broadcast_select_fusion), kind=kOutput, calls=%fused_computation.6 | convolution fusion | flops 2148007936 | bytes 10485760 | tf_op jit(solution)/shard_map/forward/dot_general | solution.py:150
  123.3 1.5 collective-permute-start.20
  124.7 9.2 %collective-permute-done.14 = bf16[256,2048]{1,0:T(8,128)(2,1)S(1)} collective-permute-done((bf16[256,2048]{1,0:T(8,128)(2,1)S(1)}, bf16[256,2048]{1,0:T(8,128)(2,1)S(1)}, u32[]{:S(2)}, u32[]{:S(2)}) %collective-permute-start.14) | collective-permute-done | bytes 1048608 | tf_op jit(solution)/shard_map/forward/ppermute | solution.py:188
  135.7 1.9 collective-permute-start.17
  137.6 4.2 %collective-permute-start.18 = (bf16[256,2048]{1,0:T(8,128)(2,1)S(1)}, bf16[256,2048]{1,0:T(8,128)(2,1)S(1)}, u32[]{:S(2)}, u32[]{:S(2)}) collective-permute-start(bf16[256,2048]{1,0:T(8,128)(2,1)S(1)} %add.285), channel_id=1, source_target_pairs={{4,0},{8,4},{12,8},{5,1},{9,5},{13,9},{6,2},{10,6},{14,10},{7,3},{... | collective-permute-start | bytes 3145736 | tf_op jit(solution)/shard_map/forward/ppermute | solution.py:188
  142.1 6.2 %convolution_convert_fusion.1 = bf16[256,2048]{1,0:T(8,128)(2,1)S(1)} fusion(bf16[2048,2048]{1,0:T(8,128)(2,1)} %param.8, bf16[304,2048]{1,0:T(8,128)(2,1)S(1)} %select_select_fusion), kind=kOutput, calls=%fused_computation.5 | convolution fusion | flops 2148007936 | bytes 10485760 | tf_op jit(solution)/shard_map/backward/dot_general | solution.py:150
  148.5 1.8 collective-permute-start.22
  150.4 6.9 %collective-permute-done.22 = bf16[1,1,64,2048]{3,2,1,0:T(8,128)(2,1)S(1)} collective-permute-done((bf16[1,1,64,2048]{3,2,1,0:T(8,128)(2,1)S(1)}, bf16[1,1,64,2048]{3,2,1,0:T(8,128)(2,1)S(1)}, u32[]{:S(2)}, u32[]{:S(2)}) %collective-permute-start.22) | collective-permute-done | bytes 262176 | tf_op jit(solution)/shard_map/backward/ppermute | solution.py:26
  157.4 1.8 collective-permute-start.26
  159.2 3.9 %collective-permute-done.17 = bf16[256,2048]{1,0:T(8,128)(2,1)S(1)} collective-permute-done((bf16[256,2048]{1,0:T(8,128)(2,1)S(1)}, bf16[256,2048]{1,0:T(8,128)(2,1)S(1)}, u32[]{:S(2)}, u32[]{:S(2)}) %collective-permute-start.17) | collective-permute-done | bytes 1048608 | tf_op jit(solution)/shard_map/forward/ppermute | solution.py:187
  163.1 1.9 collective-permute-done.18
  165.1 1.4 add_convert_fusion.1
  173.6 2.4 %collective-permute-start.27 = (bf16[64,2048]{1,0:T(8,128)(2,1)S(1)}, bf16[64,2048]{1,0:T(8,128)(2,1)S(1)}, u32[]{:S(2)}, u32[]{:S(2)}) collective-permute-start(bf16[64,2048]{1,0:T(8,128)(2,1)S(1)} %get-tuple-element.67), channel_id=1, source_target_pairs={{0,0},{1,4},{2,8},{3,12},{4,5},{5,9},{6,13},{7,1},{8,10},{9,14},{1... | collective-permute-start | bytes 786440 | tf_op jit(solution)/shard_map/backward/ppermute | solution.py:219
  176.0 4.3 %collective-permute-start.28 = (bf16[64,2048]{1,0:T(8,128)(2,1)S(1)}, bf16[64,2048]{1,0:T(8,128)(2,1)S(1)}, u32[]{:S(2)}, u32[]{:S(2)}) collective-permute-start(bf16[64,2048]{1,0:T(8,128)(2,1)S(1)} %get-tuple-element.64), channel_id=1, source_target_pairs={{0,4},{1,8},{2,12},{3,0},{4,9},{5,13},{6,1},{7,5},{8,14},{9,2},{10... | collective-permute-start | bytes 786440 | tf_op jit(solution)/shard_map/backward/ppermute | solution.py:219
  180.3 3.1 %collective-permute-start.29 = (bf16[64,2048]{1,0:T(8,128)(2,1)S(1)}, bf16[64,2048]{1,0:T(8,128)(2,1)S(1)}, u32[]{:S(2)}, u32[]{:S(2)}) collective-permute-start(bf16[64,2048]{1,0:T(8,128)(2,1)S(1)} %get-tuple-element.66), channel_id=1, source_target_pairs={{0,8},{1,12},{2,0},{3,4},{4,13},{5,1},{6,5},{7,9},{8,2},{9,6},{10,... | collective-permute-start | bytes 786440 | tf_op jit(solution)/shard_map/backward/ppermute | solution.py:219
  183.4 3.4 %collective-permute-start.30 = (bf16[64,2048]{1,0:T(8,128)(2,1)S(1)}, bf16[64,2048]{1,0:T(8,128)(2,1)S(1)}, u32[]{:S(2)}, u32[]{:S(2)}) collective-permute-start(bf16[64,2048]{1,0:T(8,128)(2,1)S(1)} %get-tuple-element.65), channel_id=1, source_target_pairs={{0,12},{1,0},{2,4},{3,8},{4,1},{5,5},{6,9},{7,13},{8,6},{9,10},{10... | collective-permute-start | bytes 786440 | tf_op jit(solution)/shard_map/backward/ppermute | solution.py:219
  186.8 2.7 %fusion.21 = f32[32,16,2048]{2,1,0:T(8,128)} fusion(bf16[128,2048,1]{1,0,2:T(8,128)(2,1)S(1)} %bitcast.171, s32[128]{0:T(128)S(1)} %iota.42, s32[128]{0:T(128)S(1)} %eq.208), kind=kOutput, calls=%fused_computation.89 | convolution fusion | flops 268632064 | bytes 4719616 | tf_op jit(solution)/shard_map/tables/dot_general | solution.py:253
  189.6 2.7 %fusion.23 = f32[32,16,2048]{2,1,0:T(8,128)} fusion(bf16[128,2048,1]{1,0,2:T(8,128)(2,1)S(1)} %bitcast.170, s32[128]{0:T(128)S(1)} %iota.42, s32[128]{0:T(128)S(1)} %eq.208), kind=kOutput, calls=%fused_computation.90 | convolution fusion | flops 268632064 | bytes 4719616 | tf_op jit(solution)/shard_map/tables/dot_general | solution.py:253
  192.3 2.4 %collective-permute-done.27 = bf16[64,2048]{1,0:T(8,128)(2,1)S(1)} collective-permute-done((bf16[64,2048]{1,0:T(8,128)(2,1)S(1)}, bf16[64,2048]{1,0:T(8,128)(2,1)S(1)}, u32[]{:S(2)}, u32[]{:S(2)}) %collective-permute-start.27) | collective-permute-done | bytes 262176 | tf_op jit(solution)/shard_map/backward/ppermute | solution.py:219
  194.7 6.2 %collective-permute-done.28 = bf16[64,2048]{1,0:T(8,128)(2,1)S(1)} collective-permute-done((bf16[64,2048]{1,0:T(8,128)(2,1)S(1)}, bf16[64,2048]{1,0:T(8,128)(2,1)S(1)}, u32[]{:S(2)}, u32[]{:S(2)}) %collective-permute-start.28) | collective-permute-done | bytes 262176 | tf_op jit(solution)/shard_map/backward/ppermute | solution.py:219
  200.9 1.4 collective-permute-done.29
  (156 shorter events, 26.8 us)
Async XLA Ops:
  0.6 1.6 copy-start
  2.8 5.6 %copy-start.10 = (bf16[2,16,2048]{2,1,0:T(8,128)(2,1)}, bf16[2,16,2048]{2,1,0:T(8,128)(2,1)S(1)}, u32[]{:S(2)}) copy-start(bf16[2,16,2048]{2,1,0:T(8,128)(2,1)S(1)} %gather_fusion.1) | copy-start | bytes 393220
  6.6 6.0 %copy-start.7 = (bf16[256,2048]{1,0:T(8,128)(2,1)S(1)}, bf16[256,2048]{1,0:T(8,128)(2,1)}, u32[]{:S(2)}) copy-start(bf16[256,2048]{1,0:T(8,128)(2,1)} %param.11) | copy-start | bytes 3145732
  8.4 4.1 %collective-permute-start.3 = (f32[2,2,16,128]{3,2,1,0:T(8,128)S(1)}, f32[2,2,16,128]{3,2,1,0:T(8,128)S(1)}, u32[]{:S(2)}, u32[]{:S(2)}) collective-permute-start(f32[2,2,16,128]{3,2,1,0:T(8,128)S(1)} %pad_maximum_fusion.11), channel_id=1, source_target_pairs={{0,1},{1,0},{2,3},{3,2},{4,5},{5,4},{6,7},{7,6},{8,9},{9,8},{10,11... | collective-permute-start | bytes 98312 | tf_op jit(solution)/shard_map/ranks/ppermute | solution.py:26
  8.5 17.6 %all-to-all-start = ((bf16[4,64,2048]{2,1,0:T(8,128)(2,1)}), bf16[4,64,2048]{2,1,0:T(8,128)(2,1)S(1)}, u32[]{:S(2)}, u32[]{:S(2)}) async-start(bf16[4,64,2048]{2,1,0:T(8,128)(2,1)} %bitcast), calls=%async_computation | async-start | bytes 2097152 | tf_op jit(solution)/shard_map/spread_tokens/all_to_all | solution.py:67
  12.5 13.5 %collective-permute-start.4 = (f32[2,2,16,128]{3,2,1,0:T(8,128)S(1)}, f32[2,2,16,128]{3,2,1,0:T(8,128)S(1)}, u32[]{:S(2)}, u32[]{:S(2)}) collective-permute-start(f32[2,2,16,128]{3,2,1,0:T(8,128)S(1)} %fusion.47), channel_id=1, source_target_pairs={{0,2},{1,3},{2,0},{3,1},{4,6},{5,7},{6,4},{7,5},{8,10},{9,11},{10,... | collective-permute-start | bytes 98312 | tf_op jit(solution)/shard_map/ranks/ppermute | solution.py:26
  26.1 19.6 %collective-permute-start.5 = (bf16[64,2048]{1,0:T(8,128)(2,1)S(1)}, bf16[64,2048]{1,0:T(8,128)(2,1)S(1)}, u32[]{:S(2)}, u32[]{:S(2)}) collective-permute-start(bf16[64,2048]{1,0:T(8,128)(2,1)S(1)} %get-tuple-element.74), channel_id=1, source_target_pairs={{0,4},{4,8},{8,12},{12,0},{1,5},{5,9},{9,13},{13,1},{2,6},{6,10},{... | collective-permute-start | bytes 786440 | tf_op jit(solution)/shard_map/spread_tokens/ppermute | solution.py:29
  27.8 17.9 %collective-permute-start.6 = (bf16[64,2048]{1,0:T(8,128)(2,1)S(1)}, bf16[64,2048]{1,0:T(8,128)(2,1)S(1)}, u32[]{:S(2)}, u32[]{:S(2)}) collective-permute-start(bf16[64,2048]{1,0:T(8,128)(2,1)S(1)} %get-tuple-element.73), channel_id=1, source_target_pairs={{0,12},{4,0},{8,4},{12,8},{1,13},{5,1},{9,5},{13,9},{2,14},{6,2},{... | collective-permute-start | bytes 786440 | tf_op jit(solution)/shard_map/spread_tokens/ppermute | solution.py:29
  29.9 24.2 %collective-permute-start = (bf16[64,2048]{1,0:T(8,128)(2,1)S(1)}, bf16[64,2048]{1,0:T(8,128)(2,1)S(1)}, u32[]{:S(2)}, u32[]{:S(2)}) collective-permute-start(bf16[64,2048]{1,0:T(8,128)(2,1)S(1)} %get-tuple-element.75), channel_id=1, source_target_pairs={{0,8},{4,12},{8,0},{12,4},{1,9},{5,13},{9,1},{13,5},{2,10},{6,14},... | collective-permute-start | bytes 786440 | tf_op jit(solution)/shard_map/spread_tokens/ppermute | solution.py:29
  45.8 12.8 %collective-permute-start.7 = (bf16[2,64,2048]{2,1,0:T(8,128)(2,1)S(1)}, bf16[2,64,2048]{2,1,0:T(8,128)(2,1)S(1)}, u32[]{:S(2)}, u32[]{:S(2)}) collective-permute-start(bf16[2,64,2048]{2,1,0:T(8,128)(2,1)S(1)} %pad_maximum_fusion.7), channel_id=1, source_target_pairs={{0,2},{1,3},{2,0},{3,1},{4,6},{5,7},{6,4},{7,5},{8,10},{9,11},{10,... | collective-permute-start | bytes 1572872 | tf_op jit(solution)/shard_map/spread_tokens/ppermute | solution.py:26
  47.8 29.2 %collective-permute-start.11 = (bf16[304,2048]{1,0:T(8,128)(2,1)S(1)}, bf16[304,2048]{1,0:T(8,128)(2,1)S(1)}, u32[]{:S(2)}, u32[]{:S(2)}) collective-permute-start(bf16[304,2048]{1,0:T(8,128)(2,1)S(1)} %maximum_maximum_fusion), channel_id=1, source_target_pairs={{0,4},{4,8},{8,12},{1,5},{5,9},{9,13},{2,6},{6,10},{10,14},{3,7},{... | collective-permute-start | bytes 3735560 | tf_op jit(solution)/shard_map/spread_cotangent/ppermute | solution.py:62
  52.2 26.5 %collective-permute-start.12 = (bf16[304,2048]{1,0:T(8,128)(2,1)S(1)}, bf16[304,2048]{1,0:T(8,128)(2,1)S(1)}, u32[]{:S(2)}, u32[]{:S(2)}) collective-permute-start(bf16[304,2048]{1,0:T(8,128)(2,1)S(1)} %maximum_maximum_fusion), channel_id=1, source_target_pairs={{4,0},{8,4},{12,8},{5,1},{9,5},{13,9},{6,2},{10,6},{14,10},{7,3},{... | collective-permute-start | bytes 3735560 | tf_op jit(solution)/shard_map/spread_cotangent/ppermute | solution.py:63
  54.2 12.4 %collective-permute-start.1 = (bf16[2,64,2048]{2,1,0:T(8,128)(2,1)S(1)}, bf16[2,64,2048]{2,1,0:T(8,128)(2,1)S(1)}, u32[]{:S(2)}, u32[]{:S(2)}) collective-permute-start(bf16[2,64,2048]{2,1,0:T(8,128)(2,1)S(1)} %pad_maximum_fusion.6), channel_id=1, source_target_pairs={{0,2},{1,3},{2,0},{3,1},{4,6},{5,7},{6,4},{7,5},{8,10},{9,11},{10,... | collective-permute-start | bytes 1572872 | tf_op jit(solution)/shard_map/spread_tokens/ppermute | solution.py:26
  58.6 2.0 copy-start.11
  58.7 8.1 %collective-permute-start.8 = (bf16[2,2,64,2048]{3,2,0,1:T(8,128)(2,1)S(1)}, bf16[2,2,64,2048]{3,2,0,1:T(8,128)(2,1)S(1)}, u32[]{:S(2)}, u32[]{:S(2)}) collective-permute-start(bf16[2,2,64,2048]{3,2,0,1:T(8,128)(2,1)S(1)} %pad_maximum_fusion.3), channel_id=1, source_target_pairs={{0,1},{1,0},{2,3},{3,2},{4,5},{5,4},{6,7},{7,6},{8,9},{9,8},{10,11... | collective-permute-start | bytes 3145736 | tf_op jit(solution)/shard_map/spread_tokens/ppermute | solution.py:26
  66.6 2.2 %slice-start.5 = ((s8[8388608]{0:T(1024)(128)(4,1)}), s8[4194304]{0:T(1024)(128)(4,1)S(1)}, s32[]{:S(2)}) async-start(s8[8388608]{0:T(1024)(128)(4,1)} %bitcast.192), calls=%async_computation.6 | async-start | bytes 8388608
  66.8 16.9 %collective-permute-start.2 = (bf16[2,2,64,2048]{3,2,1,0:T(8,128)(2,1)S(1)}, bf16[2,2,64,2048]{3,2,1,0:T(8,128)(2,1)S(1)}, u32[]{:S(2)}, u32[]{:S(2)}) collective-permute-start(bf16[2,2,64,2048]{3,2,1,0:T(8,128)(2,1)S(1)} %pad_maximum_fusion.2), channel_id=1, source_target_pairs={{0,1},{1,0},{2,3},{3,2},{4,5},{5,4},{6,7},{7,6},{8,9},{9,8},{10,11... | collective-permute-start | bytes 3145736 | tf_op jit(solution)/shard_map/spread_tokens/ppermute | solution.py:26
  67.0 3.1 %slice-start.6 = ((s8[8388608]{0:T(1024)(128)(4,1)}), s8[4194304]{0:T(1024)(128)(4,1)S(1)}, s32[]{:S(2)}) async-start(s8[8388608]{0:T(1024)(128)(4,1)} %bitcast.192), calls=%async_computation.7 | async-start | bytes 8388608
  74.8 22.7 %collective-permute-start.10 = (bf16[256,2048]{1,0:T(8,128)(2,1)S(1)}, bf16[256,2048]{1,0:T(8,128)(2,1)S(1)}, u32[]{:S(2)}, u32[]{:S(2)}) collective-permute-start(bf16[256,2048]{1,0:T(8,128)(2,1)S(1)} %convolution_convert_fusion.4), channel_id=1, source_target_pairs={{12,8},{13,9},{14,10},{15,11},{28,24},{29,25},{30,26},{31,27}} | collective-permute-start | bytes 3145736 | tf_op jit(solution)/shard_map/forward/ppermute | solution.py:188
  75.6 26.5 %collective-permute-start.9 = (bf16[256,2048]{1,0:T(8,128)(2,1)S(1)}, bf16[256,2048]{1,0:T(8,128)(2,1)S(1)}, u32[]{:S(2)}, u32[]{:S(2)}) collective-permute-start(bf16[256,2048]{1,0:T(8,128)(2,1)S(1)} %convolution_convert_fusion.5), channel_id=1, source_target_pairs={{0,4},{1,5},{2,6},{3,7},{16,20},{17,21},{18,22},{19,23}} | collective-permute-start | bytes 3145736 | tf_op jit(solution)/shard_map/forward/ppermute | solution.py:187
  78.7 30.6 %collective-permute-start.15 = (bf16[304,2048]{1,0:T(8,128)(2,1)S(1)}, bf16[304,2048]{1,0:T(8,128)(2,1)S(1)}, u32[]{:S(2)}, u32[]{:S(2)}) collective-permute-start(bf16[304,2048]{1,0:T(8,128)(2,1)S(1)} %collective-permute-done.11), channel_id=1, source_target_pairs={{4,8},{8,12},{5,9},{9,13},{6,10},{10,14},{7,11},{11,15},{20,24},{2... | collective-permute-start | bytes 3735560 | tf_op jit(solution)/shard_map/spread_cotangent/ppermute | solution.py:62
  81.4 32.2 %collective-permute-start.16 = (bf16[304,2048]{1,0:T(8,128)(2,1)S(1)}, bf16[304,2048]{1,0:T(8,128)(2,1)S(1)}, u32[]{:S(2)}, u32[]{:S(2)}) collective-permute-start(bf16[304,2048]{1,0:T(8,128)(2,1)S(1)} %collective-permute-done.12), channel_id=1, source_target_pairs={{4,0},{8,4},{5,1},{9,5},{6,2},{10,6},{7,3},{11,7},{20,16},{24,20},... | collective-permute-start | bytes 3735560 | tf_op jit(solution)/shard_map/spread_cotangent/ppermute | solution.py:63
  83.7 84.7 %copy-start.2 = (bf16[304,2048]{1,0:T(8,128)(2,1)}, bf16[304,2048]{1,0:T(8,128)(2,1)S(1)}, u32[]{:S(2)}) copy-start(bf16[304,2048]{1,0:T(8,128)(2,1)S(1)} %broadcast_select_fusion.1) | copy-start | bytes 3735556
  103.5 19.6 %collective-permute-start.19 = (bf16[2,2,64,2048]{3,2,0,1:T(8,128)(2,1)}, bf16[2,2,64,2048]{3,2,0,1:T(8,128)(2,1)S(1)}, u32[]{:S(2)}, u32[]{:S(2)}) collective-permute-start(bf16[2,2,64,2048]{3,2,0,1:T(8,128)(2,1)} %bitcast.163), channel_id=1, source_target_pairs={{0,1},{1,0},{2,3},{3,2},{4,5},{5,4},{6,7},{7,6},{8,9},{9,8},{10,11... | collective-permute-start | bytes 3145736 | tf_op jit(solution)/shard_map/forward/ppermute | solution.py:26
  103.5 30.5 %collective-permute-start.14 = (bf16[256,2048]{1,0:T(8,128)(2,1)S(1)}, bf16[256,2048]{1,0:T(8,128)(2,1)S(1)}, u32[]{:S(2)}, u32[]{:S(2)}) collective-permute-start(bf16[256,2048]{1,0:T(8,128)(2,1)S(1)} %get-tuple-element.36), channel_id=1, source_target_pairs={{8,4},{12,8},{9,5},{13,9},{10,6},{14,10},{11,7},{15,11},{24,20},{2... | collective-permute-start | bytes 3145736 | tf_op jit(solution)/shard_map/forward/ppermute | solution.py:188
  104.7 29.6 %collective-permute-start.13 = (bf16[256,2048]{1,0:T(8,128)(2,1)S(1)}, bf16[256,2048]{1,0:T(8,128)(2,1)S(1)}, u32[]{:S(2)}, u32[]{:S(2)}) collective-permute-start(bf16[256,2048]{1,0:T(8,128)(2,1)S(1)} %get-tuple-element.35), channel_id=1, source_target_pairs={{0,4},{4,8},{1,5},{5,9},{2,6},{6,10},{3,7},{7,11},{16,20},{20,24},... | collective-permute-start | bytes 3145736 | tf_op jit(solution)/shard_map/forward/ppermute | solution.py:187
  113.7 24.0 %collective-permute-start.23 = (bf16[304,2048]{1,0:T(8,128)(2,1)S(1)}, bf16[304,2048]{1,0:T(8,128)(2,1)S(1)}, u32[]{:S(2)}, u32[]{:S(2)}) collective-permute-start(bf16[304,2048]{1,0:T(8,128)(2,1)S(1)} %collective-permute-done.15), channel_id=1, source_target_pairs={{8,12},{9,13},{10,14},{11,15},{24,28},{25,29},{26,30},{27,31}} | collective-permute-start | bytes 3735560 | tf_op jit(solution)/shard_map/spread_cotangent/ppermute | solution.py:62
  114.4 27.4 %collective-permute-start.24 = (bf16[304,2048]{1,0:T(8,128)(2,1)S(1)}, bf16[304,2048]{1,0:T(8,128)(2,1)S(1)}, u32[]{:S(2)}, u32[]{:S(2)}) collective-permute-start(bf16[304,2048]{1,0:T(8,128)(2,1)S(1)} %collective-permute-done.16), channel_id=1, source_target_pairs={{4,0},{5,1},{6,2},{7,3},{20,16},{21,17},{22,18},{23,19}} | collective-permute-start | bytes 3735560 | tf_op jit(solution)/shard_map/spread_cotangent/ppermute | solution.py:63
  115.9 52.5 %copy-start.4 = (bf16[304,2048]{1,0:T(8,128)(2,1)}, bf16[304,2048]{1,0:T(8,128)(2,1)S(1)}, u32[]{:S(2)}) copy-start(bf16[304,2048]{1,0:T(8,128)(2,1)S(1)} %broadcast_select_fusion) | copy-start | bytes 3735556
  123.3 27.0 %collective-permute-start.20 = (bf16[2,1,64,2048]{3,2,0,1:T(8,128)(2,1)S(1)}, bf16[2,1,64,2048]{3,2,0,1:T(8,128)(2,1)S(1)}, u32[]{:S(2)}, u32[]{:S(2)}) collective-permute-start(bf16[2,1,64,2048]{3,2,0,1:T(8,128)(2,1)S(1)} %constant_dynamic-slice_fusion.6), channel_id=1, source_target_pairs={{0,2},{1,3},{2,0},{3,1},{4,6},{5,7},{6,4},{7,5},{8,10},{9,11},{10,... | collective-permute-start | bytes 1572872 | tf_op jit(solution)/shard_map/forward/ppermute | solution.py:26
  134.3 1.2 copy-start.8
  135.6 12.8 %collective-permute-start.21 = (bf16[1,2,64,2048]{3,2,1,0:T(8,128)(2,1)S(1)}, bf16[1,2,64,2048]{3,2,1,0:T(8,128)(2,1)S(1)}, u32[]{:S(2)}, u32[]{:S(2)}) collective-permute-start(bf16[1,2,64,2048]{3,2,1,0:T(8,128)(2,1)S(1)} %dynamic-slice_bitcast_fusion.1), channel_id=1, source_target_pairs={{0,1},{1,0},{2,3},{3,2},{4,5},{5,4},{6,7},{7,6},{8,9},{9,8},{10,11... | collective-permute-start | bytes 1572872 | tf_op jit(solution)/shard_map/backward/ppermute | solution.py:26
  135.7 27.4 %collective-permute-start.17 = (bf16[256,2048]{1,0:T(8,128)(2,1)S(1)}, bf16[256,2048]{1,0:T(8,128)(2,1)S(1)}, u32[]{:S(2)}, u32[]{:S(2)}) collective-permute-start(bf16[256,2048]{1,0:T(8,128)(2,1)S(1)} %add.284), channel_id=1, source_target_pairs={{0,4},{4,8},{8,12},{1,5},{5,9},{9,13},{2,6},{6,10},{10,14},{3,7},{... | collective-permute-start | bytes 3145736 | tf_op jit(solution)/shard_map/forward/ppermute | solution.py:187
  137.6 27.4 %collective-permute-start.18 = (bf16[256,2048]{1,0:T(8,128)(2,1)S(1)}, bf16[256,2048]{1,0:T(8,128)(2,1)S(1)}, u32[]{:S(2)}, u32[]{:S(2)}) collective-permute-start(bf16[256,2048]{1,0:T(8,128)(2,1)S(1)} %add.285), channel_id=1, source_target_pairs={{4,0},{8,4},{12,8},{5,1},{9,5},{13,9},{6,2},{10,6},{14,10},{7,3},{... | collective-permute-start | bytes 3145736 | tf_op jit(solution)/shard_map/forward/ppermute | solution.py:188
  142.1 26.4 %copy-start.5 = (bf16[304,2048]{1,0:T(8,128)(2,1)}, bf16[304,2048]{1,0:T(8,128)(2,1)S(1)}, u32[]{:S(2)}) copy-start(bf16[304,2048]{1,0:T(8,128)(2,1)S(1)} %select_select_fusion) | copy-start | bytes 3735556
  148.3 9.0 %collective-permute-start.25 = (bf16[1,2,64,2048]{3,2,1,0:T(8,128)(2,1)S(1)}, bf16[1,2,64,2048]{3,2,1,0:T(8,128)(2,1)S(1)}, u32[]{:S(2)}, u32[]{:S(2)}) collective-permute-start(bf16[1,2,64,2048]{3,2,1,0:T(8,128)(2,1)S(1)} %dynamic-slice_bitcast_fusion), channel_id=1, source_target_pairs={{0,1},{1,0},{2,3},{3,2},{4,5},{5,4},{6,7},{7,6},{8,9},{9,8},{10,11... | collective-permute-start | bytes 1572872 | tf_op jit(solution)/shard_map/backward/ppermute | solution.py:26
  148.5 8.8 %collective-permute-start.22 = (bf16[1,1,64,2048]{3,2,1,0:T(8,128)(2,1)S(1)}, bf16[1,1,64,2048]{3,2,1,0:T(8,128)(2,1)S(1)}, u32[]{:S(2)}, u32[]{:S(2)}) collective-permute-start(bf16[1,1,64,2048]{3,2,1,0:T(8,128)(2,1)S(1)} %constant_dynamic-slice_fusion.5), channel_id=1, source_target_pairs={{0,2},{1,3},{2,0},{3,1},{4,6},{5,7},{6,4},{7,5},{8,10},{9,11},{10,... | collective-permute-start | bytes 786440 | tf_op jit(solution)/shard_map/backward/ppermute | solution.py:26
  157.4 9.1 %collective-permute-start.26 = (bf16[1,1,64,2048]{3,2,1,0:T(8,128)(2,1)S(1)}, bf16[1,1,64,2048]{3,2,1,0:T(8,128)(2,1)S(1)}, u32[]{:S(2)}, u32[]{:S(2)}) collective-permute-start(bf16[1,1,64,2048]{3,2,1,0:T(8,128)(2,1)S(1)} %constant_dynamic-slice_fusion.4), channel_id=1, source_target_pairs={{0,2},{1,3},{2,0},{3,1},{4,6},{5,7},{6,4},{7,5},{8,10},{9,11},{10,... | collective-permute-start | bytes 786440 | tf_op jit(solution)/shard_map/backward/ppermute | solution.py:26
  169.7 1.5 slice-start.3
  170.0 1.5 copy-start.6
  170.4 1.4 slice-start.1
  171.2 1.3 slice-start.4
  173.6 21.1 %collective-permute-start.27 = (bf16[64,2048]{1,0:T(8,128)(2,1)S(1)}, bf16[64,2048]{1,0:T(8,128)(2,1)S(1)}, u32[]{:S(2)}, u32[]{:S(2)}) collective-permute-start(bf16[64,2048]{1,0:T(8,128)(2,1)S(1)} %get-tuple-element.67), channel_id=1, source_target_pairs={{0,0},{1,4},{2,8},{3,12},{4,5},{5,9},{6,13},{7,1},{8,10},{9,14},{1... | collective-permute-start | bytes 786440 | tf_op jit(solution)/shard_map/backward/ppermute | solution.py:219
  176.0 24.9 %collective-permute-start.28 = (bf16[64,2048]{1,0:T(8,128)(2,1)S(1)}, bf16[64,2048]{1,0:T(8,128)(2,1)S(1)}, u32[]{:S(2)}, u32[]{:S(2)}) collective-permute-start(bf16[64,2048]{1,0:T(8,128)(2,1)S(1)} %get-tuple-element.64), channel_id=1, source_target_pairs={{0,4},{1,8},{2,12},{3,0},{4,9},{5,13},{6,1},{7,5},{8,14},{9,2},{10... | collective-permute-start | bytes 786440 | tf_op jit(solution)/shard_map/backward/ppermute | solution.py:219
  180.3 22.0 %collective-permute-start.29 = (bf16[64,2048]{1,0:T(8,128)(2,1)S(1)}, bf16[64,2048]{1,0:T(8,128)(2,1)S(1)}, u32[]{:S(2)}, u32[]{:S(2)}) collective-permute-start(bf16[64,2048]{1,0:T(8,128)(2,1)S(1)} %get-tuple-element.66), channel_id=1, source_target_pairs={{0,8},{1,12},{2,0},{3,4},{4,13},{5,1},{6,5},{7,9},{8,2},{9,6},{10,... | collective-permute-start | bytes 786440 | tf_op jit(solution)/shard_map/backward/ppermute | solution.py:219
  183.4 19.7 %collective-permute-start.30 = (bf16[64,2048]{1,0:T(8,128)(2,1)S(1)}, bf16[64,2048]{1,0:T(8,128)(2,1)S(1)}, u32[]{:S(2)}, u32[]{:S(2)}) collective-permute-start(bf16[64,2048]{1,0:T(8,128)(2,1)S(1)} %get-tuple-element.65), channel_id=1, source_target_pairs={{0,12},{1,0},{2,4},{3,8},{4,1},{5,5},{6,9},{7,13},{8,6},{9,10},{10... | collective-permute-start | bytes 786440 | tf_op jit(solution)/shard_map/backward/ppermute | solution.py:219
  192.3 10.9 %copy-start.3 = (f32[2,128,2048]{2,1,0:T(8,128)S(1)}, f32[2,128,2048]{2,1,0:T(8,128)}, u32[]{:S(2)}) copy-start(f32[2,128,2048]{2,1,0:T(8,128)} %fusion.42) | copy-start | bytes 6291460
  203.2 2.0 copy-start.1
  (3 other events, 3.0 us)
